TPU v7x, 256 devices: a whole 4x4x8 slice. The times are simulated.
256 devices in a mesh: tm: 8 (over y, z_lo), tp: 32 (over z_hi, x, core).
Axes of the slice: x: 4, y: 4, z: 8 (z_hi: 4, z_lo: 2; z = z_hi * 2 + z_lo), core: 2. Of those that a mesh axis runs over, the one named last changes fastest.
Arguments:
- features: bfloat16 [8, 64, 30, 512], P('tm', None, None, 'tp'), may hold values from -6 to 6
- weight_one: bfloat16 [3, 3, 3, 512, 512], P(None, None, None, None, 'tp'), may hold values from -0.0546875 to 0.0546875
- weight_two: bfloat16 [3, 3, 3, 512, 256], replicated, may hold values from -0.0546875 to 0.0546875
- weight_three: bfloat16 [3, 3, 3, 256, 256], replicated, may hold values from -0.078125 to 0.078125
Outputs:
- decoded: bfloat16 [8, 128, 60, 256], P('tm', 'tp')
All inputs are finite; a program needn't handle non-finite values.
Results may differ from a plain program's by a relative error of at most 0.019.
Values may be sent and summed in bfloat16 or wider, within the bound.
No kernel may reach another device: no remote copies, remote signals or barrier semaphores. Data moves between devices by JAX's collectives and lax.ppermute only.
A program may use at most 128 MiB of HBM per device.

v0:
```python
import jax
import jax.numpy as jnp
from jax import lax
from jax.sharding import PartitionSpec as P


def shifted(block, axis, distance):
    devices = range(lax.axis_size(axis))
    route = [(i - distance, i) for i in devices if i - distance in devices]
    return lax.ppermute(block, axis, route)


def extended(cells, sides, width):
    for axis, dim in sides:
        count = lax.axis_size(axis)
        ends = count - 1
        head = lax.slice_in_dim(cells, 0, width, axis=dim)
        tail = lax.slice_in_dim(cells, cells.shape[dim] - width, cells.shape[dim], axis=dim)
        cells = jnp.concatenate(
            [
                lax.ppermute(tail, axis, [(i, (i + 1) % count) for i in range(ends)]),
                cells,
                lax.ppermute(head, axis, [((i + 1) % count, i) for i in range(ends)]),
            ],
            axis=dim,
        )
    return cells


def silu_round(values):
    return jax.nn.silu(values.astype(jnp.float32)).astype(jnp.bfloat16)


def spread(products, height, across, out_width):
    grid = products.reshape(height, across, 3, 3, out_width)
    padded = jnp.pad(grid, ((1, 1), (1, 1), (0, 0), (0, 0), (0, 0)))
    total = padded[0:height, 0:across, 0, 0]
    for i in range(3):
        for j in range(3):
            if i + j > 0:
                total = total + padded[i : i + height, j : j + across, i, j]
    return total


def plane_taps(padded, weight, k, height, across):
    inner = padded.shape[-1]
    total = jnp.zeros((height * across, weight.shape[4]), jnp.float32)
    for i in range(3):
        for j in range(3):
            window = padded[i : i + height, j : j + across].reshape(height * across, inner)
            total = total + jnp.dot(window, weight[k, i, j], preferred_element_type=jnp.float32)
    return total.reshape(height, across, weight.shape[4])


def stacked_taps(padded, weight, height, across):
    padded = jnp.pad(padded, ((0, 0), (0, 0), (1, 1), (0, 0)))
    total = plane_taps(padded[0], weight, 0, height, across)
    for k in range(1, 3):
        total = total + plane_taps(padded[k], weight, k, height, across)
    return total


def doubled(values, axis):
    return jnp.repeat(jnp.repeat(values, 2, axis=axis), 2, axis=axis + 1)


def wide_conv(coarse, weight):
    frame_index = lax.axis_index("tm")
    frame = doubled(coarse, 0)
    height, across, inner = frame.shape
    sequence = [frame]
    current = frame
    for offset in range(2):
        arrived = shifted(current, "tm", 1)
        current = jnp.where(frame_index == 0, frame, arrived)
        sequence.insert(0, current)
    padded = extended(jnp.stack(sequence), (("tp", 1),), 1)
    return stacked_taps(padded, weight, height, across)


def strip_conv(frame, weight):
    frame_index = lax.axis_index("tm")
    height, across, inner = frame.shape
    sequence = [frame]
    current = frame
    for offset in range(2):
        arrived = shifted(current, "tm", 1)
        current = jnp.where(frame_index == 0, frame, arrived)
        sequence.insert(0, current)
    padded = extended(jnp.stack(sequence), (("tp", 1),), 1)
    return stacked_taps(padded, weight, height, across)


def on_device(features, weight_one, weight_two, weight_three):
    frame_index = lax.axis_index("tm")
    own_block = features[0]
    height, across, shard_width = own_block.shape
    channels = weight_one.shape[3]
    act_in = silu_round(own_block)
    kernel = jnp.transpose(weight_one, (3, 0, 1, 2, 4)).reshape(channels, 27 * shard_width)
    span = 9 * shard_width
    sequence = [act_in]
    current = act_in
    for offset in range(2):
        arrived = shifted(current, "tm", 1)
        current = jnp.where(frame_index == 0, act_in, arrived)
        sequence.insert(0, current)
    gathered = (
        lax.all_gather(sequence[0], "tp", axis=2, tiled=True),
        lax.all_gather(sequence[1], "tp", axis=2, tiled=True),
        lax.all_gather(sequence[2], "tp", axis=2, tiled=True),
    )
    conv_one = jnp.zeros((height, across, shard_width), jnp.float32)
    for k in range(3):
        products = jnp.dot(
            gathered[k].reshape(height * across, channels),
            kernel[:, k * span : (k + 1) * span],
            preferred_element_type=jnp.float32,
        )
        conv_one = conv_one + spread(products, height, across, shard_width)
    level_one = (own_block.astype(jnp.float32) + conv_one).astype(jnp.bfloat16)
    act_mid = silu_round(level_one)
    coarse = lax.all_to_all(act_mid, "tp", split_axis=0, concat_axis=2, tiled=True)
    mid_terms = wide_conv(coarse, weight_two)
    block_mid = mid_terms.astype(jnp.bfloat16)
    act_out = silu_round(block_mid)
    decoded = (block_mid.astype(jnp.float32) + strip_conv(act_out, weight_three)).astype(
        jnp.bfloat16
    )
    return decoded[None]


def solution(mesh):
    return jax.shard_map(
        on_device,
        mesh=mesh,
        in_specs=(P("tm", None, None, "tp"), P(None, None, None, None, "tp"), P(), P()),
        out_specs=P("tm", "tp", None, None),
        check_vma=False,
    )
```

profile of v0, /device:TPU:79, one launch (start us, length us, event | category | flops | bytes accessed | tf_op | source)
XLA Modules:
  0.0 404.6 jit_solution(5653020462832530878)
XLA Ops:
  8.2 3.5 collective-permute-start
  11.8 3.6 collective-permute-done
  17.1 2.6 collective-permute-start.1
  19.8 4.1 %collective-permute-done.1 = bf16[64,30,16]{0,2,1:T(8,128)(2,1)S(1)} collective-permute-done((bf16[64,30,16]{0,2,1:T(8,128)(2,1)}, bf16[64,30,16]{0,2,1:T(8,128)(2,1)S(1)}, u32[]{:S(2)}, u32[]{:S(2)}) %collective-permute-start.1) | collective-permute-done | bytes 61472 | tf_op jit(solution)/shard_map/ppermute | solution.py:10
  26.6 46.9 %all-gather.8.cloned.1.call-done = bf16[64,30,512]{0,2,1:T(8,128)(2,1)} async-done(((bf16[64,30,16]{0,2,1:T(8,128)(2,1)}), bf16[64,30,512]{0,2,1:T(8,128)(2,1)}) %all-gather.8.cloned.1.call-update) | async-done | bytes 1966096 | tf_op jit(solution)/shard_map/all_gather | solution.py:111
  73.6 2.9 fusion
  76.4 60.6 %all-gather.6.cloned.1.call-done = bf16[64,30,512]{0,2,1:T(8,128)(2,1)} async-done(((bf16[64,30,16]{0,2,1:T(8,128)(2,1)}), bf16[64,30,512]{0,2,1:T(8,128)(2,1)}) %all-gather.6.cloned.1.call-update) | async-done | bytes 1966096 | tf_op jit(solution)/shard_map/all_gather | solution.py:110
  137.0 4.2 %fusion.2 = f32[64,30,3,3,16]{0,4,1,3,2:T(8,128)} fusion(bf16[3,3,16,512,1]{3,2,4,1,0:T(8,128)(2,1)S(1)} %bitcast.317, bf16[64,30,512]{0,2,1:T(8,128)(2,1)} %all-gather.6.cloned.1.call-done), kind=kOutput, calls=%fused_computation.4 | convolution fusion | flops 283115520 | bytes 3219456 | tf_op jit(solution)/shard_map/dot_general | solution.py:115
  141.3 59.2 %all-gather.4.cloned.1.call-done = bf16[64,30,512]{0,2,1:T(8,128)(2,1)} async-done(((bf16[64,30,16]{0,2,1:T(8,128)(2,1)}), bf16[64,30,512]{0,2,1:T(8,128)(2,1)}) %all-gather.4.cloned.1.call-update) | async-done | bytes 1966096 | tf_op jit(solution)/shard_map/all_gather | solution.py:109
  200.5 3.0 fusion.4
  205.4 14.1 %all_to_all.18 = bf16[32,2,480]{2,1,0:T(2,128)(2,1)S(1)} all-to-all(bf16[32,2,480]{2,1,0:T(2,128)(2,1)S(1)} %reshape.394), channel_id=1, replica_groups=mesh['tm'=8,'tp'=32] {'tp'}, dimensions={0} | all-to-all | bytes 122880 | tf_op jit(solution)/shard_map/all_to_all | solution.py:123
  220.3 3.0 collective-permute-start.2
  223.3 6.9 %collective-permute-done.2 = bf16[4,60,512]{2,0,1:T(4,128)(2,1)S(1)} collective-permute-done((bf16[4,60,512]{2,0,1:T(4,128)(2,1)S(1)}, bf16[4,60,512]{2,0,1:T(4,128)(2,1)S(1)}, u32[]{:S(2)}, u32[]{:S(2)}) %collective-permute-start.2) | collective-permute-done | bytes 245792 | tf_op jit(solution)/shard_map/ppermute | solution.py:10
  232.4 6.9 %collective-permute-done.3 = bf16[4,60,512]{2,0,1:T(4,128)(2,1)S(1)} collective-permute-done((bf16[4,60,512]{2,0,1:T(4,128)(2,1)S(1)}, bf16[4,60,512]{2,0,1:T(4,128)(2,1)S(1)}, u32[]{:S(2)}, u32[]{:S(2)}) %collective-permute-start.3) | collective-permute-done | bytes 245792 | tf_op jit(solution)/shard_map/ppermute | solution.py:10
  240.6 5.9 %collective-permute-start.4 = (bf16[3,1,60,512]{3,1,2,0:T(2,128)(2,1)S(1)}, bf16[3,1,60,512]{3,1,2,0:T(2,128)(2,1)S(1)}, u32[]{:S(2)}, u32[]{:S(2)}) collective-permute-start(bf16[3,1,60,512]{3,1,2,0:T(2,128)(2,1)S(1)} %get-tuple-element.8), channel_id=1, source_target_pairs={{0,1},{1,2},{2,3},{3,4},{4,5},{5,6},{6,7},{7,8},{8,9},{9,10},{10,1... | collective-permute-start | bytes 552968 | tf_op jit(solution)/shard_map/ppermute | solution.py:21
  246.5 2.1 collective-permute-start.5
  248.6 4.1 %collective-permute-done.4 = bf16[3,1,60,512]{3,1,2,0:T(2,128)(2,1)S(1)} collective-permute-done((bf16[3,1,60,512]{3,1,2,0:T(2,128)(2,1)S(1)}, bf16[3,1,60,512]{3,1,2,0:T(2,128)(2,1)S(1)}, u32[]{:S(2)}, u32[]{:S(2)}) %collective-permute-start.4) | collective-permute-done | bytes 184352 | tf_op jit(solution)/shard_map/ppermute | solution.py:21
  252.7 9.8 %collective-permute-done.5 = bf16[3,1,60,512]{3,1,2,0:T(2,128)(2,1)S(1)} collective-permute-done((bf16[3,1,60,512]{3,1,2,0:T(2,128)(2,1)S(1)}, bf16[3,1,60,512]{3,1,2,0:T(2,128)(2,1)S(1)}, u32[]{:S(2)}, u32[]{:S(2)}) %collective-permute-start.5) | collective-permute-done | bytes 184352 | tf_op jit(solution)/shard_map/ppermute | solution.py:23
  264.0 3.1 fusion.174
  322.6 5.1 %collective-permute-done.6 = bf16[4,60,256]{2,1,0:T(8,128)(2,1)S(1)} collective-permute-done((bf16[4,60,256]{2,1,0:T(8,128)(2,1)S(1)}, bf16[4,60,256]{2,1,0:T(8,128)(2,1)S(1)}, u32[]{:S(2)}, u32[]{:S(2)}) %collective-permute-start.6) | collective-permute-done | bytes 122912 | tf_op jit(solution)/shard_map/ppermute | solution.py:10
  329.9 4.6 %collective-permute-done.7 = bf16[4,60,256]{2,1,0:T(8,128)(2,1)S(1)} collective-permute-done((bf16[4,60,256]{2,1,0:T(8,128)(2,1)S(1)}, bf16[4,60,256]{2,1,0:T(8,128)(2,1)S(1)}, u32[]{:S(2)}, u32[]{:S(2)}) %collective-permute-start.7) | collective-permute-done | bytes 122912 | tf_op jit(solution)/shard_map/ppermute | solution.py:10
  334.6 4.2 %collective-permute-start.8 = (bf16[3,1,60,256]{3,2,1,0:T(8,128)(2,1)S(1)}, bf16[3,1,60,256]{3,2,1,0:T(8,128)(2,1)S(1)}, u32[]{:S(2)}, u32[]{:S(2)}) collective-permute-start(bf16[3,1,60,256]{3,2,1,0:T(8,128)(2,1)S(1)} %get-tuple-element.43), channel_id=1, source_target_pairs={{0,1},{1,2},{2,3},{3,4},{4,5},{5,6},{6,7},{7,8},{8,9},{9,10},{10,1... | collective-permute-start | bytes 276488 | tf_op jit(solution)/shard_map/ppermute | solution.py:21
  338.8 2.1 collective-permute-start.9
  340.9 8.2 %collective-permute-done.9 = bf16[3,1,60,256]{3,2,1,0:T(8,128)(2,1)S(1)} collective-permute-done((bf16[3,1,60,256]{3,2,1,0:T(8,128)(2,1)S(1)}, bf16[3,1,60,256]{3,2,1,0:T(8,128)(2,1)S(1)}, u32[]{:S(2)}, u32[]{:S(2)}) %collective-permute-start.9) | collective-permute-done | bytes 92192 | tf_op jit(solution)/shard_map/ppermute | solution.py:23
  (275 shorter events, 119.1 us)
Async XLA Ops:
  6.5 67.0 %all-gather.8.cloned.1.call-start = ((), (), s32[]{:S(2)}) async-start(), calls=%async_computation.3 | async-start | bytes 4055040 | tf_op jit(solution)/shard_map/all_gather | solution.py:111
  8.2 128.8 %all-gather.6.cloned.1.call-start = ((), (), s32[]{:S(2)}) async-start(), calls=%async_computation.2 | async-start | bytes 4055040 | tf_op jit(solution)/shard_map/all_gather | solution.py:110
  8.2 7.2 %collective-permute-start = (bf16[64,30,16]{0,2,1:T(8,128)(2,1)}, bf16[64,30,16]{0,2,1:T(8,128)(2,1)S(1)}, u32[]{:S(2)}, u32[]{:S(2)}) collective-permute-start(bf16[64,30,16]{0,2,1:T(8,128)(2,1)} %fusion.88), channel_id=1, source_target_pairs={{0,32},{32,64},{64,96},{96,128},{128,160},{160,192},{192,224},{1,3... | collective-permute-start | bytes 184328 | tf_op jit(solution)/shard_map/ppermute | solution.py:10
  17.1 183.4 %all-gather.4.cloned.1.call-start = ((), (), s32[]{:S(2)}) async-start(), calls=%async_computation.1 | async-start | bytes 4055040 | tf_op jit(solution)/shard_map/all_gather | solution.py:109
  17.1 6.7 %collective-permute-start.1 = (bf16[64,30,16]{0,2,1:T(8,128)(2,1)}, bf16[64,30,16]{0,2,1:T(8,128)(2,1)S(1)}, u32[]{:S(2)}, u32[]{:S(2)}) collective-permute-start(bf16[64,30,16]{0,2,1:T(8,128)(2,1)} %broadcast_select_fusion.2), channel_id=1, source_target_pairs={{0,32},{32,64},{64,96},{96,128},{128,160},{160,192},{192,224},{1,3... | collective-permute-start | bytes 184328 | tf_op jit(solution)/shard_map/ppermute | solution.py:10
  220.3 9.9 %collective-permute-start.2 = (bf16[4,60,512]{2,0,1:T(4,128)(2,1)S(1)}, bf16[4,60,512]{2,0,1:T(4,128)(2,1)S(1)}, u32[]{:S(2)}, u32[]{:S(2)}) collective-permute-start(bf16[4,60,512]{2,0,1:T(4,128)(2,1)S(1)} %bitcast.303), channel_id=1, source_target_pairs={{0,32},{32,64},{64,96},{96,128},{128,160},{160,192},{192,224},{1,3... | collective-permute-start | bytes 737288 | tf_op jit(solution)/shard_map/ppermute | solution.py:10
  230.3 9.0 %collective-permute-start.3 = (bf16[4,60,512]{2,0,1:T(4,128)(2,1)S(1)}, bf16[4,60,512]{2,0,1:T(4,128)(2,1)S(1)}, u32[]{:S(2)}, u32[]{:S(2)}) collective-permute-start(bf16[4,60,512]{2,0,1:T(4,128)(2,1)S(1)} %bitcast_select_fusion.1), channel_id=1, source_target_pairs={{0,32},{32,64},{64,96},{96,128},{128,160},{160,192},{192,224},{1,3... | collective-permute-start | bytes 737288 | tf_op jit(solution)/shard_map/ppermute | solution.py:10
  240.6 12.1 %collective-permute-start.4 = (bf16[3,1,60,512]{3,1,2,0:T(2,128)(2,1)S(1)}, bf16[3,1,60,512]{3,1,2,0:T(2,128)(2,1)S(1)}, u32[]{:S(2)}, u32[]{:S(2)}) collective-permute-start(bf16[3,1,60,512]{3,1,2,0:T(2,128)(2,1)S(1)} %get-tuple-element.8), channel_id=1, source_target_pairs={{0,1},{1,2},{2,3},{3,4},{4,5},{5,6},{6,7},{7,8},{8,9},{9,10},{10,1... | collective-permute-start | bytes 552968 | tf_op jit(solution)/shard_map/ppermute | solution.py:21
  246.5 16.0 %collective-permute-start.5 = (bf16[3,1,60,512]{3,1,2,0:T(2,128)(2,1)S(1)}, bf16[3,1,60,512]{3,1,2,0:T(2,128)(2,1)S(1)}, u32[]{:S(2)}, u32[]{:S(2)}) collective-permute-start(bf16[3,1,60,512]{3,1,2,0:T(2,128)(2,1)S(1)} %get-tuple-element.9), channel_id=1, source_target_pairs={{1,0},{2,1},{3,2},{4,3},{5,4},{6,5},{7,6},{8,7},{9,8},{10,9},{11,1... | collective-permute-start | bytes 552968 | tf_op jit(solution)/shard_map/ppermute | solution.py:23
  293.1 23.5 %slice-start = ((s8[7077888]{0:T(1024)(128)(4,1)}), s8[2883584]{0:T(1024)(128)(4,1)S(1)}, s32[]{:S(2)}) async-start(s8[7077888]{0:T(1024)(128)(4,1)} %bitcast.301), calls=%async_computation.4 | async-start | bytes 5767168
  305.4 7.4 %copy-start.7 = (bf16[240,512]{1,0:T(8,128)(2,1)S(1)}, bf16[240,512]{1,0:T(8,128)(2,1)}, u32[]{:S(2)}) copy-start(bf16[240,512]{1,0:T(8,128)(2,1)} %reshape.341) | copy-start | bytes 737284
  305.4 8.6 %copy-start.8 = (bf16[240,512]{1,0:T(8,128)(2,1)S(1)}, bf16[240,512]{1,0:T(8,128)(2,1)}, u32[]{:S(2)}) copy-start(bf16[240,512]{1,0:T(8,128)(2,1)} %reshape.342) | copy-start | bytes 737284
  305.4 9.9 %copy-start.9 = (f32[240,256]{1,0:T(8,128)S(1)}, f32[240,256]{1,0:T(8,128)}, u32[]{:S(2)}) copy-start(f32[240,256]{1,0:T(8,128)} %fusion.42) | copy-start | bytes 737284
  305.4 9.9 %copy-start.10 = (bf16[240,512]{1,0:T(8,128)(2,1)S(1)}, bf16[240,512]{1,0:T(8,128)(2,1)}, u32[]{:S(2)}) copy-start(bf16[240,512]{1,0:T(8,128)(2,1)} %reshape.327) | copy-start | bytes 737284
  305.4 11.2 %slice-start.1 = ((s8[7077888]{0:T(1024)(128)(4,1)}), s8[4194304]{0:T(1024)(128)(4,1)S(1)}, s32[]{:S(2)}) async-start(s8[7077888]{0:T(1024)(128)(4,1)} %bitcast.301), calls=%async_computation.5 | async-start | bytes 8388608
  306.9 9.6 %copy-start.11 = (bf16[240,512]{1,0:T(8,128)(2,1)S(1)}, bf16[240,512]{1,0:T(8,128)(2,1)}, u32[]{:S(2)}) copy-start(bf16[240,512]{1,0:T(8,128)(2,1)} %reshape.328) | copy-start | bytes 737284
  308.7 8.1 %copy-start.12 = (bf16[240,512]{1,0:T(8,128)(2,1)S(1)}, bf16[240,512]{1,0:T(8,128)(2,1)}, u32[]{:S(2)}) copy-start(bf16[240,512]{1,0:T(8,128)(2,1)} %reshape.329) | copy-start | bytes 737284
  310.1 7.0 %copy-start.13 = (bf16[240,512]{1,0:T(8,128)(2,1)S(1)}, bf16[240,512]{1,0:T(8,128)(2,1)}, u32[]{:S(2)}) copy-start(bf16[240,512]{1,0:T(8,128)(2,1)} %reshape.330) | copy-start | bytes 737284
  320.7 7.1 %collective-permute-start.6 = (bf16[4,60,256]{2,1,0:T(8,128)(2,1)S(1)}, bf16[4,60,256]{2,1,0:T(8,128)(2,1)S(1)}, u32[]{:S(2)}, u32[]{:S(2)}) collective-permute-start(bf16[4,60,256]{2,1,0:T(8,128)(2,1)S(1)} %multiply_convert_fusion.1), channel_id=1, source_target_pairs={{0,32},{32,64},{64,96},{96,128},{128,160},{160,192},{192,224},{1,3... | collective-permute-start | bytes 368648 | tf_op jit(solution)/shard_map/ppermute | solution.py:10
  322.6 26.6 %copy-start.2 = (f32[1,4,60,256]{3,2,1,0:T(8,128)}, f32[1,4,60,256]{3,2,1,0:T(8,128)S(1)}, u32[]{:S(2)}) copy-start(f32[1,4,60,256]{3,2,1,0:T(8,128)S(1)} %reshape.375) | copy-start | bytes 737284
  327.9 6.6 %collective-permute-start.7 = (bf16[4,60,256]{2,1,0:T(8,128)(2,1)S(1)}, bf16[4,60,256]{2,1,0:T(8,128)(2,1)S(1)}, u32[]{:S(2)}, u32[]{:S(2)}) collective-permute-start(bf16[4,60,256]{2,1,0:T(8,128)(2,1)S(1)} %broadcast_select_fusion), channel_id=1, source_target_pairs={{0,32},{32,64},{64,96},{96,128},{128,160},{160,192},{192,224},{1,3... | collective-permute-start | bytes 368648 | tf_op jit(solution)/shard_map/ppermute | solution.py:10
  334.6 6.3 %collective-permute-start.8 = (bf16[3,1,60,256]{3,2,1,0:T(8,128)(2,1)S(1)}, bf16[3,1,60,256]{3,2,1,0:T(8,128)(2,1)S(1)}, u32[]{:S(2)}, u32[]{:S(2)}) collective-permute-start(bf16[3,1,60,256]{3,2,1,0:T(8,128)(2,1)S(1)} %get-tuple-element.43), channel_id=1, source_target_pairs={{0,1},{1,2},{2,3},{3,4},{4,5},{5,6},{6,7},{7,8},{8,9},{9,10},{10,1... | collective-permute-start | bytes 276488 | tf_op jit(solution)/shard_map/ppermute | solution.py:21
  338.8 10.4 %collective-permute-start.9 = (bf16[3,1,60,256]{3,2,1,0:T(8,128)(2,1)S(1)}, bf16[3,1,60,256]{3,2,1,0:T(8,128)(2,1)S(1)}, u32[]{:S(2)}, u32[]{:S(2)}) collective-permute-start(bf16[3,1,60,256]{3,2,1,0:T(8,128)(2,1)S(1)} %get-tuple-element.44), channel_id=1, source_target_pairs={{1,0},{2,1},{3,2},{4,3},{5,4},{6,5},{7,6},{8,7},{9,8},{10,9},{11,1... | collective-permute-start | bytes 276488 | tf_op jit(solution)/shard_map/ppermute | solution.py:23
  365.3 20.8 %copy-start = (bf16[3,3,3,256,256]{4,3,2,1,0:T(8,128)(2,1)S(1)}, bf16[3,3,3,256,256]{4,3,2,1,0:T(8,128)(2,1)}, u32[]{:S(2)}) copy-start(bf16[3,3,3,256,256]{4,3,2,1,0:T(8,128)(2,1)} %param.7) | copy-start | bytes 10616836
  (36 other events, 116.5 us)
Sparse Core Ops, SparseCore 0:
  9.8 63.6 all-gather.7
  76.0 60.9 all-gather.5
  139.5 60.9 all-gather.3
where the time goes:
time: 406 us; the launch traced here: 405 us
  waiting for transfers between devices  220 us (54%)
  local copies, waits for them, and re-layouts  70.3 us (17%)
  matrix products  45.9 us (11%)
  starting transfers between devices  29.6 us (7%)
  between operations  14.6 us (4%)
  blocking collectives  14.1 us (3%)
  other arithmetic  9.92 us (2%)
    all_gather x1, waiting for transfers between devices, on_device(): lax.all_gather(sequence[1], 'tp', axis=2, tiled=True)  60.6 us
    all_gather x1, waiting for transfers between devices, on_device(): lax.all_gather(sequence[0], 'tp', axis=2, tiled=True)  59.2 us
    all_gather x1, waiting for transfers between devices, on_device(): lax.all_gather(sequence[2], 'tp', axis=2, tiled=True)  46.9 us
    reshape x54, local copies, waits for them, and re-layouts, plane_taps(): window = padded[i:i + height, j:j + across].reshape(height * across, inner)  45.2 us
    dot_general x54, matrix products, plane_taps(): jnp.dot(window, weight[k, i, j], preferred_element_type=jnp.float32)  35.8 us
    ppermute x6, waiting for transfers between devices, shifted(): return lax.ppermute(block, axis, route)  31.3 us
    slice x32, local copies, waits for them, and re-layouts, plane_taps(): window = padded[i:i + height, j:j + across].reshape(height * across, inner)  20.1 us
    ppermute x2, waiting for transfers between devices, extended(): lax.ppermute(head, axis, [((i + 1) % count, i) for i in range(ends)])  18.1 us
  transfers between devices with their start and end apart: 13, of which 12 were waited for; matrix products, arithmetic and copies ran while one was open for 3% of the time, Pallas kernels for 0%

commit v1 on v0

v1 whole, which is shorter than its diff:
```python
import functools

import jax
import jax.numpy as jnp
from jax import lax
from jax.experimental import pallas as pl
from jax.experimental.pallas import tpu as pltpu
from jax.sharding import Mesh, PartitionSpec as P

PITCH = 32
EDGE = 128
BF16 = jnp.bfloat16
F32 = jnp.float32
SMEM = pl.BlockSpec(memory_space=pltpu.SMEM)
VMEM = pl.BlockSpec(memory_space=pltpu.VMEM)
LIMIT = 48 * 2**20


def call(kernel, out_shape, operands, scratch=()):
    specs = [SMEM] + [VMEM] * (len(operands) - 1)
    return pl.pallas_call(
        kernel,
        out_shape=out_shape,
        in_specs=specs,
        out_specs=jax.tree.map(lambda _: VMEM, out_shape),
        scratch_shapes=scratch,
        compiler_params=pltpu.CompilerParams(vmem_limit_bytes=LIMIT),
    )(*operands)


def silu(v):
    return v / (1.0 + jnp.exp(-v))


def column_mask(shape, axis, across):
    return lax.rem(lax.broadcasted_iota(jnp.int32, shape, axis), PITCH) < across


def coarse_kernel(height, at_ref, field_ref, weight_ref, *refs):
    blocks, (first_ref, second_ref, own_ref, all_ref, prod_ref) = refs[:8], refs[8:]
    shard = field_ref.shape[0]
    cells = height * PITCH
    z, x, c, t = at_ref[0], at_ref[1], at_ref[2], at_ref[3]
    for n, block in enumerate(blocks):
        x_from = lax.rem(x + 4 - n // 2, 4)
        c_from = c if n % 2 == 0 else 1 - c
        for p in range(4):
            z_from = lax.rem(z + 4 - p, 4)
            base = pl.multiple_of(((z_from * 4 + x_from) * 2 + c_from) * shard, shard)
            all_ref[pl.ds(base, shard), :] = block[p * shard : (p + 1) * shard, :]
    rows = prod_ref.shape[0]
    prod_ref[:, :EDGE] = jnp.zeros((rows, EDGE), F32)
    prod_ref[:, EDGE + cells :] = jnp.zeros((rows, EDGE), F32)
    span = 512
    for n in range(cells // span):
        prod_ref[:, EDGE + n * span : EDGE + (n + 1) * span] = jnp.dot(
            weight_ref[...], all_ref[:, n * span : (n + 1) * span], preferred_element_type=F32
        )
    start = t == 0
    span = 512
    for n in range(cells // span):
        lo = n * span
        sums = []
        for k in range(3):
            total = None
            for i in range(3):
                for j in range(3):
                    tap = (k * 3 + i) * 3 + j
                    off = (i - 1) * PITCH + j - 1
                    wide = prod_ref[tap * shard : (tap + 1) * shard, lo : lo + span + 2 * EDGE]
                    if off != 0:
                        wide = pltpu.roll(wide, (-off) % (span + 2 * EDGE), 1)
                    piece = wide[:, EDGE : EDGE + span]
                    total = piece if total is None else total + piece
            sums.append(total)
        late = sums[0] + sums[1]
        first_ref[:, lo : lo + span] = jnp.where(start, late, sums[1]).astype(BF16)
        second_ref[:, lo : lo + span] = sums[0].astype(BF16)
        own = field_ref[:, lo : lo + span].astype(F32) + sums[2]
        own_ref[:, lo : lo + span] = jnp.where(start, own + late, own)


def strips_kernel(height, across, at_ref, own_ref, first_ref, second_ref, out_ref, wide_ref):
    t = at_ref[3]
    cells = height * PITCH
    shard = own_ref.shape[0]
    wide_ref[:, :EDGE] = jnp.zeros((shard, EDGE), F32)
    wide_ref[:, EDGE + cells :] = jnp.zeros((shard, EDGE), F32)
    zero = jnp.zeros((shard, cells), F32)
    level = (
        own_ref[...]
        + jnp.where(t >= 1, first_ref[...].astype(F32), zero)
        + jnp.where(t >= 2, second_ref[...].astype(F32), zero)
    )
    act = silu(level.astype(BF16).astype(F32))
    wide_ref[:, EDGE : EDGE + cells] = jnp.where(column_mask(act.shape, 1, across), act, 0.0)
    for s in range(height // 2):
        lo = EDGE + 2 * s * PITCH - PITCH
        base = lo // 128 * 128
        piece = pltpu.roll(wide_ref[:, base : base + 256], 256 - (lo - base), 1)[:, :128]
        out_ref[s] = piece.astype(BF16)


def down(v):
    return pltpu.roll(v, 1, 0)


def up(v):
    return pltpu.roll(v, v.shape[0] - 1, 0)


def fine_kernel(across, at_ref, a0_ref, a1_ref, a2_ref, wide_ref, last_ref, first_ref, second_ref, own_ref):
    t, strip, strips = at_ref[3], at_ref[4], at_ref[5]
    frames = []
    a0 = a0_ref[...].astype(F32)
    a1 = jnp.where(t >= 1, a1_ref[...].astype(F32), a0)
    a2 = jnp.where(t >= 2, a2_ref[...].astype(F32), a1)
    for a in (a2, a1, a0):
        frames.append(a.T.astype(BF16))
    spans = ((0, 3), (0, 4), (1, 4))
    maps = ((0, 0, 1, 1, 2, 2), (0, 1, 1, 2, 2, 3), (0, 0, 1, 1, 2, 2))
    even, odd = [None] * 6, [None] * 6
    for i in range(3):
        lo, hi = spans[i]
        sums = []
        for j in range(3):
            total = None
            for k in range(3):
                part = jnp.dot(frames[k][lo * PITCH : hi * PITCH], wide_ref[k, i, j], preferred_element_type=F32)
                total = part if total is None else total + part
            sums.append(total)
        at_even = down(sums[0]) + sums[1] + sums[2]
        at_odd = sums[0] + sums[1] + up(sums[2])
        for r in range(6):
            at = slice(maps[i][r] * PITCH, (maps[i][r] + 1) * PITCH)
            even[r] = at_even[at] if even[r] is None else even[r] + at_even[at]
            odd[r] = at_odd[at] if odd[r] is None else odd[r] + at_odd[at]
    mid = [jnp.concatenate(rows, 0).astype(BF16).astype(F32) for rows in (even, odd)]
    shape = mid[0].shape
    row = lax.broadcasted_iota(jnp.int32, shape, 0) // PITCH
    keep = column_mask(shape, 0, across)
    keep = keep & ((row > 0) | (strip > 0)) & ((row < 5) | (strip < strips - 1))
    acts = [jnp.where(keep, silu(m), 0.0).astype(BF16) for m in mid]
    size = 4 * PITCH
    sums = []
    for k in range(3):
        parts = []
        for j in range(3):
            total = None
            for i in range(3):
                rows = slice(i * PITCH, i * PITCH + size)
                both = jnp.concatenate([acts[0][rows], acts[1][rows]], 0)
                part = jnp.dot(both, last_ref[k, i, j], preferred_element_type=F32)
                total = part if total is None else total + part
            parts.append(total)
        at_even = down(parts[0][size:]) + parts[1][:size] + parts[2][size:]
        at_odd = parts[0][:size] + parts[1][size:] + up(parts[2][:size])
        sums.append(jnp.concatenate([at_even, at_odd], 0))
    start = t == 0
    late = sums[0] + sums[1]
    first_ref[...] = jnp.where(start, late, sums[1]).astype(BF16)
    second_ref[...] = sums[0].astype(BF16)
    rows = slice(PITCH, PITCH + size)
    own = jnp.concatenate([mid[0][rows], mid[1][rows]], 0) + sums[2]
    own_ref[...] = jnp.where(start, own + late, own)


def last_kernel(across, at_ref, own_ref, first_ref, second_ref, out_ref, order_ref):
    t = at_ref[3]
    zero = jnp.zeros(own_ref.shape, F32)
    total = (
        own_ref[...]
        + jnp.where(t >= 1, first_ref[...].astype(F32), zero)
        + jnp.where(t >= 2, second_ref[...].astype(F32), zero)
    )
    for parity in range(2):
        for h in range(4):
            at = (parity * 4 + h) * PITCH
            for half in range(2):
                order_ref[half, pl.ds(4 * parity + h, PITCH, stride=8), :] = total[
                    at : at + PITCH, 128 * half : 128 * half + 128
                ]
    for half in range(2):
        out_ref[:, 128 * half : 128 * half + 128] = order_ref[half, : 4 * across * 2].astype(BF16)


def turned(block, axis, distance):
    count = lax.axis_size(axis)
    return lax.ppermute(block, axis, [(i, (i + distance) % count) for i in range(count)])


def on_device(features, weight_one, weight_two, weight_three):
    own_block = features[0]
    height, across, shard = own_block.shape
    channels = weight_one.shape[3]
    cells = height * PITCH
    tp = ("z", "x", "c")
    at = jnp.stack(
        [lax.axis_index(a) for a in ("z", "x", "c", "tm")] + [lax.axis_index(tp), lax.axis_size(tp)]
    ).astype(jnp.int32)
    field = jnp.pad(jnp.transpose(own_block, (2, 0, 1)), ((0, 0), (0, 0), (0, PITCH - across))).reshape(shard, cells)
    act_in = silu(field.astype(F32)).astype(BF16)
    column = jnp.concatenate([act_in] + [turned(act_in, "z", d) for d in (1, 2, 3)], 0)
    blocks = []
    for d in range(4):
        block = turned(column, "x", d) if d else column
        blocks += [block, turned(block, "c", 1)]
    kernel = jnp.transpose(weight_one, (0, 1, 2, 4, 3)).reshape(27 * shard, channels)
    small = jax.ShapeDtypeStruct((shard, cells), BF16)
    first, second, own = call(
        functools.partial(coarse_kernel, height),
        (small, small, jax.ShapeDtypeStruct((shard, cells), F32)),
        (at, field, kernel, *blocks),
        (pltpu.VMEM((channels, cells), BF16), pltpu.VMEM((27 * shard, cells + 2 * EDGE), F32)),
    )
    strips = lax.axis_size(tp)
    cut = call(
        functools.partial(strips_kernel, height, across),
        jax.ShapeDtypeStruct((strips, shard, 4 * PITCH), BF16),
        (at, own, turned(first, "tm", 1), turned(second, "tm", 2)),
        (pltpu.VMEM((shard, cells + 2 * EDGE), F32),),
    )
    strip = lax.all_to_all(cut, tp, 0, 0, tiled=True).reshape(channels, 4 * PITCH)
    width = weight_two.shape[4]
    small = jax.ShapeDtypeStruct((8 * PITCH, width), BF16)
    first, second, own = call(
        functools.partial(fine_kernel, across),
        (small, small, jax.ShapeDtypeStruct((8 * PITCH, width), F32)),
        (at, strip, turned(strip, "tm", 1), turned(strip, "tm", 2), weight_two, weight_three),
    )
    decoded = call(
        functools.partial(last_kernel, across),
        jax.ShapeDtypeStruct((8 * across, width), BF16),
        (at, own, turned(first, "tm", 1), turned(second, "tm", 2)),
        (pltpu.VMEM((2, 8 * PITCH, 128), F32),),
    )
    return jnp.transpose(decoded.reshape(2 * across, 4, width), (1, 0, 2))[None]


def solution(mesh):
    grid = Mesh(mesh.devices.reshape(mesh.shape["tm"], 4, 4, 2), ("tm", "z", "x", "c"))
    tp = ("z", "x", "c")
    return jax.shard_map(
        on_device,
        mesh=grid,
        in_specs=(P("tm", None, None, tp), P(None, None, None, None, tp), P(), P()),
        out_specs=P("tm", tp, None, None),
        check_vma=False,
    )
```

time: 406 us -> 98.7 us (0.24)
  the two profiles are of different devices: /device:TPU:79 before, /device:TPU:1 now
where the time goes in v1:
time: 98.7 us; the launch traced here: 98.3 us
  waiting for transfers between devices  32 us (32%)
  starting transfers between devices  28.1 us (28%)
  blocking collectives  18.5 us (19%)
  Pallas kernels  9.93 us (10%)
  local copies, waits for them, and re-layouts  8.14 us (8%)
  other arithmetic  1.6 us (2%)
    ppermute x16, waiting for transfers between devices, turned(): lax.ppermute(block, axis, [(i, (i + distance) % count) for i in range(cou...  32 us
    ppermute x16, starting transfers between devices, turned(): lax.ppermute(block, axis, [(i, (i + distance) % count) for i in range(cou...  28.1 us
    all_to_all x1, blocking collectives, on_device(): lax.all_to_all(cut, tp, 0, 0, tiled=True).reshape(channels, 4 * PITCH)  18.5 us
    pallas_call x4, Pallas kernels, call(): pl.pallas_call(kernel, out_shape=out_shape, in_specs=specs, out_specs=jax...  9.93 us
    unnamed x7, local copies, waits for them, and re-layouts  3.81 us
  transfers between devices with their start and end apart: 16, of which 10 were waited for; matrix products, arithmetic and copies ran while one was open for 0% of the time, Pallas kernels for 0%

profile of v1, /device:TPU:1, one launch (start us, length us, event | category | flops | bytes accessed | tf_op | source)
XLA Modules:
  0.0 98.3 jit_solution(9493628346951274096)
XLA Ops:
  0.0 2.0 %copy.7 = bf16[16,64,30]{2,1,0:T(8,128)(2,1)} copy(bf16[16,64,30]{1,0,2:T(8,128)(2,1)} %bitcast.19) | data formatting | bytes 122880
  2.0 1.7 %pad.4.clone = bf16[16,64,32]{2,1,0:T(8,128)(2,1)} pad(bf16[16,64,30]{2,1,0:T(8,128)(2,1)} %copy.7, bf16[]{:T(256)} %constant.25.clone.1), padding=0_0x0_0x0_2 | pad | bytes 126978 | tf_op jit(solution)/shard_map/jit(_pad)/pad | solution.py:201
  3.7 1.9 %reshape.12.field_ref = bf16[16,2048]{1,0:T(8,128)(2,1)} reshape(bf16[16,64,32]{2,1,0:T(8,128)(2,1)} %pad.4.clone) | data formatting | bytes 131072 | tf_op jit(solution)/shard_map/reshape | solution.py:201
  6.4 6.9 %collective-permute-start.2 = (bf16[16,2048]{1,0:T(8,128)(2,1)S(1)}, bf16[16,2048]{1,0:T(8,128)(2,1)S(1)}, u32[]{:S(2)}, u32[]{:S(2)}) collective-permute-start(bf16[16,2048]{1,0:T(8,128)(2,1)S(1)} %fusion.2), channel_id=1, source_target_pairs={{0,24},{8,0},{16,8},{24,16},{1,25},{9,1},{17,9},{25,17},{2,26},{10... | collective-permute-start | bytes 196616 | tf_op jit(solution)/shard_map/ppermute | solution.py:189
  13.3 1.0 %collective-permute-start.1 = (bf16[16,2048]{1,0:T(8,128)(2,1)S(1)}, bf16[16,2048]{1,0:T(8,128)(2,1)S(1)}, u32[]{:S(2)}, u32[]{:S(2)}) collective-permute-start(bf16[16,2048]{1,0:T(8,128)(2,1)S(1)} %fusion.2), channel_id=1, source_target_pairs={{0,16},{8,24},{16,0},{24,8},{1,17},{9,25},{17,1},{25,9},{2,18},{10... | collective-permute-start | bytes 196616 | tf_op jit(solution)/shard_map/ppermute | solution.py:189
  14.3 2.3 %collective-permute-start = (bf16[16,2048]{1,0:T(8,128)(2,1)S(1)}, bf16[16,2048]{1,0:T(8,128)(2,1)S(1)}, u32[]{:S(2)}, u32[]{:S(2)}) collective-permute-start(bf16[16,2048]{1,0:T(8,128)(2,1)S(1)} %fusion.2), channel_id=1, source_target_pairs={{0,8},{8,16},{16,24},{24,0},{1,9},{9,17},{17,25},{25,1},{2,10},{10... | collective-permute-start | bytes 196616 | tf_op jit(solution)/shard_map/ppermute | solution.py:189
  16.6 4.0 %collective-permute-done.1 = bf16[16,2048]{1,0:T(8,128)(2,1)S(1)} collective-permute-done((bf16[16,2048]{1,0:T(8,128)(2,1)S(1)}, bf16[16,2048]{1,0:T(8,128)(2,1)S(1)}, u32[]{:S(2)}, u32[]{:S(2)}) %collective-permute-start.1) | collective-permute-done | bytes 65568 | tf_op jit(solution)/shard_map/ppermute | solution.py:189
  22.0 2.5 %collective-permute-start.8 = (bf16[64,2048]{1,0:T(8,128)(2,1)}, bf16[64,2048]{1,0:T(8,128)(2,1)}, u32[]{:S(2)}, u32[]{:S(2)}) collective-permute-start(bf16[64,2048]{1,0:T(8,128)(2,1)} %pad_maximum_fusion.refs_0_), channel_id=1, source_target_pairs={{0,6},{2,0},{4,2},{6,4},{1,7},{3,1},{5,3},{7,5},{8,14},{10,8},{12,... | collective-permute-start | bytes 786440 | tf_op jit(solution)/shard_map/ppermute | solution.py:189
  25.6 3.1 %collective-permute-start.3 = (bf16[64,2048]{1,0:T(8,128)(2,1)}, bf16[64,2048]{1,0:T(8,128)(2,1)}, u32[]{:S(2)}, u32[]{:S(2)}) collective-permute-start(bf16[64,2048]{1,0:T(8,128)(2,1)} %pad_maximum_fusion.refs_0_), channel_id=1, source_target_pairs={{0,1},{1,0},{2,3},{3,2},{4,5},{5,4},{6,7},{7,6},{8,9},{9,8},{10,11... | collective-permute-start | bytes 786440 | tf_op jit(solution)/shard_map/ppermute | solution.py:189
  28.7 2.1 %collective-permute-done.8.refs_6_ = bf16[64,2048]{1,0:T(8,128)(2,1)} collective-permute-done((bf16[64,2048]{1,0:T(8,128)(2,1)}, bf16[64,2048]{1,0:T(8,128)(2,1)}, u32[]{:S(2)}, u32[]{:S(2)}) %collective-permute-start.8) | collective-permute-done | bytes 262176 | tf_op jit(solution)/shard_map/ppermute | solution.py:189
  30.8 6.1 %collective-permute-start.9 = (bf16[64,2048]{1,0:T(8,128)(2,1)}, bf16[64,2048]{1,0:T(8,128)(2,1)}, u32[]{:S(2)}, u32[]{:S(2)}) collective-permute-start(bf16[64,2048]{1,0:T(8,128)(2,1)} %collective-permute-done.8.refs_6_), channel_id=1, source_target_pairs={{0,1},{1,0},{2,3},{3,2},{4,5},{5,4},{6,7},{7,6},{8,9},{9,8},{10,11... | collective-permute-start | bytes 786440 | tf_op jit(solution)/shard_map/ppermute | solution.py:189
  37.9 1.8 %collective-permute-done.4.refs_2_ = bf16[64,2048]{1,0:T(8,128)(2,1)} collective-permute-done((bf16[64,2048]{1,0:T(8,128)(2,1)}, bf16[64,2048]{1,0:T(8,128)(2,1)}, u32[]{:S(2)}, u32[]{:S(2)}) %collective-permute-start.4) | collective-permute-done | bytes 262176 | tf_op jit(solution)/shard_map/ppermute | solution.py:189
  40.7 1.4 %collective-permute-done.5.refs_3_ = bf16[64,2048]{1,0:T(8,128)(2,1)} collective-permute-done((bf16[64,2048]{1,0:T(8,128)(2,1)}, bf16[64,2048]{1,0:T(8,128)(2,1)}, u32[]{:S(2)}, u32[]{:S(2)}) %collective-permute-start.5) | collective-permute-done | bytes 262176 | tf_op jit(solution)/shard_map/ppermute | solution.py:189
  43.0 1.0 %copy-done.2 = bf16[3,3,3,512,16]{3,4,2,1,0:T(8,128)(2,1)S(1)} copy-done((bf16[3,3,3,512,16]{3,4,2,1,0:T(8,128)(2,1)S(1)}, bf16[3,3,3,512,16]{3,4,2,1,0:T(8,128)(2,1)}, u32[]{:S(2)}) %copy-start.2) | copy-done | bytes 442392
  44.0 3.0 %shard_map.46 = (bf16[16,2048]{1,0:T(8,128)(2,1)S(1)}, bf16[16,2048]{1,0:T(8,128)(2,1)S(1)}, f32[16,2048]{1,0:T(8,128)S(1)}) custom-call(s32[6]{0:T(128)S(1)} %stack.23.at_ref, bf16[16,2048]{1,0:T(8,128)(2,1)S(1)} %copy-done.1, bf16[432,512]{1,0:T(8,128)(2,1)S(1)} %bitcast.18, bf16[64,2048]{1,0:T(8,128)(2,1)} %pad_maximum_fusion.refs_0_, ...), custom_call_target="tpu_custom_call" | custom-call | tf_op jit(solution)/shard_map/pallas_call | solution.py:21
  47.0 1.0 %collective-permute-start.10 = (bf16[16,2048]{1,0:T(8,128)(2,1)S(1)}, bf16[16,2048]{1,0:T(8,128)(2,1)S(1)}, u32[]{:S(2)}, u32[]{:S(2)}) collective-permute-start(bf16[16,2048]{1,0:T(8,128)(2,1)S(1)} %get-tuple-element.12), channel_id=1, source_target_pairs={{0,32},{32,64},{64,96},{96,128},{128,160},{160,192},{192,224},{224... | collective-permute-start | bytes 196616 | tf_op jit(solution)/shard_map/ppermute | solution.py:189
  48.0 1.3 %collective-permute-start.11 = (bf16[16,2048]{1,0:T(8,128)(2,1)S(1)}, bf16[16,2048]{1,0:T(8,128)(2,1)S(1)}, u32[]{:S(2)}, u32[]{:S(2)}) collective-permute-start(bf16[16,2048]{1,0:T(8,128)(2,1)S(1)} %get-tuple-element.13), channel_id=1, source_target_pairs={{0,64},{32,96},{64,128},{96,160},{128,192},{160,224},{192,0},{224,... | collective-permute-start | bytes 196616 | tf_op jit(solution)/shard_map/ppermute | solution.py:189
  49.3 3.0 %collective-permute-done.10.first_ref = bf16[16,2048]{1,0:T(8,128)(2,1)S(1)} collective-permute-done((bf16[16,2048]{1,0:T(8,128)(2,1)S(1)}, bf16[16,2048]{1,0:T(8,128)(2,1)S(1)}, u32[]{:S(2)}, u32[]{:S(2)}) %collective-permute-start.10) | collective-permute-done | bytes 65568 | tf_op jit(solution)/shard_map/ppermute | solution.py:189
  52.4 2.2 %collective-permute-done.11.second_ref = bf16[16,2048]{1,0:T(8,128)(2,1)S(1)} collective-permute-done((bf16[16,2048]{1,0:T(8,128)(2,1)S(1)}, bf16[16,2048]{1,0:T(8,128)(2,1)S(1)}, u32[]{:S(2)}, u32[]{:S(2)}) %collective-permute-start.11) | collective-permute-done | bytes 65568 | tf_op jit(solution)/shard_map/ppermute | solution.py:189
  55.2 18.5 %all_to_all.5 = bf16[32,16,128]{2,1,0:T(8,128)(2,1)S(1)} all-to-all(bf16[32,16,128]{2,1,0:T(8,128)(2,1)S(1)} %shard_map.47), channel_id=1, replica_groups=mesh['tm'=8,'z'=4,'x'=4,'c'=2] {'z','x','c'}, dimensions={0} | all-to-all | bytes 262144 | tf_op jit(solution)/shard_map/all_to_all | solution.py:223
  74.4 8.3 %collective-permute-done.13.a2_ref = bf16[512,128]{1,0:T(8,128)(2,1)S(1)} collective-permute-done((bf16[512,128]{1,0:T(8,128)(2,1)S(1)}, bf16[512,128]{1,0:T(8,128)(2,1)S(1)}, u32[]{:S(2)}, u32[]{:S(2)}) %collective-permute-start.13) | collective-permute-done | bytes 131104 | tf_op jit(solution)/shard_map/ppermute | solution.py:189
  82.7 5.6 %shard_map.48 = (bf16[256,256]{1,0:T(8,128)(2,1)S(1)}, bf16[256,256]{1,0:T(8,128)(2,1)S(1)}, f32[256,256]{1,0:T(8,128)S(1)}) custom-call(s32[6]{0:T(128)S(1)} %stack.23.at_ref, bf16[512,128]{1,0:T(8,128)(2,1)S(1)} %bitcast.17, bf16[512,128]{1,0:T(8,128)(2,1)S(1)} %collective-permute-done.12.a1_ref, bf16[512,128]{1,0:T(8,128)(2,1)S(1)} %collective-permute-done.13.a2_ref, ...), custom_call_target="tpu_custom_call" | custom-call | tf_op jit(solution)/shard_map/pallas_call | solution.py:21
  88.4 5.9 %collective-permute-done.14.first_ref = bf16[256,256]{1,0:T(8,128)(2,1)S(1)} collective-permute-done((bf16[256,256]{1,0:T(8,128)(2,1)S(1)}, bf16[256,256]{1,0:T(8,128)(2,1)S(1)}, u32[]{:S(2)}, u32[]{:S(2)}) %collective-permute-start.14) | collective-permute-done | bytes 131104 | tf_op jit(solution)/shard_map/ppermute | solution.py:189
  94.3 2.6 %collective-permute-done.15.second_ref = bf16[256,256]{1,0:T(8,128)(2,1)S(1)} collective-permute-done((bf16[256,256]{1,0:T(8,128)(2,1)S(1)}, bf16[256,256]{1,0:T(8,128)(2,1)S(1)}, u32[]{:S(2)}, u32[]{:S(2)}) %collective-permute-start.15) | collective-permute-done | bytes 131104 | tf_op jit(solution)/shard_map/ppermute | solution.py:189
  (26 shorter events, 9.2 us)
Async XLA Ops:
  0.0 82.7 %copy-start = (bf16[3,3,3,256,256]{4,3,2,1,0:T(8,128)(2,1)S(1)}, bf16[3,3,3,256,256]{4,3,2,1,0:T(8,128)(2,1)}, u32[]{:S(2)}) copy-start(bf16[3,3,3,256,256]{4,3,2,1,0:T(8,128)(2,1)} %last_ref.1) | copy-start | bytes 10616836
  6.4 10.2 %collective-permute-start.2 = (bf16[16,2048]{1,0:T(8,128)(2,1)S(1)}, bf16[16,2048]{1,0:T(8,128)(2,1)S(1)}, u32[]{:S(2)}, u32[]{:S(2)}) collective-permute-start(bf16[16,2048]{1,0:T(8,128)(2,1)S(1)} %fusion.2), channel_id=1, source_target_pairs={{0,24},{8,0},{16,8},{24,16},{1,25},{9,1},{17,9},{25,17},{2,26},{10... | collective-permute-start | bytes 196616 | tf_op jit(solution)/shard_map/ppermute | solution.py:189
  13.3 7.2 %collective-permute-start.1 = (bf16[16,2048]{1,0:T(8,128)(2,1)S(1)}, bf16[16,2048]{1,0:T(8,128)(2,1)S(1)}, u32[]{:S(2)}, u32[]{:S(2)}) collective-permute-start(bf16[16,2048]{1,0:T(8,128)(2,1)S(1)} %fusion.2), channel_id=1, source_target_pairs={{0,16},{8,24},{16,0},{24,8},{1,17},{9,25},{17,1},{25,9},{2,18},{10... | collective-permute-start | bytes 196616 | tf_op jit(solution)/shard_map/ppermute | solution.py:189
  14.3 6.9 %collective-permute-start = (bf16[16,2048]{1,0:T(8,128)(2,1)S(1)}, bf16[16,2048]{1,0:T(8,128)(2,1)S(1)}, u32[]{:S(2)}, u32[]{:S(2)}) collective-permute-start(bf16[16,2048]{1,0:T(8,128)(2,1)S(1)} %fusion.2), channel_id=1, source_target_pairs={{0,8},{8,16},{16,24},{24,0},{1,9},{9,17},{17,25},{25,1},{2,10},{10... | collective-permute-start | bytes 196616 | tf_op jit(solution)/shard_map/ppermute | solution.py:189
  22.0 8.8 %collective-permute-start.8 = (bf16[64,2048]{1,0:T(8,128)(2,1)}, bf16[64,2048]{1,0:T(8,128)(2,1)}, u32[]{:S(2)}, u32[]{:S(2)}) collective-permute-start(bf16[64,2048]{1,0:T(8,128)(2,1)} %pad_maximum_fusion.refs_0_), channel_id=1, source_target_pairs={{0,6},{2,0},{4,2},{6,4},{1,7},{3,1},{5,3},{7,5},{8,14},{10,8},{12,... | collective-permute-start | bytes 786440 | tf_op jit(solution)/shard_map/ppermute | solution.py:189
  24.5 12.5 %collective-permute-start.6 = (bf16[64,2048]{1,0:T(8,128)(2,1)}, bf16[64,2048]{1,0:T(8,128)(2,1)}, u32[]{:S(2)}, u32[]{:S(2)}) collective-permute-start(bf16[64,2048]{1,0:T(8,128)(2,1)} %pad_maximum_fusion.refs_0_), channel_id=1, source_target_pairs={{0,4},{2,6},{4,0},{6,2},{1,5},{3,7},{5,1},{7,3},{8,12},{10,14},{12... | collective-permute-start | bytes 786440 | tf_op jit(solution)/shard_map/ppermute | solution.py:189
  25.0 14.7 %collective-permute-start.4 = (bf16[64,2048]{1,0:T(8,128)(2,1)}, bf16[64,2048]{1,0:T(8,128)(2,1)}, u32[]{:S(2)}, u32[]{:S(2)}) collective-permute-start(bf16[64,2048]{1,0:T(8,128)(2,1)} %pad_maximum_fusion.refs_0_), channel_id=1, source_target_pairs={{0,2},{2,4},{4,6},{6,0},{1,3},{3,5},{5,7},{7,1},{8,10},{10,12},{12... | collective-permute-start | bytes 786440 | tf_op jit(solution)/shard_map/ppermute | solution.py:189
  25.6 15.1 %collective-permute-start.3 = (bf16[64,2048]{1,0:T(8,128)(2,1)}, bf16[64,2048]{1,0:T(8,128)(2,1)}, u32[]{:S(2)}, u32[]{:S(2)}) collective-permute-start(bf16[64,2048]{1,0:T(8,128)(2,1)} %pad_maximum_fusion.refs_0_), channel_id=1, source_target_pairs={{0,1},{1,0},{2,3},{3,2},{4,5},{5,4},{6,7},{7,6},{8,9},{9,8},{10,11... | collective-permute-start | bytes 786440 | tf_op jit(solution)/shard_map/ppermute | solution.py:189
  30.8 9.9 %collective-permute-start.9 = (bf16[64,2048]{1,0:T(8,128)(2,1)}, bf16[64,2048]{1,0:T(8,128)(2,1)}, u32[]{:S(2)}, u32[]{:S(2)}) collective-permute-start(bf16[64,2048]{1,0:T(8,128)(2,1)} %collective-permute-done.8.refs_6_), channel_id=1, source_target_pairs={{0,1},{1,0},{2,3},{3,2},{4,5},{5,4},{6,7},{7,6},{8,9},{9,8},{10,11... | collective-permute-start | bytes 786440 | tf_op jit(solution)/shard_map/ppermute | solution.py:189
  36.9 3.8 %collective-permute-start.7 = (bf16[64,2048]{1,0:T(8,128)(2,1)}, bf16[64,2048]{1,0:T(8,128)(2,1)}, u32[]{:S(2)}, u32[]{:S(2)}) collective-permute-start(bf16[64,2048]{1,0:T(8,128)(2,1)} %collective-permute-done.6.refs_4_), channel_id=1, source_target_pairs={{0,1},{1,0},{2,3},{3,2},{4,5},{5,4},{6,7},{7,6},{8,9},{9,8},{10,11... | collective-permute-start | bytes 786440 | tf_op jit(solution)/shard_map/ppermute | solution.py:189
  39.7 2.5 %collective-permute-start.5 = (bf16[64,2048]{1,0:T(8,128)(2,1)}, bf16[64,2048]{1,0:T(8,128)(2,1)}, u32[]{:S(2)}, u32[]{:S(2)}) collective-permute-start(bf16[64,2048]{1,0:T(8,128)(2,1)} %collective-permute-done.4.refs_2_), channel_id=1, source_target_pairs={{0,1},{1,0},{2,3},{3,2},{4,5},{5,4},{6,7},{7,6},{8,9},{9,8},{10,11... | collective-permute-start | bytes 786440 | tf_op jit(solution)/shard_map/ppermute | solution.py:189
  42.1 0.8 copy-start.1
  43.0 1.0 %copy-start.2 = (bf16[3,3,3,512,16]{3,4,2,1,0:T(8,128)(2,1)S(1)}, bf16[3,3,3,512,16]{3,4,2,1,0:T(8,128)(2,1)}, u32[]{:S(2)}) copy-start(bf16[3,3,3,512,16]{3,4,2,1,0:T(8,128)(2,1)} %param.5) | copy-start | bytes 1327108
  47.0 5.4 %collective-permute-start.10 = (bf16[16,2048]{1,0:T(8,128)(2,1)S(1)}, bf16[16,2048]{1,0:T(8,128)(2,1)S(1)}, u32[]{:S(2)}, u32[]{:S(2)}) collective-permute-start(bf16[16,2048]{1,0:T(8,128)(2,1)S(1)} %get-tuple-element.12), channel_id=1, source_target_pairs={{0,32},{32,64},{64,96},{96,128},{128,160},{160,192},{192,224},{224... | collective-permute-start | bytes 196616 | tf_op jit(solution)/shard_map/ppermute | solution.py:189
  48.0 6.5 %collective-permute-start.11 = (bf16[16,2048]{1,0:T(8,128)(2,1)S(1)}, bf16[16,2048]{1,0:T(8,128)(2,1)S(1)}, u32[]{:S(2)}, u32[]{:S(2)}) collective-permute-start(bf16[16,2048]{1,0:T(8,128)(2,1)S(1)} %get-tuple-element.13), channel_id=1, source_target_pairs={{0,64},{32,96},{64,128},{96,160},{128,192},{160,224},{192,0},{224,... | collective-permute-start | bytes 196616 | tf_op jit(solution)/shard_map/ppermute | solution.py:189
  73.7 8.9 %collective-permute-start.13 = (bf16[512,128]{1,0:T(8,128)(2,1)S(1)}, bf16[512,128]{1,0:T(8,128)(2,1)S(1)}, u32[]{:S(2)}, u32[]{:S(2)}) collective-permute-start(bf16[512,128]{1,0:T(8,128)(2,1)S(1)} %bitcast.15), channel_id=1, source_target_pairs={{0,64},{32,96},{64,128},{96,160},{128,192},{160,224},{192,0},{224,... | collective-permute-start | bytes 393224 | tf_op jit(solution)/shard_map/ppermute | solution.py:189
  73.7 8.9 %collective-permute-start.12 = (bf16[512,128]{1,0:T(8,128)(2,1)S(1)}, bf16[512,128]{1,0:T(8,128)(2,1)S(1)}, u32[]{:S(2)}, u32[]{:S(2)}) collective-permute-start(bf16[512,128]{1,0:T(8,128)(2,1)S(1)} %bitcast.16), channel_id=1, source_target_pairs={{0,32},{32,64},{64,96},{96,128},{128,160},{160,192},{192,224},{224... | collective-permute-start | bytes 393224 | tf_op jit(solution)/shard_map/ppermute | solution.py:189
  88.2 6.1 %collective-permute-start.14 = (bf16[256,256]{1,0:T(8,128)(2,1)S(1)}, bf16[256,256]{1,0:T(8,128)(2,1)S(1)}, u32[]{:S(2)}, u32[]{:S(2)}) collective-permute-start(bf16[256,256]{1,0:T(8,128)(2,1)S(1)} %get-tuple-element.15), channel_id=1, source_target_pairs={{0,32},{32,64},{64,96},{96,128},{128,160},{160,192},{192,224},{224... | collective-permute-start | bytes 393224 | tf_op jit(solution)/shard_map/ppermute | solution.py:189
  88.3 8.6 %collective-permute-start.15 = (bf16[256,256]{1,0:T(8,128)(2,1)S(1)}, bf16[256,256]{1,0:T(8,128)(2,1)S(1)}, u32[]{:S(2)}, u32[]{:S(2)}) collective-permute-start(bf16[256,256]{1,0:T(8,128)(2,1)S(1)} %get-tuple-element.16), channel_id=1, source_target_pairs={{0,64},{32,96},{64,128},{96,160},{128,192},{160,224},{192,0},{224,... | collective-permute-start | bytes 393224 | tf_op jit(solution)/shard_map/ppermute | solution.py:189

commit v2 on v1

v2 whole, which is shorter than its diff:
```python
import functools

import jax
import jax.numpy as jnp
from jax import lax
from jax.experimental import pallas as pl
from jax.experimental.pallas import tpu as pltpu
from jax.sharding import Mesh, PartitionSpec as P

PITCH = 32
LANES = 128
QUARTERS = 4
BF16 = jnp.bfloat16
F32 = jnp.float32
SMEM = pl.BlockSpec(memory_space=pltpu.SMEM)
ANY = pl.BlockSpec(memory_space=pl.ANY)
VMEM = pl.BlockSpec(memory_space=pltpu.VMEM)
LIMIT = 20 * 2**20


def call(kernel, out_shape, operands, scratch=(), specs=None):
    specs = specs or [SMEM] + [VMEM] * (len(operands) - 1)
    return pl.pallas_call(
        kernel,
        out_shape=out_shape,
        in_specs=specs,
        out_specs=jax.tree.map(lambda _: VMEM, out_shape),
        scratch_shapes=scratch,
        compiler_params=pltpu.CompilerParams(vmem_limit_bytes=LIMIT),
    )(*operands)


def silu(v):
    return v / (1.0 + jnp.exp(-v))


def column_mask(shape, axis, across):
    return lax.rem(lax.broadcasted_iota(jnp.int32, shape, axis), PITCH) < across


def before(block):
    lane = lax.broadcasted_iota(jnp.int32, block.shape, 1)
    return jnp.where(lane >= PITCH, pltpu.roll(block, PITCH, 1), 0.0)


def after(block):
    lane = lax.broadcasted_iota(jnp.int32, block.shape, 1)
    return jnp.where(lane < LANES - PITCH, pltpu.roll(block, LANES - PITCH, 1), 0.0)


def pack_kernel(field_ref, weight_ref, packed_ref, act_ref, slices_ref, raw_ref, columns_ref, rows_ref, sems):
    across, shard, height = field_ref.shape
    deep = height // QUARTERS
    load = pltpu.make_async_copy(field_ref, raw_ref, sems.at[4])
    load.start()
    width = weight_ref.shape[1] // 4
    copies = []
    for d in range(4):
        source = weight_ref.at[:, d * width : (d + 1) * width]
        copies.append(pltpu.make_async_copy(source, slices_ref.at[d], sems.at[d]))
        copies[d].start()
    columns_ref[...] = jnp.zeros(columns_ref.shape, F32)
    load.wait()
    columns_ref[: across * shard, :height] = raw_ref[...].astype(F32).reshape(across * shard, height)
    for c in range(shard):
        cells = columns_ref[pl.ds(c, PITCH, stride=shard), :].T
        quarters = [cells[q * deep : (q + 1) * deep] for q in range(QUARTERS)]
        rows_ref[pl.ds(c, deep, stride=shard), :] = jnp.concatenate(quarters, 1)
    for v in range(deep):
        values = rows_ref[v * shard : (v + 1) * shard, :]
        packed_ref[:, v * LANES : (v + 1) * LANES] = values.astype(BF16)
        act_ref[:, v * LANES : (v + 1) * LANES] = silu(values).astype(BF16)
    for copy in copies:
        copy.wait()


def coarse_kernel(at_ref, field_ref, slices_ref, *refs):
    blocks, (out_ref, all_ref, taps_ref, sum_ref) = refs[:8], refs[8:]
    shard, cells = field_ref.shape
    deep = cells // LANES
    group = 8 * shard
    wide = 4 * shard
    z, x, c, t = at_ref[0], at_ref[1], at_ref[2], at_ref[3]
    for n, block in enumerate(blocks):
        x_from = lax.rem(x + 4 - n // 2, 4)
        c_from = c if n % 2 == 0 else 1 - c
        base = (x_from * 2 + c_from) * shard
        for k in range(3):
            part = pl.multiple_of(jnp.minimum(t, 2 - k) * shard, shard)
            all_ref[pl.ds(pl.multiple_of(k * group + base, shard), shard), LANES : LANES + cells] = block[
                pl.ds(part, shard), :
            ]
    first, last = all_ref[:, LANES : 2 * LANES], all_ref[:, cells : cells + LANES]
    all_ref[:, :LANES] = before(last.astype(F32)).astype(BF16)
    all_ref[:, LANES + cells :] = after(first.astype(F32)).astype(BF16)
    for d in range(4):
        for k in range(3):
            for i in range(3):
                for j in range(3):
                    tap = (k * 3 + i) * 3 + j
                    to = j * wide + d * shard
                    taps_ref[i, to : to + shard, k * group : (k + 1) * group] = slices_ref[
                        d, tap * shard : (tap + 1) * shard, :
                    ]
    span = 4 * LANES
    for n in range(cells // span):
        total = None
        for i in range(3):
            lo = i * LANES + n * span
            part = jnp.dot(taps_ref[i], all_ref[:, lo : lo + span], preferred_element_type=F32)
            total = part if total is None else total + part
        for v in range(4):
            left, here, right = (total[j * wide : (j + 1) * wide, v * LANES : (v + 1) * LANES] for j in range(3))
            lo = LANES + n * span + v * LANES
            sum_ref[:, lo : lo + LANES] = pltpu.roll(left, 1, 1) + here + pltpu.roll(right, LANES - 1, 1)
    own = pl.ds(pl.multiple_of(z * shard, shard), shard)
    sum_ref[own, LANES : LANES + cells] = sum_ref[own, LANES : LANES + cells] + field_ref[...].astype(F32)
    sum_ref[:, :LANES] = before(sum_ref[:, cells : cells + LANES])
    sum_ref[:, LANES + cells :] = after(sum_ref[:, LANES : 2 * LANES])
    at = lax.broadcasted_iota(jnp.int32, (wide, LANES), 1) // PITCH
    for m in range(deep // 2):
        rows = [sum_ref[:, (2 * m + r) * LANES : (2 * m + r + 1) * LANES] for r in range(4)]
        for q in range(QUARTERS):
            moved = [pltpu.roll(rows[r], (r - q) % 4 * PITCH, 1) if r != q else rows[r] for r in range(4)]
            strip = jnp.where(at < 2, jnp.where(at < 1, moved[0], moved[1]), jnp.where(at < 3, moved[2], moved[3]))
            out_ref[q * (deep // 2) + m] = strip.astype(BF16)


def strip_kernel(across, parts_ref, out_ref, order_ref):
    shard = parts_ref.shape[1] // 4
    for n in range(8):
        total = None
        for z in range(4):
            part = parts_ref[z * 8 + n].astype(F32)
            total = part if total is None else total + part
        act = silu(total.astype(BF16).astype(F32))
        act = jnp.where(column_mask(act.shape, 1, across), act, 0.0)
        for z in range(4):
            order_ref[(z * 8 + n) * shard : (z * 8 + n + 1) * shard, :] = act[z * shard : (z + 1) * shard]
    out_ref[...] = order_ref[...].T.astype(BF16)


def down(v):
    return pltpu.roll(v, 1, 0)


def up(v):
    return pltpu.roll(v, v.shape[0] - 1, 0)


def fine_kernel(across, at_ref, a0_ref, a1_ref, a2_ref, wide_ref, last_ref, first_ref, second_ref, own_ref):
    t, strip, strips = at_ref[3], at_ref[4], at_ref[5]
    a0 = a0_ref[...].astype(F32)
    a1 = jnp.where(t >= 1, a1_ref[...].astype(F32), a0)
    a2 = jnp.where(t >= 2, a2_ref[...].astype(F32), a1)
    frames = jnp.concatenate([a2, a1, a0], 1).astype(BF16)
    spans = ((0, 3), (0, 4), (1, 4))
    maps = ((0, 0, 1, 1, 2, 2), (0, 1, 1, 2, 2, 3), (0, 0, 1, 1, 2, 2))
    even, odd = [None] * 6, [None] * 6
    for i in range(3):
        lo, hi = spans[i]
        sums = []
        for j in range(3):
            sums.append(
                jnp.dot(frames[lo * PITCH : hi * PITCH], wide_ref[i * 3 + j], preferred_element_type=F32)
            )
        at_even = down(sums[0]) + sums[1] + sums[2]
        at_odd = sums[0] + sums[1] + up(sums[2])
        for r in range(6):
            at = slice(maps[i][r] * PITCH, (maps[i][r] + 1) * PITCH)
            even[r] = at_even[at] if even[r] is None else even[r] + at_even[at]
            odd[r] = at_odd[at] if odd[r] is None else odd[r] + at_odd[at]
    mid = [jnp.concatenate(rows, 0).astype(BF16).astype(F32) for rows in (even, odd)]
    shape = mid[0].shape
    row = lax.broadcasted_iota(jnp.int32, shape, 0) // PITCH
    keep = column_mask(shape, 0, across)
    keep = keep & ((row > 0) | (strip > 0)) & ((row < 5) | (strip < strips - 1))
    acts = [jnp.where(keep, silu(m), 0.0).astype(BF16) for m in mid]
    size = 4 * PITCH
    sums = []
    for k in range(3):
        parts = []
        for j in range(3):
            total = None
            for i in range(3):
                rows = slice(i * PITCH, i * PITCH + size)
                both = jnp.concatenate([acts[0][rows], acts[1][rows]], 0)
                part = jnp.dot(both, last_ref[k, i, j], preferred_element_type=F32)
                total = part if total is None else total + part
            parts.append(total)
        at_even = down(parts[0][size:]) + parts[1][:size] + parts[2][size:]
        at_odd = parts[0][:size] + parts[1][size:] + up(parts[2][:size])
        sums.append(jnp.concatenate([at_even, at_odd], 0))
    start = t == 0
    late = sums[0] + sums[1]
    first_ref[...] = jnp.where(start, late, sums[1]).astype(BF16)
    second_ref[...] = sums[0].astype(BF16)
    rows = slice(PITCH, PITCH + size)
    own = jnp.concatenate([mid[0][rows], mid[1][rows]], 0) + sums[2]
    own_ref[...] = jnp.where(start, own + late, own)


def last_kernel(across, at_ref, own_ref, first_ref, second_ref, out_ref, order_ref):
    t = at_ref[3]
    zero = jnp.zeros(own_ref.shape, F32)
    total = (
        own_ref[...]
        + jnp.where(t >= 1, first_ref[...].astype(F32), zero)
        + jnp.where(t >= 2, second_ref[...].astype(F32), zero)
    )
    for parity in range(2):
        for h in range(4):
            at = (parity * 4 + h) * PITCH
            for half in range(2):
                order_ref[half, pl.ds(4 * parity + h, PITCH, stride=8), :] = total[
                    at : at + PITCH, 128 * half : 128 * half + 128
                ]
    for half in range(2):
        out_ref[:, 128 * half : 128 * half + 128] = order_ref[half, : 4 * across * 2].astype(BF16)


def turned(block, axis, distance):
    count = lax.axis_size(axis)
    return lax.ppermute(block, axis, [(i, (i + distance) % count) for i in range(count)])


def on_device(features, weight_one, weight_two, weight_three):
    own_block = features[0]
    height, across, shard = own_block.shape
    channels = weight_one.shape[3]
    cells = height * PITCH
    tp = ("z", "x", "c")
    at = jnp.stack(
        [lax.axis_index(a) for a in ("z", "x", "c", "tm")] + [lax.axis_index(tp), lax.axis_size(tp)]
    ).astype(jnp.int32)
    kernel = jnp.transpose(weight_one, (0, 1, 2, 4, 3)).reshape(27 * shard, channels)
    small = jax.ShapeDtypeStruct((shard, cells), BF16)
    field, act_in, slices = call(
        pack_kernel,
        (small, small, jax.ShapeDtypeStruct((4, 27 * shard, channels // 4), BF16)),
        (jnp.transpose(own_block, (1, 2, 0)), kernel),
        (
            pltpu.VMEM((across, shard, height), BF16),
            pltpu.VMEM((PITCH * shard, LANES), F32),
            pltpu.VMEM((cells // LANES * shard, LANES), F32),
            pltpu.SemaphoreType.DMA((5,)),
        ),
        [ANY, ANY],
    )
    frames = jnp.concatenate([act_in, turned(act_in, "tm", 1), turned(act_in, "tm", 2)], 0)
    slices = lax.all_to_all(slices, "z", 0, 0, tiled=True)
    blocks = []
    for d in range(4):
        block = turned(frames, "x", d) if d else frames
        blocks += [block, turned(block, "c", 1)]
    strips = lax.axis_size(tp)
    cut = call(
        coarse_kernel,
        jax.ShapeDtypeStruct((strips, 4 * shard, LANES), BF16),
        (at, field, slices, *blocks),
        (
            pltpu.VMEM((3 * channels // 4, cells + 2 * LANES), BF16),
            pltpu.VMEM((3, 12 * shard, 3 * channels // 4), BF16),
            pltpu.VMEM((4 * shard, cells + 2 * LANES), F32),
        ),
    )
    parts = lax.all_to_all(cut, tp, 0, 0, tiled=True)
    strip = pl.pallas_call(
        functools.partial(strip_kernel, across),
        out_shape=jax.ShapeDtypeStruct((LANES, channels), BF16),
        scratch_shapes=[pltpu.VMEM((channels, LANES), F32)],
        compiler_params=pltpu.CompilerParams(vmem_limit_bytes=LIMIT),
    )(parts)
    width = weight_two.shape[4]
    wide = jnp.transpose(weight_two, (1, 2, 0, 3, 4)).reshape(9, 3 * channels, width)
    small = jax.ShapeDtypeStruct((8 * PITCH, width), BF16)
    first, second, own = call(
        functools.partial(fine_kernel, across),
        (small, small, jax.ShapeDtypeStruct((8 * PITCH, width), F32)),
        (at, strip, turned(strip, "tm", 1), turned(strip, "tm", 2), wide, weight_three),
    )
    decoded = call(
        functools.partial(last_kernel, across),
        jax.ShapeDtypeStruct((8 * across, width), BF16),
        (at, own, turned(first, "tm", 1), turned(second, "tm", 2)),
        (pltpu.VMEM((2, 8 * PITCH, 128), F32),),
    )
    return jnp.transpose(decoded.reshape(2 * across, 4, width), (1, 0, 2))[None]


def solution(mesh):
    grid = Mesh(mesh.devices.reshape(mesh.shape["tm"], 4, 4, 2), ("tm", "z", "x", "c"))
    tp = ("z", "x", "c")
    return jax.shard_map(
        on_device,
        mesh=grid,
        in_specs=(P("tm", None, None, tp), P(None, None, None, None, tp), P(), P()),
        out_specs=P("tm", tp, None, None),
        check_vma=False,
    )
```

time: 98.7 us -> 80.5 us (0.82)
  waiting for transfers between devices: 32 us -> 10.5 us
  blocking collectives: 18.5 us -> 24.2 us
  starting transfers between devices: 28.1 us -> 30.7 us
  Pallas kernels: 9.93 us -> 7.96 us
  other arithmetic: 1.6 us -> 0 us
  local copies, waits for them, and re-layouts: 8.14 us -> 6.69 us
    ppermute x16 -> x13, waiting for transfers between devices: 32 us -> 10.5 us  [turned(): lax.ppermute(block, axis, [(i, (i + distance) % count) for i in range(cou...]
    all_to_all x0 -> x1, starting transfers between devices: none -> 7.28 us  [on_device(): slices = lax.all_to_all(slices, 'z', 0, 0, tiled=True)]
    all_to_all x1, blocking collectives: 18.5 us -> 24.2 us  [on_device(): parts = lax.all_to_all(cut, tp, 0, 0, tiled=True)]
    ppermute x16 -> x13, starting transfers between devices: 28.1 us -> 23.5 us  [turned(): lax.ppermute(block, axis, [(i, (i + distance) % count) for i in range(cou...]
    transpose x0 -> x1, local copies, waits for them, and re-layouts: none -> 3.61 us  [on_device(): jnp.transpose(weight_two, (1, 2, 0, 3, 4)).reshape(9, 3 * channels, width)]
    pallas_call x4, Pallas kernels: 9.93 us -> 7.74 us  [call(): pl.pallas_call(kernel, out_shape=out_shape, in_specs=specs, out_specs=jax...]
    reshape x1 -> x0, local copies, waits for them, and re-layouts: 1.86 us -> none  [on_device(): jnp.pad(jnp.transpose(own_block, (2, 0, 1)), ((0, 0), (0, 0), (0, PITCH -...]
    pad x1 -> x0, local copies, waits for them, and re-layouts: 1.71 us -> none  [on_device(): jnp.pad(jnp.transpose(own_block, (2, 0, 1)), ((0, 0), (0, 0), (0, PITCH -...]
  transfers between devices with their start and end apart: 16 -> 14, of which waited for: 10 -> 5; matrix products, arithmetic and copies ran while one was open for 0% -> 5% of each run, Pallas kernels for 0% -> 0%
where the time goes in v2:
time: 80.5 us; the launch traced here: 80.3 us
  starting transfers between devices  30.7 us (38%)
  blocking collectives  24.2 us (30%)
  waiting for transfers between devices  10.5 us (13%)
  Pallas kernels  7.96 us (10%)
  local copies, waits for them, and re-layouts  6.69 us (8%)
    all_to_all x1, blocking collectives, on_device(): parts = lax.all_to_all(cut, tp, 0, 0, tiled=True)  24.2 us
    ppermute x13, starting transfers between devices, turned(): lax.ppermute(block, axis, [(i, (i + distance) % count) for i in range(cou...  23.5 us
    ppermute x13, waiting for transfers between devices, turned(): lax.ppermute(block, axis, [(i, (i + distance) % count) for i in range(cou...  10.5 us
    pallas_call x4, Pallas kernels, call(): pl.pallas_call(kernel, out_shape=out_shape, in_specs=specs, out_specs=jax...  7.74 us
    all_to_all x1, starting transfers between devices, on_device(): slices = lax.all_to_all(slices, 'z', 0, 0, tiled=True)  7.28 us
    transpose x1, local copies, waits for them, and re-layouts, on_device(): jnp.transpose(weight_two, (1, 2, 0, 3, 4)).reshape(9, 3 * channels, width)  3.61 us
    unnamed x8, local copies, waits for them, and re-layouts  2.3 us
  transfers between devices with their start and end apart: 14, of which 5 were waited for; matrix products, arithmetic and copies ran while one was open for 5% of the time, Pallas kernels for 0%

profile of v2, /device:TPU:1, one launch (start us, length us, event | category | flops | bytes accessed | tf_op | source)
XLA Modules:
  0.0 80.3 jit_solution(14434768537366325159)
XLA Ops:
  0.0 1.0 %copy-done.1 = bf16[3,3,3,512,16]{3,4,2,1,0:T(8,128)(2,1)S(1)} copy-done((bf16[3,3,3,512,16]{3,4,2,1,0:T(8,128)(2,1)S(1)}, bf16[3,3,3,512,16]{3,4,2,1,0:T(8,128)(2,1)}, u32[]{:S(2)}) %copy-start.1) | copy-done | bytes 442392
  1.0 0.9 %copy-done.2 = bf16[1,64,30,16]{1,3,2,0:T(8,128)(2,1)S(1)} copy-done((bf16[1,64,30,16]{1,3,2,0:T(8,128)(2,1)S(1)}, bf16[1,64,30,16]{1,3,2,0:T(8,128)(2,1)}, u32[]{:S(2)}) %copy-start.2) | copy-done | bytes 61464
  1.9 1.4 %shard_map.46 = (bf16[16,2048]{1,0:T(8,128)(2,1)S(1)}, bf16[16,2048]{1,0:T(8,128)(2,1)S(1)}, bf16[4,432,128]{2,1,0:T(8,128)(2,1)}) custom-call(bf16[30,16,64]{2,1,0:T(8,128)(2,1)S(1)} %bitcast.18, bf16[432,512]{1,0:T(8,128)(2,1)S(1)} %bitcast.17), custom_call_target="tpu_custom_call" | custom-call | tf_op jit(solution)/shard_map/pallas_call | solution.py:23
  3.3 2.2 %collective-permute-start.1 = (bf16[16,2048]{1,0:T(8,128)(2,1)S(1)}, bf16[16,2048]{1,0:T(8,128)(2,1)S(1)}, u32[]{:S(2)}, u32[]{:S(2)}) collective-permute-start(bf16[16,2048]{1,0:T(8,128)(2,1)S(1)} %get-tuple-element.13), channel_id=1, source_target_pairs={{0,64},{32,96},{64,128},{96,160},{128,192},{160,224},{192,0},{224,... | collective-permute-start | bytes 196616 | tf_op jit(solution)/shard_map/ppermute | solution.py:224
  5.5 1.6 %collective-permute-start = (bf16[16,2048]{1,0:T(8,128)(2,1)S(1)}, bf16[16,2048]{1,0:T(8,128)(2,1)S(1)}, u32[]{:S(2)}, u32[]{:S(2)}) collective-permute-start(bf16[16,2048]{1,0:T(8,128)(2,1)S(1)} %get-tuple-element.13), channel_id=1, source_target_pairs={{0,32},{32,64},{64,96},{96,128},{128,160},{160,192},{192,224},{224... | collective-permute-start | bytes 196616 | tf_op jit(solution)/shard_map/ppermute | solution.py:224
  7.2 7.3 %all-to-all-start = ((bf16[4,432,128]{2,1,0:T(8,128)(2,1)}), bf16[4,432,128]{2,1,0:T(8,128)(2,1)S(1)}, u32[]{:S(2)}, u32[]{:S(2)}) async-start(bf16[4,432,128]{2,1,0:T(8,128)(2,1)} %get-tuple-element.12), calls=%async_computation | async-start | bytes 884736 | tf_op jit(solution)/shard_map/all_to_all | solution.py:251
  14.5 2.6 %collective-permute-start.7 = (bf16[48,2048]{1,0:T(8,128)(2,1)S(1)}, bf16[48,2048]{1,0:T(8,128)(2,1)S(1)}, u32[]{:S(2)}, u32[]{:S(2)}) collective-permute-start(bf16[48,2048]{1,0:T(8,128)(2,1)S(1)} %constant_dynamic-update-slice_fusion.refs_0_), channel_id=1, source_target_pairs={{0,6},{2,0},{4,2},{6,4},{1,7},{3,1},{5,3},{7,5},{8,14},{10,8},{12,... | collective-permute-start | bytes 589832 | tf_op jit(solution)/shard_map/ppermute | solution.py:224
  18.2 2.4 %collective-permute-start.2 = (bf16[48,2048]{1,0:T(8,128)(2,1)S(1)}, bf16[48,2048]{1,0:T(8,128)(2,1)S(1)}, u32[]{:S(2)}, u32[]{:S(2)}) collective-permute-start(bf16[48,2048]{1,0:T(8,128)(2,1)S(1)} %constant_dynamic-update-slice_fusion.refs_0_), channel_id=1, source_target_pairs={{0,1},{1,0},{2,3},{3,2},{4,5},{5,4},{6,7},{7,6},{8,9},{9,8},{10,11... | collective-permute-start | bytes 589832 | tf_op jit(solution)/shard_map/ppermute | solution.py:224
  20.6 1.1 %collective-permute-done.7.refs_6_ = bf16[48,2048]{1,0:T(8,128)(2,1)S(1)} collective-permute-done((bf16[48,2048]{1,0:T(8,128)(2,1)S(1)}, bf16[48,2048]{1,0:T(8,128)(2,1)S(1)}, u32[]{:S(2)}, u32[]{:S(2)}) %collective-permute-start.7) | collective-permute-done | bytes 196640 | tf_op jit(solution)/shard_map/ppermute | solution.py:224
  21.7 4.8 %collective-permute-start.8 = (bf16[48,2048]{1,0:T(8,128)(2,1)S(1)}, bf16[48,2048]{1,0:T(8,128)(2,1)S(1)}, u32[]{:S(2)}, u32[]{:S(2)}) collective-permute-start(bf16[48,2048]{1,0:T(8,128)(2,1)S(1)} %collective-permute-done.7.refs_6_), channel_id=1, source_target_pairs={{0,1},{1,0},{2,3},{3,2},{4,5},{5,4},{6,7},{7,6},{8,9},{9,8},{10,11... | collective-permute-start | bytes 589832 | tf_op jit(solution)/shard_map/ppermute | solution.py:224
  26.4 1.6 %collective-permute-start.6 = (bf16[48,2048]{1,0:T(8,128)(2,1)S(1)}, bf16[48,2048]{1,0:T(8,128)(2,1)S(1)}, u32[]{:S(2)}, u32[]{:S(2)}) collective-permute-start(bf16[48,2048]{1,0:T(8,128)(2,1)S(1)} %collective-permute-done.5.refs_4_), channel_id=1, source_target_pairs={{0,1},{1,0},{2,3},{3,2},{4,5},{5,4},{6,7},{7,6},{8,9},{9,8},{10,11... | collective-permute-start | bytes 589832 | tf_op jit(solution)/shard_map/ppermute | solution.py:224
  28.1 1.1 %collective-permute-done.3.refs_2_ = bf16[48,2048]{1,0:T(8,128)(2,1)S(1)} collective-permute-done((bf16[48,2048]{1,0:T(8,128)(2,1)S(1)}, bf16[48,2048]{1,0:T(8,128)(2,1)S(1)}, u32[]{:S(2)}, u32[]{:S(2)}) %collective-permute-start.3) | collective-permute-done | bytes 196640 | tf_op jit(solution)/shard_map/ppermute | solution.py:224
  29.2 0.9 %collective-permute-start.4 = (bf16[48,2048]{1,0:T(8,128)(2,1)S(1)}, bf16[48,2048]{1,0:T(8,128)(2,1)S(1)}, u32[]{:S(2)}, u32[]{:S(2)}) collective-permute-start(bf16[48,2048]{1,0:T(8,128)(2,1)S(1)} %collective-permute-done.3.refs_2_), channel_id=1, source_target_pairs={{0,1},{1,0},{2,3},{3,2},{4,5},{5,4},{6,7},{7,6},{8,9},{9,8},{10,11... | collective-permute-start | bytes 589832 | tf_op jit(solution)/shard_map/ppermute | solution.py:224
  30.2 1.0 %collective-permute-done.4.refs_3_ = bf16[48,2048]{1,0:T(8,128)(2,1)S(1)} collective-permute-done((bf16[48,2048]{1,0:T(8,128)(2,1)S(1)}, bf16[48,2048]{1,0:T(8,128)(2,1)S(1)}, u32[]{:S(2)}, u32[]{:S(2)}) %collective-permute-start.4) | collective-permute-done | bytes 196640 | tf_op jit(solution)/shard_map/ppermute | solution.py:224
  31.2 2.6 %shard_map.47 = bf16[32,64,128]{2,1,0:T(8,128)(2,1)S(1)} custom-call(s32[6]{0:T(128)S(1)} %stack.23.at_ref, bf16[16,2048]{1,0:T(8,128)(2,1)S(1)} %get-tuple-element.11.field_ref, bf16[4,432,128]{2,1,0:T(8,128)(2,1)S(1)} %all-to-all-done.slices_ref, bf16[48,2048]{1,0:T(8,128)(2,1)S(1)} %constant_dynamic-update-slice_fusion.refs_0_, ...), custom_call_target="tpu_custom_call" | custom-call | tf_op jit(solution)/shard_map/pallas_call | solution.py:23
  33.8 24.2 %all_to_all.10.parts_ref = bf16[32,64,128]{2,1,0:T(8,128)(2,1)S(1)} all-to-all(bf16[32,64,128]{2,1,0:T(8,128)(2,1)S(1)} %shard_map.47), channel_id=1, replica_groups=mesh['tm'=8,'z'=4,'x'=4,'c'=2] {'z','x','c'}, dimensions={0} | all-to-all | bytes 1048576 | tf_op jit(solution)/shard_map/all_to_all | solution.py:267
  58.3 1.5 %collective-permute-start.10 = (bf16[128,512]{1,0:T(8,128)(2,1)S(1)}, bf16[128,512]{1,0:T(8,128)(2,1)S(1)}, u32[]{:S(2)}, u32[]{:S(2)}) collective-permute-start(bf16[128,512]{1,0:T(8,128)(2,1)S(1)} %shard_map.48.a0_ref), channel_id=1, source_target_pairs={{0,64},{32,96},{64,128},{96,160},{128,192},{160,224},{192,0},{224,... | collective-permute-start | bytes 393224 | tf_op jit(solution)/shard_map/ppermute | solution.py:224
  59.8 2.5 %collective-permute-start.9 = (bf16[128,512]{1,0:T(8,128)(2,1)S(1)}, bf16[128,512]{1,0:T(8,128)(2,1)S(1)}, u32[]{:S(2)}, u32[]{:S(2)}) collective-permute-start(bf16[128,512]{1,0:T(8,128)(2,1)S(1)} %shard_map.48.a0_ref), channel_id=1, source_target_pairs={{0,32},{32,64},{64,96},{96,128},{128,160},{160,192},{192,224},{224... | collective-permute-start | bytes 393224 | tf_op jit(solution)/shard_map/ppermute | solution.py:224
  62.3 3.6 %copy.5 = bf16[3,3,3,512,256]{4,3,2,1,0:T(8,128)(2,1)S(1)} copy(bf16[3,3,3,512,256]{4,3,1,0,2:T(8,128)(2,1)} %bitcast.19) | data formatting | bytes 14155776 | tf_op jit(solution)/shard_map/transpose | solution.py:275
  66.3 3.0 %shard_map.49 = (bf16[256,256]{1,0:T(8,128)(2,1)S(1)}, bf16[256,256]{1,0:T(8,128)(2,1)S(1)}, f32[256,256]{1,0:T(8,128)S(1)}) custom-call(s32[6]{0:T(128)S(1)} %stack.23.at_ref, bf16[128,512]{1,0:T(8,128)(2,1)S(1)} %shard_map.48.a0_ref, bf16[128,512]{1,0:T(8,128)(2,1)S(1)} %collective-permute-done.9.a1_ref, ...), custom_call_target="tpu_custom_call" | custom-call | tf_op jit(solution)/shard_map/pallas_call | solution.py:23
  69.3 1.4 %collective-permute-start.11 = (bf16[256,256]{1,0:T(8,128)(2,1)S(1)}, bf16[256,256]{1,0:T(8,128)(2,1)S(1)}, u32[]{:S(2)}, u32[]{:S(2)}) collective-permute-start(bf16[256,256]{1,0:T(8,128)(2,1)S(1)} %get-tuple-element.15), channel_id=1, source_target_pairs={{0,32},{32,64},{64,96},{96,128},{128,160},{160,192},{192,224},{224... | collective-permute-start | bytes 393224 | tf_op jit(solution)/shard_map/ppermute | solution.py:224
  70.7 1.0 %collective-permute-start.12 = (bf16[256,256]{1,0:T(8,128)(2,1)S(1)}, bf16[256,256]{1,0:T(8,128)(2,1)S(1)}, u32[]{:S(2)}, u32[]{:S(2)}) collective-permute-start(bf16[256,256]{1,0:T(8,128)(2,1)S(1)} %get-tuple-element.16), channel_id=1, source_target_pairs={{0,64},{32,96},{64,128},{96,160},{128,192},{160,224},{192,0},{224,... | collective-permute-start | bytes 393224 | tf_op jit(solution)/shard_map/ppermute | solution.py:224
  71.6 3.8 %collective-permute-done.11.first_ref = bf16[256,256]{1,0:T(8,128)(2,1)S(1)} collective-permute-done((bf16[256,256]{1,0:T(8,128)(2,1)S(1)}, bf16[256,256]{1,0:T(8,128)(2,1)S(1)}, u32[]{:S(2)}, u32[]{:S(2)}) %collective-permute-start.11) | collective-permute-done | bytes 131104 | tf_op jit(solution)/shard_map/ppermute | solution.py:224
  75.4 3.5 %collective-permute-done.12.second_ref = bf16[256,256]{1,0:T(8,128)(2,1)S(1)} collective-permute-done((bf16[256,256]{1,0:T(8,128)(2,1)S(1)}, bf16[256,256]{1,0:T(8,128)(2,1)S(1)}, u32[]{:S(2)}, u32[]{:S(2)}) %collective-permute-start.12) | collective-permute-done | bytes 131104 | tf_op jit(solution)/shard_map/ppermute | solution.py:224
  (22 shorter events, 3.2 us)
Async XLA Ops:
  0.0 1.0 %copy-start.1 = (bf16[3,3,3,512,16]{3,4,2,1,0:T(8,128)(2,1)S(1)}, bf16[3,3,3,512,16]{3,4,2,1,0:T(8,128)(2,1)}, u32[]{:S(2)}) copy-start(bf16[3,3,3,512,16]{3,4,2,1,0:T(8,128)(2,1)} %param.5) | copy-start | bytes 1327108
  1.0 0.9 %copy-start.2 = (bf16[1,64,30,16]{1,3,2,0:T(8,128)(2,1)S(1)}, bf16[1,64,30,16]{1,3,2,0:T(8,128)(2,1)}, u32[]{:S(2)}) copy-start(bf16[1,64,30,16]{1,3,2,0:T(8,128)(2,1)} %param.4) | copy-start | bytes 184324
  3.3 11.2 %collective-permute-start.1 = (bf16[16,2048]{1,0:T(8,128)(2,1)S(1)}, bf16[16,2048]{1,0:T(8,128)(2,1)S(1)}, u32[]{:S(2)}, u32[]{:S(2)}) collective-permute-start(bf16[16,2048]{1,0:T(8,128)(2,1)S(1)} %get-tuple-element.13), channel_id=1, source_target_pairs={{0,64},{32,96},{64,128},{96,160},{128,192},{160,224},{192,0},{224,... | collective-permute-start | bytes 196616 | tf_op jit(solution)/shard_map/ppermute | solution.py:224
  5.5 8.9 %collective-permute-start = (bf16[16,2048]{1,0:T(8,128)(2,1)S(1)}, bf16[16,2048]{1,0:T(8,128)(2,1)S(1)}, u32[]{:S(2)}, u32[]{:S(2)}) collective-permute-start(bf16[16,2048]{1,0:T(8,128)(2,1)S(1)} %get-tuple-element.13), channel_id=1, source_target_pairs={{0,32},{32,64},{64,96},{96,128},{128,160},{160,192},{192,224},{224... | collective-permute-start | bytes 196616 | tf_op jit(solution)/shard_map/ppermute | solution.py:224
  7.2 24.0 %all-to-all-start = ((bf16[4,432,128]{2,1,0:T(8,128)(2,1)}), bf16[4,432,128]{2,1,0:T(8,128)(2,1)S(1)}, u32[]{:S(2)}, u32[]{:S(2)}) async-start(bf16[4,432,128]{2,1,0:T(8,128)(2,1)} %get-tuple-element.12), calls=%async_computation | async-start | bytes 884736 | tf_op jit(solution)/shard_map/all_to_all | solution.py:251
  14.5 7.1 %collective-permute-start.7 = (bf16[48,2048]{1,0:T(8,128)(2,1)S(1)}, bf16[48,2048]{1,0:T(8,128)(2,1)S(1)}, u32[]{:S(2)}, u32[]{:S(2)}) collective-permute-start(bf16[48,2048]{1,0:T(8,128)(2,1)S(1)} %constant_dynamic-update-slice_fusion.refs_0_), channel_id=1, source_target_pairs={{0,6},{2,0},{4,2},{6,4},{1,7},{3,1},{5,3},{7,5},{8,14},{10,8},{12,... | collective-permute-start | bytes 589832 | tf_op jit(solution)/shard_map/ppermute | solution.py:224
  17.1 9.4 %collective-permute-start.5 = (bf16[48,2048]{1,0:T(8,128)(2,1)S(1)}, bf16[48,2048]{1,0:T(8,128)(2,1)S(1)}, u32[]{:S(2)}, u32[]{:S(2)}) collective-permute-start(bf16[48,2048]{1,0:T(8,128)(2,1)S(1)} %constant_dynamic-update-slice_fusion.refs_0_), channel_id=1, source_target_pairs={{0,4},{2,6},{4,0},{6,2},{1,5},{3,7},{5,1},{7,3},{8,12},{10,14},{12... | collective-permute-start | bytes 589832 | tf_op jit(solution)/shard_map/ppermute | solution.py:224
  17.6 11.6 %collective-permute-start.3 = (bf16[48,2048]{1,0:T(8,128)(2,1)S(1)}, bf16[48,2048]{1,0:T(8,128)(2,1)S(1)}, u32[]{:S(2)}, u32[]{:S(2)}) collective-permute-start(bf16[48,2048]{1,0:T(8,128)(2,1)S(1)} %constant_dynamic-update-slice_fusion.refs_0_), channel_id=1, source_target_pairs={{0,2},{2,4},{4,6},{6,0},{1,3},{3,5},{5,7},{7,1},{8,10},{10,12},{12... | collective-permute-start | bytes 589832 | tf_op jit(solution)/shard_map/ppermute | solution.py:224
  18.2 12.0 %collective-permute-start.2 = (bf16[48,2048]{1,0:T(8,128)(2,1)S(1)}, bf16[48,2048]{1,0:T(8,128)(2,1)S(1)}, u32[]{:S(2)}, u32[]{:S(2)}) collective-permute-start(bf16[48,2048]{1,0:T(8,128)(2,1)S(1)} %constant_dynamic-update-slice_fusion.refs_0_), channel_id=1, source_target_pairs={{0,1},{1,0},{2,3},{3,2},{4,5},{5,4},{6,7},{7,6},{8,9},{9,8},{10,11... | collective-permute-start | bytes 589832 | tf_op jit(solution)/shard_map/ppermute | solution.py:224
  21.7 8.5 %collective-permute-start.8 = (bf16[48,2048]{1,0:T(8,128)(2,1)S(1)}, bf16[48,2048]{1,0:T(8,128)(2,1)S(1)}, u32[]{:S(2)}, u32[]{:S(2)}) collective-permute-start(bf16[48,2048]{1,0:T(8,128)(2,1)S(1)} %collective-permute-done.7.refs_6_), channel_id=1, source_target_pairs={{0,1},{1,0},{2,3},{3,2},{4,5},{5,4},{6,7},{7,6},{8,9},{9,8},{10,11... | collective-permute-start | bytes 589832 | tf_op jit(solution)/shard_map/ppermute | solution.py:224
  26.4 3.8 %collective-permute-start.6 = (bf16[48,2048]{1,0:T(8,128)(2,1)S(1)}, bf16[48,2048]{1,0:T(8,128)(2,1)S(1)}, u32[]{:S(2)}, u32[]{:S(2)}) collective-permute-start(bf16[48,2048]{1,0:T(8,128)(2,1)S(1)} %collective-permute-done.5.refs_4_), channel_id=1, source_target_pairs={{0,1},{1,0},{2,3},{3,2},{4,5},{5,4},{6,7},{7,6},{8,9},{9,8},{10,11... | collective-permute-start | bytes 589832 | tf_op jit(solution)/shard_map/ppermute | solution.py:224
  29.2 2.0 %collective-permute-start.4 = (bf16[48,2048]{1,0:T(8,128)(2,1)S(1)}, bf16[48,2048]{1,0:T(8,128)(2,1)S(1)}, u32[]{:S(2)}, u32[]{:S(2)}) collective-permute-start(bf16[48,2048]{1,0:T(8,128)(2,1)S(1)} %collective-permute-done.3.refs_2_), channel_id=1, source_target_pairs={{0,1},{1,0},{2,3},{3,2},{4,5},{5,4},{6,7},{7,6},{8,9},{9,8},{10,11... | collective-permute-start | bytes 589832 | tf_op jit(solution)/shard_map/ppermute | solution.py:224
  58.3 7.6 %collective-permute-start.10 = (bf16[128,512]{1,0:T(8,128)(2,1)S(1)}, bf16[128,512]{1,0:T(8,128)(2,1)S(1)}, u32[]{:S(2)}, u32[]{:S(2)}) collective-permute-start(bf16[128,512]{1,0:T(8,128)(2,1)S(1)} %shard_map.48.a0_ref), channel_id=1, source_target_pairs={{0,64},{32,96},{64,128},{96,160},{128,192},{160,224},{192,0},{224,... | collective-permute-start | bytes 393224 | tf_op jit(solution)/shard_map/ppermute | solution.py:224
  59.8 6.1 %collective-permute-start.9 = (bf16[128,512]{1,0:T(8,128)(2,1)S(1)}, bf16[128,512]{1,0:T(8,128)(2,1)S(1)}, u32[]{:S(2)}, u32[]{:S(2)}) collective-permute-start(bf16[128,512]{1,0:T(8,128)(2,1)S(1)} %shard_map.48.a0_ref), channel_id=1, source_target_pairs={{0,32},{32,64},{64,96},{96,128},{128,160},{160,192},{192,224},{224... | collective-permute-start | bytes 393224 | tf_op jit(solution)/shard_map/ppermute | solution.py:224
  62.3 4.0 %copy-start = (bf16[3,3,3,256,256]{4,3,2,1,0:T(8,128)(2,1)S(1)}, bf16[3,3,3,256,256]{4,3,2,1,0:T(8,128)(2,1)}, u32[]{:S(2)}) copy-start(bf16[3,3,3,256,256]{4,3,2,1,0:T(8,128)(2,1)} %last_ref.1) | copy-start | bytes 10616836
  69.3 6.1 %collective-permute-start.11 = (bf16[256,256]{1,0:T(8,128)(2,1)S(1)}, bf16[256,256]{1,0:T(8,128)(2,1)S(1)}, u32[]{:S(2)}, u32[]{:S(2)}) collective-permute-start(bf16[256,256]{1,0:T(8,128)(2,1)S(1)} %get-tuple-element.15), channel_id=1, source_target_pairs={{0,32},{32,64},{64,96},{96,128},{128,160},{160,192},{192,224},{224... | collective-permute-start | bytes 393224 | tf_op jit(solution)/shard_map/ppermute | solution.py:224
  70.7 8.2 %collective-permute-start.12 = (bf16[256,256]{1,0:T(8,128)(2,1)S(1)}, bf16[256,256]{1,0:T(8,128)(2,1)S(1)}, u32[]{:S(2)}, u32[]{:S(2)}) collective-permute-start(bf16[256,256]{1,0:T(8,128)(2,1)S(1)} %get-tuple-element.16), channel_id=1, source_target_pairs={{0,64},{32,96},{64,128},{96,160},{128,192},{160,224},{192,0},{224,... | collective-permute-start | bytes 393224 | tf_op jit(solution)/shard_map/ppermute | solution.py:224

commit v3 on v2

--- a/solution.py
+++ b/solution.py
@@ -13,7 +13,7 @@
 BF16 = jnp.bfloat16
 F32 = jnp.float32
 SMEM = pl.BlockSpec(memory_space=pltpu.SMEM)
-ANY = pl.BlockSpec(memory_space=pl.ANY)
+HBM = pl.BlockSpec(memory_space=pltpu.HBM)
 VMEM = pl.BlockSpec(memory_space=pltpu.VMEM)
 LIMIT = 20 * 2**20
 
@@ -238,14 +238,14 @@
     field, act_in, slices = call(
         pack_kernel,
         (small, small, jax.ShapeDtypeStruct((4, 27 * shard, channels // 4), BF16)),
-        (jnp.transpose(own_block, (1, 2, 0)), kernel),
+        tuple(pltpu.with_memory_space_constraint(a, pltpu.HBM) for a in (jnp.transpose(own_block, (1, 2, 0)), kernel)),
         (
             pltpu.VMEM((across, shard, height), BF16),
             pltpu.VMEM((PITCH * shard, LANES), F32),
             pltpu.VMEM((cells // LANES * shard, LANES), F32),
             pltpu.SemaphoreType.DMA((5,)),
         ),
-        [ANY, ANY],
+        [HBM, HBM],
     )
     frames = jnp.concatenate([act_in, turned(act_in, "tm", 1), turned(act_in, "tm", 2)], 0)
     slices = lax.all_to_all(slices, "z", 0, 0, tiled=True)

time: 80.5 us -> 79.2 us (0.984)
  local copies, waits for them, and re-layouts: 6.69 us -> 4.77 us
    unnamed x8 -> x4, local copies, waits for them, and re-layouts: 2.3 us -> 0.39 us
where the time goes in v3:
time: 79.2 us; the launch traced here: 79 us
  starting transfers between devices  30.7 us (39%)
  blocking collectives  24.3 us (31%)
  waiting for transfers between devices  10.5 us (13%)
  Pallas kernels  8.64 us (11%)
  local copies, waits for them, and re-layouts  4.77 us (6%)
    all_to_all x1, blocking collectives, on_device(): parts = lax.all_to_all(cut, tp, 0, 0, tiled=True)  24.3 us
    ppermute x13, starting transfers between devices, turned(): lax.ppermute(block, axis, [(i, (i + distance) % count) for i in range(cou...  23.5 us
    ppermute x13, waiting for transfers between devices, turned(): lax.ppermute(block, axis, [(i, (i + distance) % count) for i in range(cou...  10.5 us
    pallas_call x4, Pallas kernels, call(): pl.pallas_call(kernel, out_shape=out_shape, in_specs=specs, out_specs=jax...  8.42 us
    all_to_all x1, starting transfers between devices, on_device(): slices = lax.all_to_all(slices, 'z', 0, 0, tiled=True)  7.28 us
    transpose x1, local copies, waits for them, and re-layouts, on_device(): jnp.transpose(weight_two, (1, 2, 0, 3, 4)).reshape(9, 3 * channels, width)  3.61 us
  transfers between devices with their start and end apart: 14, of which 5 were waited for; matrix products, arithmetic and copies ran while one was open for 5% of the time, Pallas kernels for 0%

profile of v3, /device:TPU:1, one launch (start us, length us, event | category | flops | bytes accessed | tf_op | source)
XLA Modules:
  0.0 79.0 jit_solution(8645874415909226859)
XLA Ops:
  0.0 2.1 %shard_map.46 = (bf16[16,2048]{1,0:T(8,128)(2,1)S(1)}, bf16[16,2048]{1,0:T(8,128)(2,1)S(1)}, bf16[4,432,128]{2,1,0:T(8,128)(2,1)}) custom-call(bf16[30,16,64]{2,1,0:T(8,128)(2,1)} %bitcast.19, bf16[432,512]{1,0:T(8,128)(2,1)} %bitcast.18), custom_call_target="tpu_custom_call" | custom-call | tf_op jit(solution)/shard_map/pallas_call | solution.py:23
  2.1 2.2 %collective-permute-start.1 = (bf16[16,2048]{1,0:T(8,128)(2,1)S(1)}, bf16[16,2048]{1,0:T(8,128)(2,1)S(1)}, u32[]{:S(2)}, u32[]{:S(2)}) collective-permute-start(bf16[16,2048]{1,0:T(8,128)(2,1)S(1)} %get-tuple-element.13), channel_id=1, source_target_pairs={{0,64},{32,96},{64,128},{96,160},{128,192},{160,224},{192,0},{224,... | collective-permute-start | bytes 196616 | tf_op jit(solution)/shard_map/ppermute | solution.py:224
  4.3 1.6 %collective-permute-start = (bf16[16,2048]{1,0:T(8,128)(2,1)S(1)}, bf16[16,2048]{1,0:T(8,128)(2,1)S(1)}, u32[]{:S(2)}, u32[]{:S(2)}) collective-permute-start(bf16[16,2048]{1,0:T(8,128)(2,1)S(1)} %get-tuple-element.13), channel_id=1, source_target_pairs={{0,32},{32,64},{64,96},{96,128},{128,160},{160,192},{192,224},{224... | collective-permute-start | bytes 196616 | tf_op jit(solution)/shard_map/ppermute | solution.py:224
  5.9 7.3 %all-to-all-start = ((bf16[4,432,128]{2,1,0:T(8,128)(2,1)}), bf16[4,432,128]{2,1,0:T(8,128)(2,1)S(1)}, u32[]{:S(2)}, u32[]{:S(2)}) async-start(bf16[4,432,128]{2,1,0:T(8,128)(2,1)} %get-tuple-element.12), calls=%async_computation | async-start | bytes 884736 | tf_op jit(solution)/shard_map/all_to_all | solution.py:251
  13.3 2.6 %collective-permute-start.7 = (bf16[48,2048]{1,0:T(8,128)(2,1)S(1)}, bf16[48,2048]{1,0:T(8,128)(2,1)S(1)}, u32[]{:S(2)}, u32[]{:S(2)}) collective-permute-start(bf16[48,2048]{1,0:T(8,128)(2,1)S(1)} %constant_dynamic-update-slice_fusion.refs_0_), channel_id=1, source_target_pairs={{0,6},{2,0},{4,2},{6,4},{1,7},{3,1},{5,3},{7,5},{8,14},{10,8},{12,... | collective-permute-start | bytes 589832 | tf_op jit(solution)/shard_map/ppermute | solution.py:224
  17.0 2.4 %collective-permute-start.2 = (bf16[48,2048]{1,0:T(8,128)(2,1)S(1)}, bf16[48,2048]{1,0:T(8,128)(2,1)S(1)}, u32[]{:S(2)}, u32[]{:S(2)}) collective-permute-start(bf16[48,2048]{1,0:T(8,128)(2,1)S(1)} %constant_dynamic-update-slice_fusion.refs_0_), channel_id=1, source_target_pairs={{0,1},{1,0},{2,3},{3,2},{4,5},{5,4},{6,7},{7,6},{8,9},{9,8},{10,11... | collective-permute-start | bytes 589832 | tf_op jit(solution)/shard_map/ppermute | solution.py:224
  19.3 1.1 %collective-permute-done.7.refs_6_ = bf16[48,2048]{1,0:T(8,128)(2,1)S(1)} collective-permute-done((bf16[48,2048]{1,0:T(8,128)(2,1)S(1)}, bf16[48,2048]{1,0:T(8,128)(2,1)S(1)}, u32[]{:S(2)}, u32[]{:S(2)}) %collective-permute-start.7) | collective-permute-done | bytes 196640 | tf_op jit(solution)/shard_map/ppermute | solution.py:224
  20.4 4.8 %collective-permute-start.8 = (bf16[48,2048]{1,0:T(8,128)(2,1)S(1)}, bf16[48,2048]{1,0:T(8,128)(2,1)S(1)}, u32[]{:S(2)}, u32[]{:S(2)}) collective-permute-start(bf16[48,2048]{1,0:T(8,128)(2,1)S(1)} %collective-permute-done.7.refs_6_), channel_id=1, source_target_pairs={{0,1},{1,0},{2,3},{3,2},{4,5},{5,4},{6,7},{7,6},{8,9},{9,8},{10,11... | collective-permute-start | bytes 589832 | tf_op jit(solution)/shard_map/ppermute | solution.py:224
  25.2 1.6 %collective-permute-start.6 = (bf16[48,2048]{1,0:T(8,128)(2,1)S(1)}, bf16[48,2048]{1,0:T(8,128)(2,1)S(1)}, u32[]{:S(2)}, u32[]{:S(2)}) collective-permute-start(bf16[48,2048]{1,0:T(8,128)(2,1)S(1)} %collective-permute-done.5.refs_4_), channel_id=1, source_target_pairs={{0,1},{1,0},{2,3},{3,2},{4,5},{5,4},{6,7},{7,6},{8,9},{9,8},{10,11... | collective-permute-start | bytes 589832 | tf_op jit(solution)/shard_map/ppermute | solution.py:224
  26.8 1.1 %collective-permute-done.3.refs_2_ = bf16[48,2048]{1,0:T(8,128)(2,1)S(1)} collective-permute-done((bf16[48,2048]{1,0:T(8,128)(2,1)S(1)}, bf16[48,2048]{1,0:T(8,128)(2,1)S(1)}, u32[]{:S(2)}, u32[]{:S(2)}) %collective-permute-start.3) | collective-permute-done | bytes 196640 | tf_op jit(solution)/shard_map/ppermute | solution.py:224
  28.0 0.9 %collective-permute-start.4 = (bf16[48,2048]{1,0:T(8,128)(2,1)S(1)}, bf16[48,2048]{1,0:T(8,128)(2,1)S(1)}, u32[]{:S(2)}, u32[]{:S(2)}) collective-permute-start(bf16[48,2048]{1,0:T(8,128)(2,1)S(1)} %collective-permute-done.3.refs_2_), channel_id=1, source_target_pairs={{0,1},{1,0},{2,3},{3,2},{4,5},{5,4},{6,7},{7,6},{8,9},{9,8},{10,11... | collective-permute-start | bytes 589832 | tf_op jit(solution)/shard_map/ppermute | solution.py:224
  29.0 1.0 %collective-permute-done.4.refs_3_ = bf16[48,2048]{1,0:T(8,128)(2,1)S(1)} collective-permute-done((bf16[48,2048]{1,0:T(8,128)(2,1)S(1)}, bf16[48,2048]{1,0:T(8,128)(2,1)S(1)}, u32[]{:S(2)}, u32[]{:S(2)}) %collective-permute-start.4) | collective-permute-done | bytes 196640 | tf_op jit(solution)/shard_map/ppermute | solution.py:224
  30.0 2.6 %shard_map.47 = bf16[32,64,128]{2,1,0:T(8,128)(2,1)S(1)} custom-call(s32[6]{0:T(128)S(1)} %stack.23.at_ref, bf16[16,2048]{1,0:T(8,128)(2,1)S(1)} %get-tuple-element.11.field_ref, bf16[4,432,128]{2,1,0:T(8,128)(2,1)S(1)} %all-to-all-done.slices_ref, bf16[48,2048]{1,0:T(8,128)(2,1)S(1)} %constant_dynamic-update-slice_fusion.refs_0_, ...), custom_call_target="tpu_custom_call" | custom-call | tf_op jit(solution)/shard_map/pallas_call | solution.py:23
  32.6 24.3 %all_to_all.10.parts_ref = bf16[32,64,128]{2,1,0:T(8,128)(2,1)S(1)} all-to-all(bf16[32,64,128]{2,1,0:T(8,128)(2,1)S(1)} %shard_map.47), channel_id=1, replica_groups=mesh['tm'=8,'z'=4,'x'=4,'c'=2] {'z','x','c'}, dimensions={0} | all-to-all | bytes 1048576 | tf_op jit(solution)/shard_map/all_to_all | solution.py:267
  57.1 1.5 %collective-permute-start.10 = (bf16[128,512]{1,0:T(8,128)(2,1)S(1)}, bf16[128,512]{1,0:T(8,128)(2,1)S(1)}, u32[]{:S(2)}, u32[]{:S(2)}) collective-permute-start(bf16[128,512]{1,0:T(8,128)(2,1)S(1)} %shard_map.48.a0_ref), channel_id=1, source_target_pairs={{0,64},{32,96},{64,128},{96,160},{128,192},{160,224},{192,0},{224,... | collective-permute-start | bytes 393224 | tf_op jit(solution)/shard_map/ppermute | solution.py:224
  58.6 2.5 %collective-permute-start.9 = (bf16[128,512]{1,0:T(8,128)(2,1)S(1)}, bf16[128,512]{1,0:T(8,128)(2,1)S(1)}, u32[]{:S(2)}, u32[]{:S(2)}) collective-permute-start(bf16[128,512]{1,0:T(8,128)(2,1)S(1)} %shard_map.48.a0_ref), channel_id=1, source_target_pairs={{0,32},{32,64},{64,96},{96,128},{128,160},{160,192},{192,224},{224... | collective-permute-start | bytes 393224 | tf_op jit(solution)/shard_map/ppermute | solution.py:224
  61.0 3.6 %copy.5 = bf16[3,3,3,512,256]{4,3,2,1,0:T(8,128)(2,1)S(1)} copy(bf16[3,3,3,512,256]{4,3,1,0,2:T(8,128)(2,1)} %bitcast.17) | data formatting | bytes 14155776 | tf_op jit(solution)/shard_map/transpose | solution.py:275
  65.0 3.0 %shard_map.49 = (bf16[256,256]{1,0:T(8,128)(2,1)S(1)}, bf16[256,256]{1,0:T(8,128)(2,1)S(1)}, f32[256,256]{1,0:T(8,128)S(1)}) custom-call(s32[6]{0:T(128)S(1)} %stack.23.at_ref, bf16[128,512]{1,0:T(8,128)(2,1)S(1)} %shard_map.48.a0_ref, bf16[128,512]{1,0:T(8,128)(2,1)S(1)} %collective-permute-done.9.a1_ref, ...), custom_call_target="tpu_custom_call" | custom-call | tf_op jit(solution)/shard_map/pallas_call | solution.py:23
  68.1 1.4 %collective-permute-start.11 = (bf16[256,256]{1,0:T(8,128)(2,1)S(1)}, bf16[256,256]{1,0:T(8,128)(2,1)S(1)}, u32[]{:S(2)}, u32[]{:S(2)}) collective-permute-start(bf16[256,256]{1,0:T(8,128)(2,1)S(1)} %get-tuple-element.15), channel_id=1, source_target_pairs={{0,32},{32,64},{64,96},{96,128},{128,160},{160,192},{192,224},{224... | collective-permute-start | bytes 393224 | tf_op jit(solution)/shard_map/ppermute | solution.py:224
  69.5 0.9 %collective-permute-start.12 = (bf16[256,256]{1,0:T(8,128)(2,1)S(1)}, bf16[256,256]{1,0:T(8,128)(2,1)S(1)}, u32[]{:S(2)}, u32[]{:S(2)}) collective-permute-start(bf16[256,256]{1,0:T(8,128)(2,1)S(1)} %get-tuple-element.16), channel_id=1, source_target_pairs={{0,64},{32,96},{64,128},{96,160},{128,192},{160,224},{192,0},{224,... | collective-permute-start | bytes 393224 | tf_op jit(solution)/shard_map/ppermute | solution.py:224
  70.4 3.8 %collective-permute-done.11.first_ref = bf16[256,256]{1,0:T(8,128)(2,1)S(1)} collective-permute-done((bf16[256,256]{1,0:T(8,128)(2,1)S(1)}, bf16[256,256]{1,0:T(8,128)(2,1)S(1)}, u32[]{:S(2)}, u32[]{:S(2)}) %collective-permute-start.11) | collective-permute-done | bytes 131104 | tf_op jit(solution)/shard_map/ppermute | solution.py:224
  74.2 3.5 %collective-permute-done.12.second_ref = bf16[256,256]{1,0:T(8,128)(2,1)S(1)} collective-permute-done((bf16[256,256]{1,0:T(8,128)(2,1)S(1)}, bf16[256,256]{1,0:T(8,128)(2,1)S(1)}, u32[]{:S(2)}, u32[]{:S(2)}) %collective-permute-start.12) | collective-permute-done | bytes 131104 | tf_op jit(solution)/shard_map/ppermute | solution.py:224
  77.7 0.7 shard_map.50
  78.3 0.7 reshape.11
  (18 shorter events, 1.8 us)
Async XLA Ops:
  2.1 11.2 %collective-permute-start.1 = (bf16[16,2048]{1,0:T(8,128)(2,1)S(1)}, bf16[16,2048]{1,0:T(8,128)(2,1)S(1)}, u32[]{:S(2)}, u32[]{:S(2)}) collective-permute-start(bf16[16,2048]{1,0:T(8,128)(2,1)S(1)} %get-tuple-element.13), channel_id=1, source_target_pairs={{0,64},{32,96},{64,128},{96,160},{128,192},{160,224},{192,0},{224,... | collective-permute-start | bytes 196616 | tf_op jit(solution)/shard_map/ppermute | solution.py:224
  4.3 8.9 %collective-permute-start = (bf16[16,2048]{1,0:T(8,128)(2,1)S(1)}, bf16[16,2048]{1,0:T(8,128)(2,1)S(1)}, u32[]{:S(2)}, u32[]{:S(2)}) collective-permute-start(bf16[16,2048]{1,0:T(8,128)(2,1)S(1)} %get-tuple-element.13), channel_id=1, source_target_pairs={{0,32},{32,64},{64,96},{96,128},{128,160},{160,192},{192,224},{224... | collective-permute-start | bytes 196616 | tf_op jit(solution)/shard_map/ppermute | solution.py:224
  5.9 24.0 %all-to-all-start = ((bf16[4,432,128]{2,1,0:T(8,128)(2,1)}), bf16[4,432,128]{2,1,0:T(8,128)(2,1)S(1)}, u32[]{:S(2)}, u32[]{:S(2)}) async-start(bf16[4,432,128]{2,1,0:T(8,128)(2,1)} %get-tuple-element.12), calls=%async_computation | async-start | bytes 884736 | tf_op jit(solution)/shard_map/all_to_all | solution.py:251
  13.3 7.1 %collective-permute-start.7 = (bf16[48,2048]{1,0:T(8,128)(2,1)S(1)}, bf16[48,2048]{1,0:T(8,128)(2,1)S(1)}, u32[]{:S(2)}, u32[]{:S(2)}) collective-permute-start(bf16[48,2048]{1,0:T(8,128)(2,1)S(1)} %constant_dynamic-update-slice_fusion.refs_0_), channel_id=1, source_target_pairs={{0,6},{2,0},{4,2},{6,4},{1,7},{3,1},{5,3},{7,5},{8,14},{10,8},{12,... | collective-permute-start | bytes 589832 | tf_op jit(solution)/shard_map/ppermute | solution.py:224
  15.8 9.4 %collective-permute-start.5 = (bf16[48,2048]{1,0:T(8,128)(2,1)S(1)}, bf16[48,2048]{1,0:T(8,128)(2,1)S(1)}, u32[]{:S(2)}, u32[]{:S(2)}) collective-permute-start(bf16[48,2048]{1,0:T(8,128)(2,1)S(1)} %constant_dynamic-update-slice_fusion.refs_0_), channel_id=1, source_target_pairs={{0,4},{2,6},{4,0},{6,2},{1,5},{3,7},{5,1},{7,3},{8,12},{10,14},{12... | collective-permute-start | bytes 589832 | tf_op jit(solution)/shard_map/ppermute | solution.py:224
  16.4 11.6 %collective-permute-start.3 = (bf16[48,2048]{1,0:T(8,128)(2,1)S(1)}, bf16[48,2048]{1,0:T(8,128)(2,1)S(1)}, u32[]{:S(2)}, u32[]{:S(2)}) collective-permute-start(bf16[48,2048]{1,0:T(8,128)(2,1)S(1)} %constant_dynamic-update-slice_fusion.refs_0_), channel_id=1, source_target_pairs={{0,2},{2,4},{4,6},{6,0},{1,3},{3,5},{5,7},{7,1},{8,10},{10,12},{12... | collective-permute-start | bytes 589832 | tf_op jit(solution)/shard_map/ppermute | solution.py:224
  17.0 12.0 %collective-permute-start.2 = (bf16[48,2048]{1,0:T(8,128)(2,1)S(1)}, bf16[48,2048]{1,0:T(8,128)(2,1)S(1)}, u32[]{:S(2)}, u32[]{:S(2)}) collective-permute-start(bf16[48,2048]{1,0:T(8,128)(2,1)S(1)} %constant_dynamic-update-slice_fusion.refs_0_), channel_id=1, source_target_pairs={{0,1},{1,0},{2,3},{3,2},{4,5},{5,4},{6,7},{7,6},{8,9},{9,8},{10,11... | collective-permute-start | bytes 589832 | tf_op jit(solution)/shard_map/ppermute | solution.py:224
  20.4 8.5 %collective-permute-start.8 = (bf16[48,2048]{1,0:T(8,128)(2,1)S(1)}, bf16[48,2048]{1,0:T(8,128)(2,1)S(1)}, u32[]{:S(2)}, u32[]{:S(2)}) collective-permute-start(bf16[48,2048]{1,0:T(8,128)(2,1)S(1)} %collective-permute-done.7.refs_6_), channel_id=1, source_target_pairs={{0,1},{1,0},{2,3},{3,2},{4,5},{5,4},{6,7},{7,6},{8,9},{9,8},{10,11... | collective-permute-start | bytes 589832 | tf_op jit(solution)/shard_map/ppermute | solution.py:224
  25.2 3.8 %collective-permute-start.6 = (bf16[48,2048]{1,0:T(8,128)(2,1)S(1)}, bf16[48,2048]{1,0:T(8,128)(2,1)S(1)}, u32[]{:S(2)}, u32[]{:S(2)}) collective-permute-start(bf16[48,2048]{1,0:T(8,128)(2,1)S(1)} %collective-permute-done.5.refs_4_), channel_id=1, source_target_pairs={{0,1},{1,0},{2,3},{3,2},{4,5},{5,4},{6,7},{7,6},{8,9},{9,8},{10,11... | collective-permute-start | bytes 589832 | tf_op jit(solution)/shard_map/ppermute | solution.py:224
  28.0 2.0 %collective-permute-start.4 = (bf16[48,2048]{1,0:T(8,128)(2,1)S(1)}, bf16[48,2048]{1,0:T(8,128)(2,1)S(1)}, u32[]{:S(2)}, u32[]{:S(2)}) collective-permute-start(bf16[48,2048]{1,0:T(8,128)(2,1)S(1)} %collective-permute-done.3.refs_2_), channel_id=1, source_target_pairs={{0,1},{1,0},{2,3},{3,2},{4,5},{5,4},{6,7},{7,6},{8,9},{9,8},{10,11... | collective-permute-start | bytes 589832 | tf_op jit(solution)/shard_map/ppermute | solution.py:224
  57.1 7.6 %collective-permute-start.10 = (bf16[128,512]{1,0:T(8,128)(2,1)S(1)}, bf16[128,512]{1,0:T(8,128)(2,1)S(1)}, u32[]{:S(2)}, u32[]{:S(2)}) collective-permute-start(bf16[128,512]{1,0:T(8,128)(2,1)S(1)} %shard_map.48.a0_ref), channel_id=1, source_target_pairs={{0,64},{32,96},{64,128},{96,160},{128,192},{160,224},{192,0},{224,... | collective-permute-start | bytes 393224 | tf_op jit(solution)/shard_map/ppermute | solution.py:224
  58.6 6.1 %collective-permute-start.9 = (bf16[128,512]{1,0:T(8,128)(2,1)S(1)}, bf16[128,512]{1,0:T(8,128)(2,1)S(1)}, u32[]{:S(2)}, u32[]{:S(2)}) collective-permute-start(bf16[128,512]{1,0:T(8,128)(2,1)S(1)} %shard_map.48.a0_ref), channel_id=1, source_target_pairs={{0,32},{32,64},{64,96},{96,128},{128,160},{160,192},{192,224},{224... | collective-permute-start | bytes 393224 | tf_op jit(solution)/shard_map/ppermute | solution.py:224
  61.0 4.0 %copy-start = (bf16[3,3,3,256,256]{4,3,2,1,0:T(8,128)(2,1)S(1)}, bf16[3,3,3,256,256]{4,3,2,1,0:T(8,128)(2,1)}, u32[]{:S(2)}) copy-start(bf16[3,3,3,256,256]{4,3,2,1,0:T(8,128)(2,1)} %last_ref.1) | copy-start | bytes 10616836
  68.1 6.1 %collective-permute-start.11 = (bf16[256,256]{1,0:T(8,128)(2,1)S(1)}, bf16[256,256]{1,0:T(8,128)(2,1)S(1)}, u32[]{:S(2)}, u32[]{:S(2)}) collective-permute-start(bf16[256,256]{1,0:T(8,128)(2,1)S(1)} %get-tuple-element.15), channel_id=1, source_target_pairs={{0,32},{32,64},{64,96},{96,128},{128,160},{160,192},{192,224},{224... | collective-permute-start | bytes 393224 | tf_op jit(solution)/shard_map/ppermute | solution.py:224
  69.5 8.2 %collective-permute-start.12 = (bf16[256,256]{1,0:T(8,128)(2,1)S(1)}, bf16[256,256]{1,0:T(8,128)(2,1)S(1)}, u32[]{:S(2)}, u32[]{:S(2)}) collective-permute-start(bf16[256,256]{1,0:T(8,128)(2,1)S(1)} %get-tuple-element.16), channel_id=1, source_target_pairs={{0,64},{32,96},{64,128},{96,160},{128,192},{160,224},{192,0},{224,... | collective-permute-start | bytes 393224 | tf_op jit(solution)/shard_map/ppermute | solution.py:224

commit v4 on v3

--- a/solution.py
+++ b/solution.py
@@ -118,26 +118,49 @@
     sum_ref[:, :LANES] = before(sum_ref[:, cells : cells + LANES])
     sum_ref[:, LANES + cells :] = after(sum_ref[:, LANES : 2 * LANES])
     at = lax.broadcasted_iota(jnp.int32, (wide, LANES), 1) // PITCH
-    for m in range(deep // 2):
-        rows = [sum_ref[:, (2 * m + r) * LANES : (2 * m + r + 1) * LANES] for r in range(4)]
+    half = wide // 2
+
+    def placed(pieces, q):
+        moved = [pltpu.roll(p, (r - q) % 4 * PITCH, 1) if r != q else p for r, p in enumerate(pieces)]
+        to = at[: pieces[0].shape[0]]
+        return jnp.where(to < 2, jnp.where(to < 1, moved[0], moved[1]), jnp.where(to < 3, moved[2], moved[3]))
+
+    for m in range(deep // 4):
+        rows = [sum_ref[:, (4 * m + r) * LANES : (4 * m + r + 1) * LANES] for r in range(6)]
+        rest = [rows[4][:half], rows[5][:half], rows[4][half:], rows[5][half:]]
         for q in range(QUARTERS):
-            moved = [pltpu.roll(rows[r], (r - q) % 4 * PITCH, 1) if r != q else rows[r] for r in range(4)]
-            strip = jnp.where(at < 2, jnp.where(at < 1, moved[0], moved[1]), jnp.where(at < 3, moved[2], moved[3]))
-            out_ref[q * (deep // 2) + m] = strip.astype(BF16)
+            out_ref[q * (deep // 4) + m, :wide] = placed(rows[:4], q).astype(BF16)
+            out_ref[q * (deep // 4) + m, wide:] = placed(rest, q).astype(BF16)
 
 
 def strip_kernel(across, parts_ref, out_ref, order_ref):
-    shard = parts_ref.shape[1] // 4
-    for n in range(8):
+    wide = parts_ref.shape[1] * 2 // 3
+    shard = wide // 4
+    order_ref[:, LANES:] = jnp.zeros((order_ref.shape[0], LANES), F32)
+    for n in range(4):
         total = None
         for z in range(4):
-            part = parts_ref[z * 8 + n].astype(F32)
+            part = parts_ref[z * 4 + n].astype(F32)
             total = part if total is None else total + part
         act = silu(total.astype(BF16).astype(F32))
         act = jnp.where(column_mask(act.shape, 1, across), act, 0.0)
+        rest = [act[wide:], pltpu.roll(act[wide:], LANES // 2, 1)]
         for z in range(4):
-            order_ref[(z * 8 + n) * shard : (z * 8 + n + 1) * shard, :] = act[z * shard : (z + 1) * shard]
-    out_ref[...] = order_ref[...].T.astype(BF16)
+            to = slice((z * 4 + n) * shard, (z * 4 + n + 1) * shard)
+            order_ref[to, :LANES] = act[z * shard : (z + 1) * shard]
+            order_ref[to, LANES : LANES + LANES // 2] = rest[z // 2][z % 2 * shard : (z % 2 + 1) * shard, : LANES // 2]
+    out_ref[...] = order_ref[...].T[: out_ref.shape[0]].astype(BF16)
+
+
+def stage_kernel(weight_ref, tie_ref, out_ref, sems):
+    copies = []
+    for n in range(18):
+        i, j, c = n // 6, n // 2 % 3, n % 2
+        copies.append(pltpu.make_async_copy(weight_ref.at[:, i, j, :, c], out_ref.at[n // 2, :, c], sems.at[n]))
+    for copy in copies:
+        copy.start()
+    for copy in copies:
+        copy.wait()
 
 
 def down(v):
@@ -148,12 +171,22 @@
     return pltpu.roll(v, v.shape[0] - 1, 0)
 
 
-def fine_kernel(across, at_ref, a0_ref, a1_ref, a2_ref, wide_ref, last_ref, first_ref, second_ref, own_ref):
-    t, strip, strips = at_ref[3], at_ref[4], at_ref[5]
-    a0 = a0_ref[...].astype(F32)
-    a1 = jnp.where(t >= 1, a1_ref[...].astype(F32), a0)
-    a2 = jnp.where(t >= 2, a2_ref[...].astype(F32), a1)
-    frames = jnp.concatenate([a2, a1, a0], 1).astype(BF16)
+def fine_kernel(across, at_ref, *refs):
+    halves, (wide_ref, last_ref, first_ref, second_ref, own_ref, frames_ref) = refs[:6], refs[6:]
+    c, t, strip, strips = at_ref[2], at_ref[3], at_ref[4], at_ref[5]
+    cells, channels, width = 4 * PITCH, halves[0].shape[1] * 2, own_ref.shape[1]
+    rows = pl.ds(pl.multiple_of(c * 2 * PITCH, 2 * PITCH), cells)
+
+    def put(k, part):
+        for n, side in enumerate((c, 1 - c)):
+            to = pl.multiple_of(k * channels + side * (channels // 2), channels // 2)
+            frames_ref[:, pl.ds(to, channels // 2)] = halves[2 * part + n][rows, :]
+
+    put(2, 0)
+    for k in range(2):
+        for part in range(3 - k):
+            pl.when(jnp.minimum(t, 2 - k) == part)(functools.partial(put, k, part))
+    frames = frames_ref[...]
     spans = ((0, 3), (0, 4), (1, 4))
     maps = ((0, 0, 1, 1, 2, 2), (0, 1, 1, 2, 2, 3), (0, 0, 1, 1, 2, 2))
     even, odd = [None] * 6, [None] * 6
@@ -162,7 +195,7 @@
         sums = []
         for j in range(3):
             sums.append(
-                jnp.dot(frames[lo * PITCH : hi * PITCH], wide_ref[i * 3 + j], preferred_element_type=F32)
+                jnp.dot(frames[lo * PITCH : hi * PITCH], wide_ref[i * 3 + j].reshape(3 * channels, width), preferred_element_type=F32)
             )
         at_even = down(sums[0]) + sums[1] + sums[2]
         at_odd = sums[0] + sums[1] + up(sums[2])
@@ -253,10 +286,9 @@
     for d in range(4):
         block = turned(frames, "x", d) if d else frames
         blocks += [block, turned(block, "c", 1)]
-    strips = lax.axis_size(tp)
     cut = call(
         coarse_kernel,
-        jax.ShapeDtypeStruct((strips, 4 * shard, LANES), BF16),
+        jax.ShapeDtypeStruct((16, 6 * shard, LANES), BF16),
         (at, field, slices, *blocks),
         (
             pltpu.VMEM((3 * channels // 4, cells + 2 * LANES), BF16),
@@ -264,20 +296,32 @@
             pltpu.VMEM((4 * shard, cells + 2 * LANES), F32),
         ),
     )
-    parts = lax.all_to_all(cut, tp, 0, 0, tiled=True)
-    strip = pl.pallas_call(
+    parts = lax.all_to_all(cut, ("z", "x"), 0, 0, tiled=True)
+    own = pl.pallas_call(
         functools.partial(strip_kernel, across),
-        out_shape=jax.ShapeDtypeStruct((LANES, channels), BF16),
-        scratch_shapes=[pltpu.VMEM((channels, LANES), F32)],
+        out_shape=jax.ShapeDtypeStruct((6 * PITCH, channels // 2), BF16),
+        scratch_shapes=[pltpu.VMEM((channels // 2, 2 * LANES), F32)],
         compiler_params=pltpu.CompilerParams(vmem_limit_bytes=LIMIT),
     )(parts)
     width = weight_two.shape[4]
-    wide = jnp.transpose(weight_two, (1, 2, 0, 3, 4)).reshape(9, 3 * channels, width)
+    wide = call(
+        stage_kernel,
+        jax.ShapeDtypeStruct((9, 3, 2, channels // 2 // shard, shard, width), BF16),
+        (pltpu.with_memory_space_constraint(weight_two.reshape(3, 3, 3, -1, 2, shard, width), pltpu.HBM), own),
+        (pltpu.SemaphoreType.DMA((18,)),),
+        [HBM, pl.BlockSpec(memory_space=pl.ANY)],
+    )
+    moved = [turned(own, "tm", d) for d in (1, 2)]
+    wide, *moved = lax.optimization_barrier((wide, *moved))
+    halves = []
+    for half in (own, *moved):
+        halves += [half, turned(half, "c", 1)]
     small = jax.ShapeDtypeStruct((8 * PITCH, width), BF16)
     first, second, own = call(
         functools.partial(fine_kernel, across),
         (small, small, jax.ShapeDtypeStruct((8 * PITCH, width), F32)),
-        (at, strip, turned(strip, "tm", 1), turned(strip, "tm", 2), wide, weight_three),
+        (at, *halves, wide, weight_three),
+        (pltpu.VMEM((4 * PITCH, 3 * channels), BF16),),
     )
     decoded = call(
         functools.partial(last_kernel, across),

time: 79.2 us -> 78.5 us (level)
  blocking collectives: 24.3 us -> 18.5 us
  local copies, waits for them, and re-layouts: 4.77 us -> 0.79 us
  Pallas kernels: 8.64 us -> 12.1 us
  starting transfers between devices: 30.7 us -> 33.8 us
  waiting for transfers between devices: 10.5 us -> 13 us
    all_to_all x1, blocking collectives: 24.3 us -> 18.5 us  [on_device(): parts = lax.all_to_all(cut, ('z', 'x'), 0, 0, tiled=True)]
    transpose x1 -> x0, local copies, waits for them, and re-layouts: 3.61 us -> none  [on_device(): jnp.transpose(weight_two, (1, 2, 0, 3, 4)).reshape(9, 3 * channels, width)]
    pallas_call x4 -> x5, Pallas kernels: 8.42 us -> 11.9 us  [call(): pl.pallas_call(kernel, out_shape=out_shape, in_specs=specs, out_specs=jax...]
    ppermute x13 -> x16, starting transfers between devices: 23.5 us -> 26.5 us  [turned(): lax.ppermute(block, axis, [(i, (i + distance) % count) for i in range(cou...]
    ppermute x13 -> x16, waiting for transfers between devices: 10.5 us -> 13 us  [turned(): lax.ppermute(block, axis, [(i, (i + distance) % count) for i in range(cou...]
  transfers between devices with their start and end apart: 14 -> 17, of which waited for: 5 -> 7; matrix products, arithmetic and copies ran while one was open for 5% -> 0% of each run, Pallas kernels for 0% -> 4%
where the time goes in v4:
time: 78.5 us; the launch traced here: 78.3 us
  starting transfers between devices  33.8 us (43%)
  blocking collectives  18.5 us (24%)
  waiting for transfers between devices  13 us (17%)
  Pallas kernels  12.1 us (15%)
  local copies, waits for them, and re-layouts  0.79 us (1%)
    ppermute x16, starting transfers between devices, turned(): lax.ppermute(block, axis, [(i, (i + distance) % count) for i in range(cou...  26.5 us
    all_to_all x1, blocking collectives, on_device(): parts = lax.all_to_all(cut, ('z', 'x'), 0, 0, tiled=True)  18.5 us
    ppermute x16, waiting for transfers between devices, turned(): lax.ppermute(block, axis, [(i, (i + distance) % count) for i in range(cou...  13 us
    pallas_call x5, Pallas kernels, call(): pl.pallas_call(kernel, out_shape=out_shape, in_specs=specs, out_specs=jax...  11.9 us
    all_to_all x1, starting transfers between devices, on_device(): slices = lax.all_to_all(slices, 'z', 0, 0, tiled=True)  7.28 us
  transfers between devices with their start and end apart: 17, of which 7 were waited for; matrix products, arithmetic and copies ran while one was open for 0% of the time, Pallas kernels for 4%

profile of v4, /device:TPU:1, one launch (start us, length us, event | category | flops | bytes accessed | tf_op | source)
XLA Modules:
  0.0 78.3 jit_solution(12440047471218025420)
XLA Ops:
  0.0 2.1 %shard_map.46 = (bf16[16,2048]{1,0:T(8,128)(2,1)S(1)}, bf16[16,2048]{1,0:T(8,128)(2,1)S(1)}, bf16[4,432,128]{2,1,0:T(8,128)(2,1)}) custom-call(bf16[30,16,64]{2,1,0:T(8,128)(2,1)} %bitcast.17, bf16[432,512]{1,0:T(8,128)(2,1)} %bitcast.16), custom_call_target="tpu_custom_call" | custom-call | tf_op jit(solution)/shard_map/pallas_call | solution.py:23
  2.1 2.2 %collective-permute-start.1 = (bf16[16,2048]{1,0:T(8,128)(2,1)S(1)}, bf16[16,2048]{1,0:T(8,128)(2,1)S(1)}, u32[]{:S(2)}, u32[]{:S(2)}) collective-permute-start(bf16[16,2048]{1,0:T(8,128)(2,1)S(1)} %get-tuple-element.16), channel_id=1, source_target_pairs={{0,64},{32,96},{64,128},{96,160},{128,192},{160,224},{192,0},{224,... | collective-permute-start | bytes 196616 | tf_op jit(solution)/shard_map/ppermute | solution.py:257
  4.3 1.6 %collective-permute-start = (bf16[16,2048]{1,0:T(8,128)(2,1)S(1)}, bf16[16,2048]{1,0:T(8,128)(2,1)S(1)}, u32[]{:S(2)}, u32[]{:S(2)}) collective-permute-start(bf16[16,2048]{1,0:T(8,128)(2,1)S(1)} %get-tuple-element.16), channel_id=1, source_target_pairs={{0,32},{32,64},{64,96},{96,128},{128,160},{160,192},{192,224},{224... | collective-permute-start | bytes 196616 | tf_op jit(solution)/shard_map/ppermute | solution.py:257
  5.9 7.3 %all-to-all-start = ((bf16[4,432,128]{2,1,0:T(8,128)(2,1)}), bf16[4,432,128]{2,1,0:T(8,128)(2,1)S(1)}, u32[]{:S(2)}, u32[]{:S(2)}) async-start(bf16[4,432,128]{2,1,0:T(8,128)(2,1)} %get-tuple-element.15), calls=%async_computation | async-start | bytes 884736 | tf_op jit(solution)/shard_map/all_to_all | solution.py:284
  13.3 2.6 %collective-permute-start.7 = (bf16[48,2048]{1,0:T(8,128)(2,1)S(1)}, bf16[48,2048]{1,0:T(8,128)(2,1)S(1)}, u32[]{:S(2)}, u32[]{:S(2)}) collective-permute-start(bf16[48,2048]{1,0:T(8,128)(2,1)S(1)} %constant_dynamic-update-slice_fusion.refs_0_), channel_id=1, source_target_pairs={{0,6},{2,0},{4,2},{6,4},{1,7},{3,1},{5,3},{7,5},{8,14},{10,8},{12,... | collective-permute-start | bytes 589832 | tf_op jit(solution)/shard_map/ppermute | solution.py:257
  17.0 2.4 %collective-permute-start.2 = (bf16[48,2048]{1,0:T(8,128)(2,1)S(1)}, bf16[48,2048]{1,0:T(8,128)(2,1)S(1)}, u32[]{:S(2)}, u32[]{:S(2)}) collective-permute-start(bf16[48,2048]{1,0:T(8,128)(2,1)S(1)} %constant_dynamic-update-slice_fusion.refs_0_), channel_id=1, source_target_pairs={{0,1},{1,0},{2,3},{3,2},{4,5},{5,4},{6,7},{7,6},{8,9},{9,8},{10,11... | collective-permute-start | bytes 589832 | tf_op jit(solution)/shard_map/ppermute | solution.py:257
  19.3 1.1 %collective-permute-done.7.refs_6_ = bf16[48,2048]{1,0:T(8,128)(2,1)S(1)} collective-permute-done((bf16[48,2048]{1,0:T(8,128)(2,1)S(1)}, bf16[48,2048]{1,0:T(8,128)(2,1)S(1)}, u32[]{:S(2)}, u32[]{:S(2)}) %collective-permute-start.7) | collective-permute-done | bytes 196640 | tf_op jit(solution)/shard_map/ppermute | solution.py:257
  20.4 4.8 %collective-permute-start.8 = (bf16[48,2048]{1,0:T(8,128)(2,1)S(1)}, bf16[48,2048]{1,0:T(8,128)(2,1)S(1)}, u32[]{:S(2)}, u32[]{:S(2)}) collective-permute-start(bf16[48,2048]{1,0:T(8,128)(2,1)S(1)} %collective-permute-done.7.refs_6_), channel_id=1, source_target_pairs={{0,1},{1,0},{2,3},{3,2},{4,5},{5,4},{6,7},{7,6},{8,9},{9,8},{10,11... | collective-permute-start | bytes 589832 | tf_op jit(solution)/shard_map/ppermute | solution.py:257
  25.2 1.6 %collective-permute-start.6 = (bf16[48,2048]{1,0:T(8,128)(2,1)S(1)}, bf16[48,2048]{1,0:T(8,128)(2,1)S(1)}, u32[]{:S(2)}, u32[]{:S(2)}) collective-permute-start(bf16[48,2048]{1,0:T(8,128)(2,1)S(1)} %collective-permute-done.5.refs_4_), channel_id=1, source_target_pairs={{0,1},{1,0},{2,3},{3,2},{4,5},{5,4},{6,7},{7,6},{8,9},{9,8},{10,11... | collective-permute-start | bytes 589832 | tf_op jit(solution)/shard_map/ppermute | solution.py:257
  26.8 1.1 %collective-permute-done.3.refs_2_ = bf16[48,2048]{1,0:T(8,128)(2,1)S(1)} collective-permute-done((bf16[48,2048]{1,0:T(8,128)(2,1)S(1)}, bf16[48,2048]{1,0:T(8,128)(2,1)S(1)}, u32[]{:S(2)}, u32[]{:S(2)}) %collective-permute-start.3) | collective-permute-done | bytes 196640 | tf_op jit(solution)/shard_map/ppermute | solution.py:257
  28.0 0.9 %collective-permute-start.4 = (bf16[48,2048]{1,0:T(8,128)(2,1)S(1)}, bf16[48,2048]{1,0:T(8,128)(2,1)S(1)}, u32[]{:S(2)}, u32[]{:S(2)}) collective-permute-start(bf16[48,2048]{1,0:T(8,128)(2,1)S(1)} %collective-permute-done.3.refs_2_), channel_id=1, source_target_pairs={{0,1},{1,0},{2,3},{3,2},{4,5},{5,4},{6,7},{7,6},{8,9},{9,8},{10,11... | collective-permute-start | bytes 589832 | tf_op jit(solution)/shard_map/ppermute | solution.py:257
  29.0 1.0 %collective-permute-done.4.refs_3_ = bf16[48,2048]{1,0:T(8,128)(2,1)S(1)} collective-permute-done((bf16[48,2048]{1,0:T(8,128)(2,1)S(1)}, bf16[48,2048]{1,0:T(8,128)(2,1)S(1)}, u32[]{:S(2)}, u32[]{:S(2)}) %collective-permute-start.4) | collective-permute-done | bytes 196640 | tf_op jit(solution)/shard_map/ppermute | solution.py:257
  29.9 2.5 %shard_map.47 = bf16[16,96,128]{2,1,0:T(8,128)(2,1)S(1)} custom-call(s32[6]{0:T(128)S(1)} %stack.23.at_ref, bf16[16,2048]{1,0:T(8,128)(2,1)S(1)} %get-tuple-element.14.field_ref, bf16[4,432,128]{2,1,0:T(8,128)(2,1)S(1)} %all-to-all-done.slices_ref, bf16[48,2048]{1,0:T(8,128)(2,1)S(1)} %constant_dynamic-update-slice_fusion.refs_0_, ...), custom_call_target="tpu_custom_call" | custom-call | tf_op jit(solution)/shard_map/pallas_call | solution.py:23
  32.5 18.5 %all_to_all.10.parts_ref = bf16[16,96,128]{2,1,0:T(8,128)(2,1)S(1)} all-to-all(bf16[16,96,128]{2,1,0:T(8,128)(2,1)S(1)} %shard_map.47), channel_id=1, replica_groups=mesh['tm'=8,'z'=4,'x'=4,'c'=2] {'z','x'}, dimensions={0} | all-to-all | bytes 786432 | tf_op jit(solution)/shard_map/all_to_all | solution.py:299
  51.2 1.4 %collective-permute-start.11 = (bf16[192,256]{1,0:T(8,128)(2,1)S(1)}, bf16[192,256]{1,0:T(8,128)(2,1)S(1)}, u32[]{:S(2)}, u32[]{:S(2)}) collective-permute-start(bf16[192,256]{1,0:T(8,128)(2,1)S(1)} %shard_map.48.tie_ref.refs_0_), channel_id=1, source_target_pairs={{0,64},{32,96},{64,128},{96,160},{128,192},{160,224},{192,0},{224,... | collective-permute-start | bytes 294920 | tf_op jit(solution)/shard_map/ppermute | solution.py:257
  52.6 5.0 %collective-permute-start.10 = (bf16[192,256]{1,0:T(8,128)(2,1)S(1)}, bf16[192,256]{1,0:T(8,128)(2,1)S(1)}, u32[]{:S(2)}, u32[]{:S(2)}) collective-permute-start(bf16[192,256]{1,0:T(8,128)(2,1)S(1)} %shard_map.48.tie_ref.refs_0_), channel_id=1, source_target_pairs={{0,32},{32,64},{64,96},{96,128},{128,160},{160,192},{192,224},{224... | collective-permute-start | bytes 294920 | tf_op jit(solution)/shard_map/ppermute | solution.py:257
  57.7 1.1 %collective-permute-start.9 = (bf16[192,256]{1,0:T(8,128)(2,1)S(1)}, bf16[192,256]{1,0:T(8,128)(2,1)S(1)}, u32[]{:S(2)}, u32[]{:S(2)}) collective-permute-start(bf16[192,256]{1,0:T(8,128)(2,1)S(1)} %shard_map.48.tie_ref.refs_0_), channel_id=1, source_target_pairs={{0,1},{1,0},{2,3},{3,2},{4,5},{5,4},{6,7},{7,6},{8,9},{9,8},{10,11... | collective-permute-start | bytes 294920 | tf_op jit(solution)/shard_map/ppermute | solution.py:257
  58.8 3.4 %shard_map.49.refs_6_ = bf16[9,3,2,16,16,256]{5,4,3,2,1,0:T(8,128)(2,1)S(1)} custom-call(bf16[3,3,3,16,2,16,256]{6,5,4,3,2,1,0:T(8,128)(2,1)} %bitcast.15, bf16[192,256]{1,0:T(8,128)(2,1)S(1)} %shard_map.48.tie_ref.refs_0_), custom_call_target="tpu_custom_call" | custom-call | tf_op jit(solution)/shard_map/pallas_call | solution.py:23
  62.8 0.8 %collective-permute-done.12.refs_3_ = bf16[192,256]{1,0:T(8,128)(2,1)S(1)} collective-permute-done((bf16[192,256]{1,0:T(8,128)(2,1)S(1)}, bf16[192,256]{1,0:T(8,128)(2,1)S(1)}, u32[]{:S(2)}, u32[]{:S(2)}) %collective-permute-start.12) | collective-permute-done | bytes 98336 | tf_op jit(solution)/shard_map/ppermute | solution.py:257
  63.9 3.3 %shard_map.50 = (bf16[256,256]{1,0:T(8,128)(2,1)S(1)}, bf16[256,256]{1,0:T(8,128)(2,1)S(1)}, f32[256,256]{1,0:T(8,128)S(1)}) custom-call(s32[6]{0:T(128)S(1)} %stack.23.at_ref, bf16[192,256]{1,0:T(8,128)(2,1)S(1)} %shard_map.48.tie_ref.refs_0_, bf16[192,256]{1,0:T(8,128)(2,1)S(1)} %collective-permute-done.9.refs_1_, ...), custom_call_target="tpu_custom_call" | custom-call | tf_op jit(solution)/shard_map/pallas_call | solution.py:23
  67.1 0.7 collective-permute-start.14
  68.3 5.9 %collective-permute-done.14.first_ref = bf16[256,256]{1,0:T(8,128)(2,1)S(1)} collective-permute-done((bf16[256,256]{1,0:T(8,128)(2,1)S(1)}, bf16[256,256]{1,0:T(8,128)(2,1)S(1)}, u32[]{:S(2)}, u32[]{:S(2)}) %collective-permute-start.14) | collective-permute-done | bytes 131104 | tf_op jit(solution)/shard_map/ppermute | solution.py:257
  74.3 2.7 %collective-permute-done.15.second_ref = bf16[256,256]{1,0:T(8,128)(2,1)S(1)} collective-permute-done((bf16[256,256]{1,0:T(8,128)(2,1)S(1)}, bf16[256,256]{1,0:T(8,128)(2,1)S(1)}, u32[]{:S(2)}, u32[]{:S(2)}) %collective-permute-start.15) | collective-permute-done | bytes 131104 | tf_op jit(solution)/shard_map/ppermute | solution.py:257
  77.6 0.7 reshape.11
  (24 shorter events, 3.6 us)
Async XLA Ops:
  2.1 11.2 %collective-permute-start.1 = (bf16[16,2048]{1,0:T(8,128)(2,1)S(1)}, bf16[16,2048]{1,0:T(8,128)(2,1)S(1)}, u32[]{:S(2)}, u32[]{:S(2)}) collective-permute-start(bf16[16,2048]{1,0:T(8,128)(2,1)S(1)} %get-tuple-element.16), channel_id=1, source_target_pairs={{0,64},{32,96},{64,128},{96,160},{128,192},{160,224},{192,0},{224,... | collective-permute-start | bytes 196616 | tf_op jit(solution)/shard_map/ppermute | solution.py:257
  4.3 8.9 %collective-permute-start = (bf16[16,2048]{1,0:T(8,128)(2,1)S(1)}, bf16[16,2048]{1,0:T(8,128)(2,1)S(1)}, u32[]{:S(2)}, u32[]{:S(2)}) collective-permute-start(bf16[16,2048]{1,0:T(8,128)(2,1)S(1)} %get-tuple-element.16), channel_id=1, source_target_pairs={{0,32},{32,64},{64,96},{96,128},{128,160},{160,192},{192,224},{224... | collective-permute-start | bytes 196616 | tf_op jit(solution)/shard_map/ppermute | solution.py:257
  5.9 24.0 %all-to-all-start = ((bf16[4,432,128]{2,1,0:T(8,128)(2,1)}), bf16[4,432,128]{2,1,0:T(8,128)(2,1)S(1)}, u32[]{:S(2)}, u32[]{:S(2)}) async-start(bf16[4,432,128]{2,1,0:T(8,128)(2,1)} %get-tuple-element.15), calls=%async_computation | async-start | bytes 884736 | tf_op jit(solution)/shard_map/all_to_all | solution.py:284
  13.3 7.1 %collective-permute-start.7 = (bf16[48,2048]{1,0:T(8,128)(2,1)S(1)}, bf16[48,2048]{1,0:T(8,128)(2,1)S(1)}, u32[]{:S(2)}, u32[]{:S(2)}) collective-permute-start(bf16[48,2048]{1,0:T(8,128)(2,1)S(1)} %constant_dynamic-update-slice_fusion.refs_0_), channel_id=1, source_target_pairs={{0,6},{2,0},{4,2},{6,4},{1,7},{3,1},{5,3},{7,5},{8,14},{10,8},{12,... | collective-permute-start | bytes 589832 | tf_op jit(solution)/shard_map/ppermute | solution.py:257
  15.8 9.4 %collective-permute-start.5 = (bf16[48,2048]{1,0:T(8,128)(2,1)S(1)}, bf16[48,2048]{1,0:T(8,128)(2,1)S(1)}, u32[]{:S(2)}, u32[]{:S(2)}) collective-permute-start(bf16[48,2048]{1,0:T(8,128)(2,1)S(1)} %constant_dynamic-update-slice_fusion.refs_0_), channel_id=1, source_target_pairs={{0,4},{2,6},{4,0},{6,2},{1,5},{3,7},{5,1},{7,3},{8,12},{10,14},{12... | collective-permute-start | bytes 589832 | tf_op jit(solution)/shard_map/ppermute | solution.py:257
  16.4 11.6 %collective-permute-start.3 = (bf16[48,2048]{1,0:T(8,128)(2,1)S(1)}, bf16[48,2048]{1,0:T(8,128)(2,1)S(1)}, u32[]{:S(2)}, u32[]{:S(2)}) collective-permute-start(bf16[48,2048]{1,0:T(8,128)(2,1)S(1)} %constant_dynamic-update-slice_fusion.refs_0_), channel_id=1, source_target_pairs={{0,2},{2,4},{4,6},{6,0},{1,3},{3,5},{5,7},{7,1},{8,10},{10,12},{12... | collective-permute-start | bytes 589832 | tf_op jit(solution)/shard_map/ppermute | solution.py:257
  17.0 12.0 %collective-permute-start.2 = (bf16[48,2048]{1,0:T(8,128)(2,1)S(1)}, bf16[48,2048]{1,0:T(8,128)(2,1)S(1)}, u32[]{:S(2)}, u32[]{:S(2)}) collective-permute-start(bf16[48,2048]{1,0:T(8,128)(2,1)S(1)} %constant_dynamic-update-slice_fusion.refs_0_), channel_id=1, source_target_pairs={{0,1},{1,0},{2,3},{3,2},{4,5},{5,4},{6,7},{7,6},{8,9},{9,8},{10,11... | collective-permute-start | bytes 589832 | tf_op jit(solution)/shard_map/ppermute | solution.py:257
  20.4 8.5 %collective-permute-start.8 = (bf16[48,2048]{1,0:T(8,128)(2,1)S(1)}, bf16[48,2048]{1,0:T(8,128)(2,1)S(1)}, u32[]{:S(2)}, u32[]{:S(2)}) collective-permute-start(bf16[48,2048]{1,0:T(8,128)(2,1)S(1)} %collective-permute-done.7.refs_6_), channel_id=1, source_target_pairs={{0,1},{1,0},{2,3},{3,2},{4,5},{5,4},{6,7},{7,6},{8,9},{9,8},{10,11... | collective-permute-start | bytes 589832 | tf_op jit(solution)/shard_map/ppermute | solution.py:257
  25.2 3.8 %collective-permute-start.6 = (bf16[48,2048]{1,0:T(8,128)(2,1)S(1)}, bf16[48,2048]{1,0:T(8,128)(2,1)S(1)}, u32[]{:S(2)}, u32[]{:S(2)}) collective-permute-start(bf16[48,2048]{1,0:T(8,128)(2,1)S(1)} %collective-permute-done.5.refs_4_), channel_id=1, source_target_pairs={{0,1},{1,0},{2,3},{3,2},{4,5},{5,4},{6,7},{7,6},{8,9},{9,8},{10,11... | collective-permute-start | bytes 589832 | tf_op jit(solution)/shard_map/ppermute | solution.py:257
  28.0 2.0 %collective-permute-start.4 = (bf16[48,2048]{1,0:T(8,128)(2,1)S(1)}, bf16[48,2048]{1,0:T(8,128)(2,1)S(1)}, u32[]{:S(2)}, u32[]{:S(2)}) collective-permute-start(bf16[48,2048]{1,0:T(8,128)(2,1)S(1)} %collective-permute-done.3.refs_2_), channel_id=1, source_target_pairs={{0,1},{1,0},{2,3},{3,2},{4,5},{5,4},{6,7},{7,6},{8,9},{9,8},{10,11... | collective-permute-start | bytes 589832 | tf_op jit(solution)/shard_map/ppermute | solution.py:257
  51.2 10.9 %collective-permute-start.11 = (bf16[192,256]{1,0:T(8,128)(2,1)S(1)}, bf16[192,256]{1,0:T(8,128)(2,1)S(1)}, u32[]{:S(2)}, u32[]{:S(2)}) collective-permute-start(bf16[192,256]{1,0:T(8,128)(2,1)S(1)} %shard_map.48.tie_ref.refs_0_), channel_id=1, source_target_pairs={{0,64},{32,96},{64,128},{96,160},{128,192},{160,224},{192,0},{224,... | collective-permute-start | bytes 294920 | tf_op jit(solution)/shard_map/ppermute | solution.py:257
  52.6 9.5 %collective-permute-start.10 = (bf16[192,256]{1,0:T(8,128)(2,1)S(1)}, bf16[192,256]{1,0:T(8,128)(2,1)S(1)}, u32[]{:S(2)}, u32[]{:S(2)}) collective-permute-start(bf16[192,256]{1,0:T(8,128)(2,1)S(1)} %shard_map.48.tie_ref.refs_0_), channel_id=1, source_target_pairs={{0,32},{32,64},{64,96},{96,128},{128,160},{160,192},{192,224},{224... | collective-permute-start | bytes 294920 | tf_op jit(solution)/shard_map/ppermute | solution.py:257
  57.7 5.1 %collective-permute-start.9 = (bf16[192,256]{1,0:T(8,128)(2,1)S(1)}, bf16[192,256]{1,0:T(8,128)(2,1)S(1)}, u32[]{:S(2)}, u32[]{:S(2)}) collective-permute-start(bf16[192,256]{1,0:T(8,128)(2,1)S(1)} %shard_map.48.tie_ref.refs_0_), channel_id=1, source_target_pairs={{0,1},{1,0},{2,3},{3,2},{4,5},{5,4},{6,7},{7,6},{8,9},{9,8},{10,11... | collective-permute-start | bytes 294920 | tf_op jit(solution)/shard_map/ppermute | solution.py:257
  58.8 5.1 %copy-start = (bf16[3,3,3,256,256]{4,3,2,1,0:T(8,128)(2,1)S(1)}, bf16[3,3,3,256,256]{4,3,2,1,0:T(8,128)(2,1)}, u32[]{:S(2)}) copy-start(bf16[3,3,3,256,256]{4,3,2,1,0:T(8,128)(2,1)} %refs_7_.1) | copy-start | bytes 10616836
  62.2 1.4 %collective-permute-start.12 = (bf16[192,256]{1,0:T(8,128)(2,1)S(1)}, bf16[192,256]{1,0:T(8,128)(2,1)S(1)}, u32[]{:S(2)}, u32[]{:S(2)}) collective-permute-start(bf16[192,256]{1,0:T(8,128)(2,1)S(1)} %collective-permute-done.10.refs_2_), channel_id=1, source_target_pairs={{0,1},{1,0},{2,3},{3,2},{4,5},{5,4},{6,7},{7,6},{8,9},{9,8},{10,11... | collective-permute-start | bytes 294920 | tf_op jit(solution)/shard_map/ppermute | solution.py:257
  62.6 1.3 %collective-permute-start.13 = (bf16[192,256]{1,0:T(8,128)(2,1)S(1)}, bf16[192,256]{1,0:T(8,128)(2,1)S(1)}, u32[]{:S(2)}, u32[]{:S(2)}) collective-permute-start(bf16[192,256]{1,0:T(8,128)(2,1)S(1)} %collective-permute-done.11.refs_4_), channel_id=1, source_target_pairs={{0,1},{1,0},{2,3},{3,2},{4,5},{5,4},{6,7},{7,6},{8,9},{9,8},{10,11... | collective-permute-start | bytes 294920 | tf_op jit(solution)/shard_map/ppermute | solution.py:257
  67.1 7.1 %collective-permute-start.14 = (bf16[256,256]{1,0:T(8,128)(2,1)S(1)}, bf16[256,256]{1,0:T(8,128)(2,1)S(1)}, u32[]{:S(2)}, u32[]{:S(2)}) collective-permute-start(bf16[256,256]{1,0:T(8,128)(2,1)S(1)} %get-tuple-element.21), channel_id=1, source_target_pairs={{0,32},{32,64},{64,96},{96,128},{128,160},{160,192},{192,224},{224... | collective-permute-start | bytes 393224 | tf_op jit(solution)/shard_map/ppermute | solution.py:257
  67.8 9.1 %collective-permute-start.15 = (bf16[256,256]{1,0:T(8,128)(2,1)S(1)}, bf16[256,256]{1,0:T(8,128)(2,1)S(1)}, u32[]{:S(2)}, u32[]{:S(2)}) collective-permute-start(bf16[256,256]{1,0:T(8,128)(2,1)S(1)} %get-tuple-element.22), channel_id=1, source_target_pairs={{0,64},{32,96},{64,128},{96,160},{128,192},{160,224},{192,0},{224,... | collective-permute-start | bytes 393224 | tf_op jit(solution)/shard_map/ppermute | solution.py:257

commit v5 on v4

--- a/solution.py
+++ b/solution.py
@@ -152,13 +152,12 @@
     out_ref[...] = order_ref[...].T[: out_ref.shape[0]].astype(BF16)
 
 
-def stage_kernel(weight_ref, tie_ref, out_ref, sems):
+def stage_kernel(at_ref, weight_ref, tie_ref, out_ref, sems):
+    c = at_ref[2]
     copies = []
-    for n in range(18):
-        i, j, c = n // 6, n // 2 % 3, n % 2
-        copies.append(pltpu.make_async_copy(weight_ref.at[:, i, j, :, c], out_ref.at[n // 2, :, c], sems.at[n]))
-    for copy in copies:
-        copy.start()
+    for n in range(9):
+        copies.append(pltpu.make_async_copy(weight_ref.at[:, n // 3, n % 3, :, c], out_ref.at[n], sems.at[n]))
+        copies[n].start()
     for copy in copies:
         copy.wait()
 
@@ -171,66 +170,81 @@
     return pltpu.roll(v, v.shape[0] - 1, 0)
 
 
-def fine_kernel(across, at_ref, *refs):
-    halves, (wide_ref, last_ref, first_ref, second_ref, own_ref, frames_ref) = refs[:6], refs[6:]
-    c, t, strip, strips = at_ref[2], at_ref[3], at_ref[4], at_ref[5]
-    cells, channels, width = 4 * PITCH, halves[0].shape[1] * 2, own_ref.shape[1]
-    rows = pl.ds(pl.multiple_of(c * 2 * PITCH, 2 * PITCH), cells)
+def wide_kernel(at_ref, own_ref, first_ref, second_ref, wide_ref, keep_ref, send_ref, frames_ref, sum_ref):
+    c, t = at_ref[2], at_ref[3]
+    halves = (own_ref, first_ref, second_ref)
+    half, width = own_ref.shape[1], keep_ref.shape[2]
 
     def put(k, part):
-        for n, side in enumerate((c, 1 - c)):
-            to = pl.multiple_of(k * channels + side * (channels // 2), channels // 2)
-            frames_ref[:, pl.ds(to, channels // 2)] = halves[2 * part + n][rows, :]
+        frames_ref[:, k * half : (k + 1) * half] = halves[part][...]
 
     put(2, 0)
     for k in range(2):
         for part in range(3 - k):
             pl.when(jnp.minimum(t, 2 - k) == part)(functools.partial(put, k, part))
     frames = frames_ref[...]
-    spans = ((0, 3), (0, 4), (1, 4))
-    maps = ((0, 0, 1, 1, 2, 2), (0, 1, 1, 2, 2, 3), (0, 0, 1, 1, 2, 2))
-    even, odd = [None] * 6, [None] * 6
+    spans = ((0, 5), (0, 6), (1, 6))
+    count = 10
+    even, odd = [None] * count, [None] * count
     for i in range(3):
         lo, hi = spans[i]
         sums = []
         for j in range(3):
-            sums.append(
-                jnp.dot(frames[lo * PITCH : hi * PITCH], wide_ref[i * 3 + j].reshape(3 * channels, width), preferred_element_type=F32)
-            )
+            taps = wide_ref[i * 3 + j].reshape(3 * half, width)
+            sums.append(jnp.dot(frames[lo * PITCH : hi * PITCH], taps, preferred_element_type=F32))
         at_even = down(sums[0]) + sums[1] + sums[2]
         at_odd = sums[0] + sums[1] + up(sums[2])
-        for r in range(6):
-            at = slice(maps[i][r] * PITCH, (maps[i][r] + 1) * PITCH)
+        for r in range(count):
+            n = (r + 1) // 2 if i == 1 else r // 2
+            at = slice(n * PITCH, (n + 1) * PITCH)
             even[r] = at_even[at] if even[r] is None else even[r] + at_even[at]
             odd[r] = at_odd[at] if odd[r] is None else odd[r] + at_odd[at]
-    mid = [jnp.concatenate(rows, 0).astype(BF16).astype(F32) for rows in (even, odd)]
-    shape = mid[0].shape
+    for p, rows in enumerate((even, odd)):
+        for r in range(count):
+            sum_ref[p, r * PITCH : (r + 1) * PITCH] = rows[r]
+    step = 4 * PITCH
+    size = keep_ref.shape[1]
+    keep_ref[...] = sum_ref[:, pl.ds(pl.multiple_of(c * step, step), size), :]
+    send_ref[...] = sum_ref[:, pl.ds(pl.multiple_of((1 - c) * step, step), size), :].astype(BF16)
+
+
+def taps_of(k, acts, last_ref):
+    size = 4 * PITCH
+    parts = []
+    for j in range(3):
+        total = None
+        for i in range(3):
+            rows = slice(i * PITCH, i * PITCH + size)
+            both = jnp.concatenate([acts[0][rows], acts[1][rows]], 0)
+            part = jnp.dot(both, last_ref[k, i, j], preferred_element_type=F32)
+            total = part if total is None else total + part
+        parts.append(total)
+    at_even = down(parts[0][size:]) + parts[1][:size] + parts[2][size:]
+    at_odd = parts[0][:size] + parts[1][size:] + up(parts[2][:size])
+    return jnp.concatenate([at_even, at_odd], 0)
+
+
+def fine_kernel(across, at_ref, keep_ref, got_ref, last_ref, first_ref, second_ref, mid_ref, act_ref):
+    t, strip, strips = at_ref[3], at_ref[4], at_ref[5]
+    mid = (keep_ref[...] + got_ref[...].astype(F32)).astype(BF16)
+    shape = mid.shape[1:]
     row = lax.broadcasted_iota(jnp.int32, shape, 0) // PITCH
     keep = column_mask(shape, 0, across)
     keep = keep & ((row > 0) | (strip > 0)) & ((row < 5) | (strip < strips - 1))
-    acts = [jnp.where(keep, silu(m), 0.0).astype(BF16) for m in mid]
-    size = 4 * PITCH
-    sums = []
-    for k in range(3):
-        parts = []
-        for j in range(3):
-            total = None
-            for i in range(3):
-                rows = slice(i * PITCH, i * PITCH + size)
-                both = jnp.concatenate([acts[0][rows], acts[1][rows]], 0)
-                part = jnp.dot(both, last_ref[k, i, j], preferred_element_type=F32)
-                total = part if total is None else total + part
-            parts.append(total)
-        at_even = down(parts[0][size:]) + parts[1][:size] + parts[2][size:]
-        at_odd = parts[0][:size] + parts[1][size:] + up(parts[2][:size])
-        sums.append(jnp.concatenate([at_even, at_odd], 0))
-    start = t == 0
-    late = sums[0] + sums[1]
-    first_ref[...] = jnp.where(start, late, sums[1]).astype(BF16)
+    acts = [jnp.where(keep, silu(mid[p].astype(F32)), 0.0).astype(BF16) for p in range(2)]
+    for p in range(2):
+        act_ref[p] = acts[p]
+        mid_ref[p * 4 * PITCH : (p + 1) * 4 * PITCH] = mid[p, PITCH : 5 * PITCH]
+    sums = [taps_of(k, acts, last_ref) for k in range(2)]
+    first_ref[...] = jnp.where(t == 0, sums[0] + sums[1], sums[1]).astype(BF16)
     second_ref[...] = sums[0].astype(BF16)
-    rows = slice(PITCH, PITCH + size)
-    own = jnp.concatenate([mid[0][rows], mid[1][rows]], 0) + sums[2]
-    own_ref[...] = jnp.where(start, own + late, own)
+
+
+def own_kernel(at_ref, mid_ref, act_ref, last_ref, first_ref, own_ref):
+    acts = [act_ref[p] for p in range(2)]
+    own = mid_ref[...].astype(F32) + taps_of(2, acts, last_ref)
+    late = first_ref[...].astype(F32)
+    own_ref[...] = own + jnp.where(at_ref[3] == 0, late, jnp.zeros(late.shape, F32))
 
 
 def last_kernel(across, at_ref, own_ref, first_ref, second_ref, out_ref, order_ref):
@@ -304,24 +318,31 @@
         compiler_params=pltpu.CompilerParams(vmem_limit_bytes=LIMIT),
     )(parts)
     width = weight_two.shape[4]
+    source = weight_two.reshape(3, 3, 3, -1, 2, shard, width)
     wide = call(
         stage_kernel,
-        jax.ShapeDtypeStruct((9, 3, 2, channels // 2 // shard, shard, width), BF16),
-        (pltpu.with_memory_space_constraint(weight_two.reshape(3, 3, 3, -1, 2, shard, width), pltpu.HBM), own),
-        (pltpu.SemaphoreType.DMA((18,)),),
-        [HBM, pl.BlockSpec(memory_space=pl.ANY)],
-    )
-    moved = [turned(own, "tm", d) for d in (1, 2)]
-    wide, *moved = lax.optimization_barrier((wide, *moved))
-    halves = []
-    for half in (own, *moved):
-        halves += [half, turned(half, "c", 1)]
+        jax.ShapeDtypeStruct((9, 3, channels // 2 // shard, shard, width), BF16),
+        (at, pltpu.with_memory_space_constraint(source, pltpu.HBM), own),
+        (pltpu.SemaphoreType.DMA((9,)),),
+        [SMEM, HBM, pl.BlockSpec(memory_space=pl.ANY)],
+    )
+    rows = 6 * PITCH
+    keep, send = call(
+        wide_kernel,
+        (jax.ShapeDtypeStruct((2, rows, width), F32), jax.ShapeDtypeStruct((2, rows, width), BF16)),
+        (at, own, turned(own, "tm", 1), turned(own, "tm", 2), wide),
+        (pltpu.VMEM((rows, 3 * channels // 2), BF16), pltpu.VMEM((2, 10 * PITCH, width), F32)),
+    )
     small = jax.ShapeDtypeStruct((8 * PITCH, width), BF16)
-    first, second, own = call(
+    first, second, mid, act = call(
         functools.partial(fine_kernel, across),
-        (small, small, jax.ShapeDtypeStruct((8 * PITCH, width), F32)),
-        (at, *halves, wide, weight_three),
-        (pltpu.VMEM((4 * PITCH, 3 * channels), BF16),),
+        (small, small, small, jax.ShapeDtypeStruct((2, rows, width), BF16)),
+        (at, keep, turned(send, "c", 1), weight_three),
+    )
+    own = call(
+        own_kernel,
+        jax.ShapeDtypeStruct((8 * PITCH, width), F32),
+        (at, mid, act, weight_three, first),
     )
     decoded = call(
         functools.partial(last_kernel, across),

time: 78.5 us -> 77 us (0.981); the launches traced: 78.3 us -> 75.6 us
  waiting for transfers between devices: 13 us -> 10.2 us
    ppermute x16 -> x14, waiting for transfers between devices: 13 us -> 10.2 us  [turned(): lax.ppermute(block, axis, [(i, (i + distance) % count) for i in range(cou...]
    ppermute x16 -> x14, starting transfers between devices: 26.5 us -> 26.6 us  [turned(): lax.ppermute(block, axis, [(i, (i + distance) % count) for i in range(cou...]
    pallas_call x5 -> x7, Pallas kernels: 11.9 us -> 11.9 us  [call(): pl.pallas_call(kernel, out_shape=out_shape, in_specs=specs, out_specs=jax...]
  transfers between devices with their start and end apart: 17 -> 15, of which waited for: 7 -> 7; matrix products, arithmetic and copies ran while one was open for 0% -> 0% of each run, Pallas kernels for 4% -> 5%
where the time goes in v5:
time: 77 us; the launch traced here: 75.6 us
  starting transfers between devices  33.9 us (44%)
  blocking collectives  18.5 us (24%)
  Pallas kernels  12.1 us (16%)
  waiting for transfers between devices  10.2 us (13%)
  local copies, waits for them, and re-layouts  0.79 us (1%)
    ppermute x14, starting transfers between devices, turned(): lax.ppermute(block, axis, [(i, (i + distance) % count) for i in range(cou...  26.6 us
    all_to_all x1, blocking collectives, on_device(): parts = lax.all_to_all(cut, ('z', 'x'), 0, 0, tiled=True)  18.5 us
    pallas_call x7, Pallas kernels, call(): pl.pallas_call(kernel, out_shape=out_shape, in_specs=specs, out_specs=jax...  11.9 us
    ppermute x14, waiting for transfers between devices, turned(): lax.ppermute(block, axis, [(i, (i + distance) % count) for i in range(cou...  10.2 us
    all_to_all x1, starting transfers between devices, on_device(): slices = lax.all_to_all(slices, 'z', 0, 0, tiled=True)  7.28 us
  transfers between devices with their start and end apart: 15, of which 7 were waited for; matrix products, arithmetic and copies ran while one was open for 0% of the time, Pallas kernels for 5%

profile of v5, /device:TPU:1, one launch (start us, length us, event | category | flops | bytes accessed | tf_op | source)
XLA Modules:
  0.0 75.6 jit_solution(174388019506261861)
XLA Ops:
  0.0 2.1 %shard_map.46 = (bf16[16,2048]{1,0:T(8,128)(2,1)S(1)}, bf16[16,2048]{1,0:T(8,128)(2,1)S(1)}, bf16[4,432,128]{2,1,0:T(8,128)(2,1)}) custom-call(bf16[30,16,64]{2,1,0:T(8,128)(2,1)} %bitcast.17, bf16[432,512]{1,0:T(8,128)(2,1)} %bitcast.16), custom_call_target="tpu_custom_call" | custom-call | tf_op jit(solution)/shard_map/pallas_call | solution.py:23
  2.1 2.2 %collective-permute-start.1 = (bf16[16,2048]{1,0:T(8,128)(2,1)S(1)}, bf16[16,2048]{1,0:T(8,128)(2,1)S(1)}, u32[]{:S(2)}, u32[]{:S(2)}) collective-permute-start(bf16[16,2048]{1,0:T(8,128)(2,1)S(1)} %get-tuple-element.16), channel_id=1, source_target_pairs={{0,64},{32,96},{64,128},{96,160},{128,192},{160,224},{192,0},{224,... | collective-permute-start | bytes 196616 | tf_op jit(solution)/shard_map/ppermute | solution.py:271
  4.3 1.6 %collective-permute-start = (bf16[16,2048]{1,0:T(8,128)(2,1)S(1)}, bf16[16,2048]{1,0:T(8,128)(2,1)S(1)}, u32[]{:S(2)}, u32[]{:S(2)}) collective-permute-start(bf16[16,2048]{1,0:T(8,128)(2,1)S(1)} %get-tuple-element.16), channel_id=1, source_target_pairs={{0,32},{32,64},{64,96},{96,128},{128,160},{160,192},{192,224},{224... | collective-permute-start | bytes 196616 | tf_op jit(solution)/shard_map/ppermute | solution.py:271
  5.9 7.3 %all-to-all-start = ((bf16[4,432,128]{2,1,0:T(8,128)(2,1)}), bf16[4,432,128]{2,1,0:T(8,128)(2,1)S(1)}, u32[]{:S(2)}, u32[]{:S(2)}) async-start(bf16[4,432,128]{2,1,0:T(8,128)(2,1)} %get-tuple-element.15), calls=%async_computation | async-start | bytes 884736 | tf_op jit(solution)/shard_map/all_to_all | solution.py:298
  13.3 2.6 %collective-permute-start.7 = (bf16[48,2048]{1,0:T(8,128)(2,1)S(1)}, bf16[48,2048]{1,0:T(8,128)(2,1)S(1)}, u32[]{:S(2)}, u32[]{:S(2)}) collective-permute-start(bf16[48,2048]{1,0:T(8,128)(2,1)S(1)} %constant_dynamic-update-slice_fusion.refs_0_), channel_id=1, source_target_pairs={{0,6},{2,0},{4,2},{6,4},{1,7},{3,1},{5,3},{7,5},{8,14},{10,8},{12,... | collective-permute-start | bytes 589832 | tf_op jit(solution)/shard_map/ppermute | solution.py:271
  17.0 2.4 %collective-permute-start.2 = (bf16[48,2048]{1,0:T(8,128)(2,1)S(1)}, bf16[48,2048]{1,0:T(8,128)(2,1)S(1)}, u32[]{:S(2)}, u32[]{:S(2)}) collective-permute-start(bf16[48,2048]{1,0:T(8,128)(2,1)S(1)} %constant_dynamic-update-slice_fusion.refs_0_), channel_id=1, source_target_pairs={{0,1},{1,0},{2,3},{3,2},{4,5},{5,4},{6,7},{7,6},{8,9},{9,8},{10,11... | collective-permute-start | bytes 589832 | tf_op jit(solution)/shard_map/ppermute | solution.py:271
  19.3 1.1 %collective-permute-done.7.refs_6_ = bf16[48,2048]{1,0:T(8,128)(2,1)S(1)} collective-permute-done((bf16[48,2048]{1,0:T(8,128)(2,1)S(1)}, bf16[48,2048]{1,0:T(8,128)(2,1)S(1)}, u32[]{:S(2)}, u32[]{:S(2)}) %collective-permute-start.7) | collective-permute-done | bytes 196640 | tf_op jit(solution)/shard_map/ppermute | solution.py:271
  20.4 4.8 %collective-permute-start.8 = (bf16[48,2048]{1,0:T(8,128)(2,1)S(1)}, bf16[48,2048]{1,0:T(8,128)(2,1)S(1)}, u32[]{:S(2)}, u32[]{:S(2)}) collective-permute-start(bf16[48,2048]{1,0:T(8,128)(2,1)S(1)} %collective-permute-done.7.refs_6_), channel_id=1, source_target_pairs={{0,1},{1,0},{2,3},{3,2},{4,5},{5,4},{6,7},{7,6},{8,9},{9,8},{10,11... | collective-permute-start | bytes 589832 | tf_op jit(solution)/shard_map/ppermute | solution.py:271
  25.2 1.6 %collective-permute-start.6 = (bf16[48,2048]{1,0:T(8,128)(2,1)S(1)}, bf16[48,2048]{1,0:T(8,128)(2,1)S(1)}, u32[]{:S(2)}, u32[]{:S(2)}) collective-permute-start(bf16[48,2048]{1,0:T(8,128)(2,1)S(1)} %collective-permute-done.5.refs_4_), channel_id=1, source_target_pairs={{0,1},{1,0},{2,3},{3,2},{4,5},{5,4},{6,7},{7,6},{8,9},{9,8},{10,11... | collective-permute-start | bytes 589832 | tf_op jit(solution)/shard_map/ppermute | solution.py:271
  26.8 1.1 %collective-permute-done.3.refs_2_ = bf16[48,2048]{1,0:T(8,128)(2,1)S(1)} collective-permute-done((bf16[48,2048]{1,0:T(8,128)(2,1)S(1)}, bf16[48,2048]{1,0:T(8,128)(2,1)S(1)}, u32[]{:S(2)}, u32[]{:S(2)}) %collective-permute-start.3) | collective-permute-done | bytes 196640 | tf_op jit(solution)/shard_map/ppermute | solution.py:271
  29.0 1.0 %collective-permute-done.4.refs_3_ = bf16[48,2048]{1,0:T(8,128)(2,1)S(1)} collective-permute-done((bf16[48,2048]{1,0:T(8,128)(2,1)S(1)}, bf16[48,2048]{1,0:T(8,128)(2,1)S(1)}, u32[]{:S(2)}, u32[]{:S(2)}) %collective-permute-start.4) | collective-permute-done | bytes 196640 | tf_op jit(solution)/shard_map/ppermute | solution.py:271
  29.9 2.5 %shard_map.47 = bf16[16,96,128]{2,1,0:T(8,128)(2,1)S(1)} custom-call(s32[6]{0:T(128)S(1)} %stack.23.at_ref, bf16[16,2048]{1,0:T(8,128)(2,1)S(1)} %get-tuple-element.14.field_ref, bf16[4,432,128]{2,1,0:T(8,128)(2,1)S(1)} %all-to-all-done.slices_ref, bf16[48,2048]{1,0:T(8,128)(2,1)S(1)} %constant_dynamic-update-slice_fusion.refs_0_, ...), custom_call_target="tpu_custom_call" | custom-call | tf_op jit(solution)/shard_map/pallas_call | solution.py:23
  32.5 18.5 %all_to_all.10.parts_ref = bf16[16,96,128]{2,1,0:T(8,128)(2,1)S(1)} all-to-all(bf16[16,96,128]{2,1,0:T(8,128)(2,1)S(1)} %shard_map.47), channel_id=1, replica_groups=mesh['tm'=8,'z'=4,'x'=4,'c'=2] {'z','x'}, dimensions={0} | all-to-all | bytes 786432 | tf_op jit(solution)/shard_map/all_to_all | solution.py:313
  51.2 1.4 %collective-permute-start.10 = (bf16[192,256]{1,0:T(8,128)(2,1)S(1)}, bf16[192,256]{1,0:T(8,128)(2,1)S(1)}, u32[]{:S(2)}, u32[]{:S(2)}) collective-permute-start(bf16[192,256]{1,0:T(8,128)(2,1)S(1)} %shard_map.48.tie_ref.own_ref), channel_id=1, source_target_pairs={{0,64},{32,96},{64,128},{96,160},{128,192},{160,224},{192,0},{224,... | collective-permute-start | bytes 294920 | tf_op jit(solution)/shard_map/ppermute | solution.py:271
  52.6 5.0 %collective-permute-start.9 = (bf16[192,256]{1,0:T(8,128)(2,1)S(1)}, bf16[192,256]{1,0:T(8,128)(2,1)S(1)}, u32[]{:S(2)}, u32[]{:S(2)}) collective-permute-start(bf16[192,256]{1,0:T(8,128)(2,1)S(1)} %shard_map.48.tie_ref.own_ref), channel_id=1, source_target_pairs={{0,32},{32,64},{64,96},{96,128},{128,160},{160,192},{192,224},{224... | collective-permute-start | bytes 294920 | tf_op jit(solution)/shard_map/ppermute | solution.py:271
  57.7 2.7 %shard_map.49.wide_ref = bf16[9,3,16,16,256]{4,3,2,1,0:T(8,128)(2,1)S(1)} custom-call(s32[6]{0:T(128)S(1)} %stack.23.at_ref, bf16[3,3,3,16,2,16,256]{6,5,4,3,2,1,0:T(8,128)(2,1)} %bitcast.15, bf16[192,256]{1,0:T(8,128)(2,1)S(1)} %shard_map.48.tie_ref.own_ref), custom_call_target="tpu_custom_call" | custom-call | tf_op jit(solution)/shard_map/pallas_call | solution.py:23
  60.8 1.4 %shard_map.50 = (f32[2,192,256]{2,1,0:T(8,128)S(1)}, bf16[2,192,256]{2,1,0:T(8,128)(2,1)S(1)}) custom-call(s32[6]{0:T(128)S(1)} %stack.23.at_ref, bf16[192,256]{1,0:T(8,128)(2,1)S(1)} %shard_map.48.tie_ref.own_ref, bf16[192,256]{1,0:T(8,128)(2,1)S(1)} %collective-permute-done.9.first_ref, bf16[192,256]{1,0:T(8,128)(2,1)S(1)} %collective-permute-done.10.second_ref, ...), custom_call_target="tpu_custom_call" | custom-call | tf_op jit(solution)/shard_map/pallas_call | solution.py:23
  62.3 1.9 %collective-permute-start.11 = (bf16[2,192,256]{2,1,0:T(8,128)(2,1)S(1)}, bf16[2,192,256]{2,1,0:T(8,128)(2,1)S(1)}, u32[]{:S(2)}, u32[]{:S(2)}) collective-permute-start(bf16[2,192,256]{2,1,0:T(8,128)(2,1)S(1)} %get-tuple-element.18), channel_id=1, source_target_pairs={{0,1},{1,0},{2,3},{3,2},{4,5},{5,4},{6,7},{7,6},{8,9},{9,8},{10,11... | collective-permute-start | bytes 589832 | tf_op jit(solution)/shard_map/ppermute | solution.py:271
  64.1 1.1 %collective-permute-done.11.got_ref = bf16[2,192,256]{2,1,0:T(8,128)(2,1)S(1)} collective-permute-done((bf16[2,192,256]{2,1,0:T(8,128)(2,1)S(1)}, bf16[2,192,256]{2,1,0:T(8,128)(2,1)S(1)}, u32[]{:S(2)}, u32[]{:S(2)}) %collective-permute-start.11) | collective-permute-done | bytes 196640 | tf_op jit(solution)/shard_map/ppermute | solution.py:271
  65.2 1.4 %shard_map.51 = (bf16[256,256]{1,0:T(8,128)(2,1)S(1)}, bf16[256,256]{1,0:T(8,128)(2,1)S(1)}, bf16[256,256]{1,0:T(8,128)(2,1)S(1)}, bf16[2,192,256]{2,1,0:T(8,128)(2,1)S(1)}) custom-call(s32[6]{0:T(128)S(1)} %stack.23.at_ref, f32[2,192,256]{2,1,0:T(8,128)S(1)} %get-tuple-element.17.keep_ref, bf16[2,192,256]{2,1,0:T(8,128)(2,1)S(1)} %collective-permute-done.11.got_ref, ...), custom_call_target="tpu_custom_call" | custom-call | tf_op jit(solution)/shard_map/pallas_call | solution.py:23
  66.6 1.1 %collective-permute-start.13 = (bf16[256,256]{1,0:T(8,128)(2,1)S(1)}, bf16[256,256]{1,0:T(8,128)(2,1)S(1)}, u32[]{:S(2)}, u32[]{:S(2)}) collective-permute-start(bf16[256,256]{1,0:T(8,128)(2,1)S(1)} %get-tuple-element.22), channel_id=1, source_target_pairs={{0,64},{32,96},{64,128},{96,160},{128,192},{160,224},{192,0},{224,... | collective-permute-start | bytes 393224 | tf_op jit(solution)/shard_map/ppermute | solution.py:271
  67.7 1.0 %shard_map.52.own_ref = f32[256,256]{1,0:T(8,128)S(1)} custom-call(s32[6]{0:T(128)S(1)} %stack.23.at_ref, bf16[256,256]{1,0:T(8,128)(2,1)S(1)} %get-tuple-element.19.mid_ref, bf16[2,192,256]{2,1,0:T(8,128)(2,1)S(1)} %get-tuple-element.20.act_ref, bf16[3,3,3,256,256]{4,3,2,1,0:T(8,128)(2,1)S(1)} %copy-done, bf16[256,256]{1,0:T(8,128)(2,1)S(1)} %get-tuple-element.21.first_ref), custom_call_target="tpu_custom_call" | custom-call | tf_op jit(solution)/shard_map/pallas_call | solution.py:23
  68.7 4.3 %collective-permute-done.13.second_ref = bf16[256,256]{1,0:T(8,128)(2,1)S(1)} collective-permute-done((bf16[256,256]{1,0:T(8,128)(2,1)S(1)}, bf16[256,256]{1,0:T(8,128)(2,1)S(1)}, u32[]{:S(2)}, u32[]{:S(2)}) %collective-permute-start.13) | collective-permute-done | bytes 131104 | tf_op jit(solution)/shard_map/ppermute | solution.py:271
  73.0 1.3 %collective-permute-done.12.first_ref = bf16[256,256]{1,0:T(8,128)(2,1)S(1)} collective-permute-done((bf16[256,256]{1,0:T(8,128)(2,1)S(1)}, bf16[256,256]{1,0:T(8,128)(2,1)S(1)}, u32[]{:S(2)}, u32[]{:S(2)}) %collective-permute-start.12) | collective-permute-done | bytes 131104 | tf_op jit(solution)/shard_map/ppermute | solution.py:271
  (22 shorter events, 4.1 us)
Async XLA Ops:
  2.1 11.2 %collective-permute-start.1 = (bf16[16,2048]{1,0:T(8,128)(2,1)S(1)}, bf16[16,2048]{1,0:T(8,128)(2,1)S(1)}, u32[]{:S(2)}, u32[]{:S(2)}) collective-permute-start(bf16[16,2048]{1,0:T(8,128)(2,1)S(1)} %get-tuple-element.16), channel_id=1, source_target_pairs={{0,64},{32,96},{64,128},{96,160},{128,192},{160,224},{192,0},{224,... | collective-permute-start | bytes 196616 | tf_op jit(solution)/shard_map/ppermute | solution.py:271
  4.3 8.9 %collective-permute-start = (bf16[16,2048]{1,0:T(8,128)(2,1)S(1)}, bf16[16,2048]{1,0:T(8,128)(2,1)S(1)}, u32[]{:S(2)}, u32[]{:S(2)}) collective-permute-start(bf16[16,2048]{1,0:T(8,128)(2,1)S(1)} %get-tuple-element.16), channel_id=1, source_target_pairs={{0,32},{32,64},{64,96},{96,128},{128,160},{160,192},{192,224},{224... | collective-permute-start | bytes 196616 | tf_op jit(solution)/shard_map/ppermute | solution.py:271
  5.9 24.0 %all-to-all-start = ((bf16[4,432,128]{2,1,0:T(8,128)(2,1)}), bf16[4,432,128]{2,1,0:T(8,128)(2,1)S(1)}, u32[]{:S(2)}, u32[]{:S(2)}) async-start(bf16[4,432,128]{2,1,0:T(8,128)(2,1)} %get-tuple-element.15), calls=%async_computation | async-start | bytes 884736 | tf_op jit(solution)/shard_map/all_to_all | solution.py:298
  13.3 7.1 %collective-permute-start.7 = (bf16[48,2048]{1,0:T(8,128)(2,1)S(1)}, bf16[48,2048]{1,0:T(8,128)(2,1)S(1)}, u32[]{:S(2)}, u32[]{:S(2)}) collective-permute-start(bf16[48,2048]{1,0:T(8,128)(2,1)S(1)} %constant_dynamic-update-slice_fusion.refs_0_), channel_id=1, source_target_pairs={{0,6},{2,0},{4,2},{6,4},{1,7},{3,1},{5,3},{7,5},{8,14},{10,8},{12,... | collective-permute-start | bytes 589832 | tf_op jit(solution)/shard_map/ppermute | solution.py:271
  15.8 9.4 %collective-permute-start.5 = (bf16[48,2048]{1,0:T(8,128)(2,1)S(1)}, bf16[48,2048]{1,0:T(8,128)(2,1)S(1)}, u32[]{:S(2)}, u32[]{:S(2)}) collective-permute-start(bf16[48,2048]{1,0:T(8,128)(2,1)S(1)} %constant_dynamic-update-slice_fusion.refs_0_), channel_id=1, source_target_pairs={{0,4},{2,6},{4,0},{6,2},{1,5},{3,7},{5,1},{7,3},{8,12},{10,14},{12... | collective-permute-start | bytes 589832 | tf_op jit(solution)/shard_map/ppermute | solution.py:271
  16.4 11.6 %collective-permute-start.3 = (bf16[48,2048]{1,0:T(8,128)(2,1)S(1)}, bf16[48,2048]{1,0:T(8,128)(2,1)S(1)}, u32[]{:S(2)}, u32[]{:S(2)}) collective-permute-start(bf16[48,2048]{1,0:T(8,128)(2,1)S(1)} %constant_dynamic-update-slice_fusion.refs_0_), channel_id=1, source_target_pairs={{0,2},{2,4},{4,6},{6,0},{1,3},{3,5},{5,7},{7,1},{8,10},{10,12},{12... | collective-permute-start | bytes 589832 | tf_op jit(solution)/shard_map/ppermute | solution.py:271
  17.0 12.0 %collective-permute-start.2 = (bf16[48,2048]{1,0:T(8,128)(2,1)S(1)}, bf16[48,2048]{1,0:T(8,128)(2,1)S(1)}, u32[]{:S(2)}, u32[]{:S(2)}) collective-permute-start(bf16[48,2048]{1,0:T(8,128)(2,1)S(1)} %constant_dynamic-update-slice_fusion.refs_0_), channel_id=1, source_target_pairs={{0,1},{1,0},{2,3},{3,2},{4,5},{5,4},{6,7},{7,6},{8,9},{9,8},{10,11... | collective-permute-start | bytes 589832 | tf_op jit(solution)/shard_map/ppermute | solution.py:271
  20.4 8.5 %collective-permute-start.8 = (bf16[48,2048]{1,0:T(8,128)(2,1)S(1)}, bf16[48,2048]{1,0:T(8,128)(2,1)S(1)}, u32[]{:S(2)}, u32[]{:S(2)}) collective-permute-start(bf16[48,2048]{1,0:T(8,128)(2,1)S(1)} %collective-permute-done.7.refs_6_), channel_id=1, source_target_pairs={{0,1},{1,0},{2,3},{3,2},{4,5},{5,4},{6,7},{7,6},{8,9},{9,8},{10,11... | collective-permute-start | bytes 589832 | tf_op jit(solution)/shard_map/ppermute | solution.py:271
  25.2 3.8 %collective-permute-start.6 = (bf16[48,2048]{1,0:T(8,128)(2,1)S(1)}, bf16[48,2048]{1,0:T(8,128)(2,1)S(1)}, u32[]{:S(2)}, u32[]{:S(2)}) collective-permute-start(bf16[48,2048]{1,0:T(8,128)(2,1)S(1)} %collective-permute-done.5.refs_4_), channel_id=1, source_target_pairs={{0,1},{1,0},{2,3},{3,2},{4,5},{5,4},{6,7},{7,6},{8,9},{9,8},{10,11... | collective-permute-start | bytes 589832 | tf_op jit(solution)/shard_map/ppermute | solution.py:271
  28.0 2.0 %collective-permute-start.4 = (bf16[48,2048]{1,0:T(8,128)(2,1)S(1)}, bf16[48,2048]{1,0:T(8,128)(2,1)S(1)}, u32[]{:S(2)}, u32[]{:S(2)}) collective-permute-start(bf16[48,2048]{1,0:T(8,128)(2,1)S(1)} %collective-permute-done.3.refs_2_), channel_id=1, source_target_pairs={{0,1},{1,0},{2,3},{3,2},{4,5},{5,4},{6,7},{7,6},{8,9},{9,8},{10,11... | collective-permute-start | bytes 589832 | tf_op jit(solution)/shard_map/ppermute | solution.py:271
  51.2 9.2 %collective-permute-start.10 = (bf16[192,256]{1,0:T(8,128)(2,1)S(1)}, bf16[192,256]{1,0:T(8,128)(2,1)S(1)}, u32[]{:S(2)}, u32[]{:S(2)}) collective-permute-start(bf16[192,256]{1,0:T(8,128)(2,1)S(1)} %shard_map.48.tie_ref.own_ref), channel_id=1, source_target_pairs={{0,64},{32,96},{64,128},{96,160},{128,192},{160,224},{192,0},{224,... | collective-permute-start | bytes 294920 | tf_op jit(solution)/shard_map/ppermute | solution.py:271
  52.6 8.2 %collective-permute-start.9 = (bf16[192,256]{1,0:T(8,128)(2,1)S(1)}, bf16[192,256]{1,0:T(8,128)(2,1)S(1)}, u32[]{:S(2)}, u32[]{:S(2)}) collective-permute-start(bf16[192,256]{1,0:T(8,128)(2,1)S(1)} %shard_map.48.tie_ref.own_ref), channel_id=1, source_target_pairs={{0,32},{32,64},{64,96},{96,128},{128,160},{160,192},{192,224},{224... | collective-permute-start | bytes 294920 | tf_op jit(solution)/shard_map/ppermute | solution.py:271
  60.4 4.8 %copy-start = (bf16[3,3,3,256,256]{4,3,2,1,0:T(8,128)(2,1)S(1)}, bf16[3,3,3,256,256]{4,3,2,1,0:T(8,128)(2,1)}, u32[]{:S(2)}) copy-start(bf16[3,3,3,256,256]{4,3,2,1,0:T(8,128)(2,1)} %last_ref.3) | copy-start | bytes 10616836
  62.3 2.9 %collective-permute-start.11 = (bf16[2,192,256]{2,1,0:T(8,128)(2,1)S(1)}, bf16[2,192,256]{2,1,0:T(8,128)(2,1)S(1)}, u32[]{:S(2)}, u32[]{:S(2)}) collective-permute-start(bf16[2,192,256]{2,1,0:T(8,128)(2,1)S(1)} %get-tuple-element.18), channel_id=1, source_target_pairs={{0,1},{1,0},{2,3},{3,2},{4,5},{5,4},{6,7},{7,6},{8,9},{9,8},{10,11... | collective-permute-start | bytes 589832 | tf_op jit(solution)/shard_map/ppermute | solution.py:271
  66.6 6.4 %collective-permute-start.13 = (bf16[256,256]{1,0:T(8,128)(2,1)S(1)}, bf16[256,256]{1,0:T(8,128)(2,1)S(1)}, u32[]{:S(2)}, u32[]{:S(2)}) collective-permute-start(bf16[256,256]{1,0:T(8,128)(2,1)S(1)} %get-tuple-element.22), channel_id=1, source_target_pairs={{0,64},{32,96},{64,128},{96,160},{128,192},{160,224},{192,0},{224,... | collective-permute-start | bytes 393224 | tf_op jit(solution)/shard_map/ppermute | solution.py:271
  67.7 6.6 %collective-permute-start.12 = (bf16[256,256]{1,0:T(8,128)(2,1)S(1)}, bf16[256,256]{1,0:T(8,128)(2,1)S(1)}, u32[]{:S(2)}, u32[]{:S(2)}) collective-permute-start(bf16[256,256]{1,0:T(8,128)(2,1)S(1)} %get-tuple-element.21.first_ref), channel_id=1, source_target_pairs={{0,32},{32,64},{64,96},{96,128},{128,160},{160,192},{192,224},{224... | collective-permute-start | bytes 393224 | tf_op jit(solution)/shard_map/ppermute | solution.py:271

commit v6 on v5

--- a/solution.py
+++ b/solution.py
@@ -99,16 +99,12 @@
                 for j in range(3):
                     tap = (k * 3 + i) * 3 + j
                     to = j * wide + d * shard
-                    taps_ref[i, to : to + shard, k * group : (k + 1) * group] = slices_ref[
-                        d, tap * shard : (tap + 1) * shard, :
-                    ]
+                    at = (i * 3 + k) * group
+                    taps_ref[to : to + shard, at : at + group] = slices_ref[d, tap * shard : (tap + 1) * shard, :]
     span = 4 * LANES
     for n in range(cells // span):
-        total = None
-        for i in range(3):
-            lo = i * LANES + n * span
-            part = jnp.dot(taps_ref[i], all_ref[:, lo : lo + span], preferred_element_type=F32)
-            total = part if total is None else total + part
+        shifted = [all_ref[:, i * LANES + n * span : i * LANES + (n + 1) * span] for i in range(3)]
+        total = jnp.dot(taps_ref[...], jnp.concatenate(shifted, 0), preferred_element_type=F32)
         for v in range(4):
             left, here, right = (total[j * wide : (j + 1) * wide, v * LANES : (v + 1) * LANES] for j in range(3))
             lo = LANES + n * span + v * LANES
@@ -306,7 +302,7 @@
         (at, field, slices, *blocks),
         (
             pltpu.VMEM((3 * channels // 4, cells + 2 * LANES), BF16),
-            pltpu.VMEM((3, 12 * shard, 3 * channels // 4), BF16),
+            pltpu.VMEM((12 * shard, 9 * channels // 4), BF16),
             pltpu.VMEM((4 * shard, cells + 2 * LANES), F32),
         ),
     )

time: 77 us -> 76.8 us (level)
  no operation moved by 1% of the time
where the time goes in v6:
time: 76.8 us; the launch traced here: 75.5 us
  starting transfers between devices  33.9 us (44%)
  blocking collectives  18.5 us (24%)
  Pallas kernels  11.9 us (15%)
  waiting for transfers between devices  10.2 us (13%)
  local copies, waits for them, and re-layouts  0.79 us (1%)
    ppermute x14, starting transfers between devices, turned(): lax.ppermute(block, axis, [(i, (i + distance) % count) for i in range(cou...  26.6 us
    all_to_all x1, blocking collectives, on_device(): parts = lax.all_to_all(cut, ('z', 'x'), 0, 0, tiled=True)  18.5 us
    pallas_call x7, Pallas kernels, call(): pl.pallas_call(kernel, out_shape=out_shape, in_specs=specs, out_specs=jax...  11.7 us
    ppermute x14, waiting for transfers between devices, turned(): lax.ppermute(block, axis, [(i, (i + distance) % count) for i in range(cou...  10.2 us
    all_to_all x1, starting transfers between devices, on_device(): slices = lax.all_to_all(slices, 'z', 0, 0, tiled=True)  7.28 us
  transfers between devices with their start and end apart: 15, of which 7 were waited for; matrix products, arithmetic and copies ran while one was open for 0% of the time, Pallas kernels for 5%

profile of v6, /device:TPU:1, one launch (start us, length us, event | category | flops | bytes accessed | tf_op | source)
XLA Modules:
  0.0 75.5 jit_solution(13158201858855765003)
XLA Ops:
  0.0 2.1 %shard_map.46 = (bf16[16,2048]{1,0:T(8,128)(2,1)S(1)}, bf16[16,2048]{1,0:T(8,128)(2,1)S(1)}, bf16[4,432,128]{2,1,0:T(8,128)(2,1)}) custom-call(bf16[30,16,64]{2,1,0:T(8,128)(2,1)} %bitcast.17, bf16[432,512]{1,0:T(8,128)(2,1)} %bitcast.16), custom_call_target="tpu_custom_call" | custom-call | tf_op jit(solution)/shard_map/pallas_call | solution.py:23
  2.1 2.2 %collective-permute-start.1 = (bf16[16,2048]{1,0:T(8,128)(2,1)S(1)}, bf16[16,2048]{1,0:T(8,128)(2,1)S(1)}, u32[]{:S(2)}, u32[]{:S(2)}) collective-permute-start(bf16[16,2048]{1,0:T(8,128)(2,1)S(1)} %get-tuple-element.16), channel_id=1, source_target_pairs={{0,64},{32,96},{64,128},{96,160},{128,192},{160,224},{192,0},{224,... | collective-permute-start | bytes 196616 | tf_op jit(solution)/shard_map/ppermute | solution.py:267
  4.3 1.6 %collective-permute-start = (bf16[16,2048]{1,0:T(8,128)(2,1)S(1)}, bf16[16,2048]{1,0:T(8,128)(2,1)S(1)}, u32[]{:S(2)}, u32[]{:S(2)}) collective-permute-start(bf16[16,2048]{1,0:T(8,128)(2,1)S(1)} %get-tuple-element.16), channel_id=1, source_target_pairs={{0,32},{32,64},{64,96},{96,128},{128,160},{160,192},{192,224},{224... | collective-permute-start | bytes 196616 | tf_op jit(solution)/shard_map/ppermute | solution.py:267
  5.9 7.3 %all-to-all-start = ((bf16[4,432,128]{2,1,0:T(8,128)(2,1)}), bf16[4,432,128]{2,1,0:T(8,128)(2,1)S(1)}, u32[]{:S(2)}, u32[]{:S(2)}) async-start(bf16[4,432,128]{2,1,0:T(8,128)(2,1)} %get-tuple-element.15), calls=%async_computation | async-start | bytes 884736 | tf_op jit(solution)/shard_map/all_to_all | solution.py:294
  13.3 2.6 %collective-permute-start.7 = (bf16[48,2048]{1,0:T(8,128)(2,1)S(1)}, bf16[48,2048]{1,0:T(8,128)(2,1)S(1)}, u32[]{:S(2)}, u32[]{:S(2)}) collective-permute-start(bf16[48,2048]{1,0:T(8,128)(2,1)S(1)} %constant_dynamic-update-slice_fusion.refs_0_), channel_id=1, source_target_pairs={{0,6},{2,0},{4,2},{6,4},{1,7},{3,1},{5,3},{7,5},{8,14},{10,8},{12,... | collective-permute-start | bytes 589832 | tf_op jit(solution)/shard_map/ppermute | solution.py:267
  17.0 2.4 %collective-permute-start.2 = (bf16[48,2048]{1,0:T(8,128)(2,1)S(1)}, bf16[48,2048]{1,0:T(8,128)(2,1)S(1)}, u32[]{:S(2)}, u32[]{:S(2)}) collective-permute-start(bf16[48,2048]{1,0:T(8,128)(2,1)S(1)} %constant_dynamic-update-slice_fusion.refs_0_), channel_id=1, source_target_pairs={{0,1},{1,0},{2,3},{3,2},{4,5},{5,4},{6,7},{7,6},{8,9},{9,8},{10,11... | collective-permute-start | bytes 589832 | tf_op jit(solution)/shard_map/ppermute | solution.py:267
  19.3 1.1 %collective-permute-done.7.refs_6_ = bf16[48,2048]{1,0:T(8,128)(2,1)S(1)} collective-permute-done((bf16[48,2048]{1,0:T(8,128)(2,1)S(1)}, bf16[48,2048]{1,0:T(8,128)(2,1)S(1)}, u32[]{:S(2)}, u32[]{:S(2)}) %collective-permute-start.7) | collective-permute-done | bytes 196640 | tf_op jit(solution)/shard_map/ppermute | solution.py:267
  20.4 4.8 %collective-permute-start.8 = (bf16[48,2048]{1,0:T(8,128)(2,1)S(1)}, bf16[48,2048]{1,0:T(8,128)(2,1)S(1)}, u32[]{:S(2)}, u32[]{:S(2)}) collective-permute-start(bf16[48,2048]{1,0:T(8,128)(2,1)S(1)} %collective-permute-done.7.refs_6_), channel_id=1, source_target_pairs={{0,1},{1,0},{2,3},{3,2},{4,5},{5,4},{6,7},{7,6},{8,9},{9,8},{10,11... | collective-permute-start | bytes 589832 | tf_op jit(solution)/shard_map/ppermute | solution.py:267
  25.2 1.6 %collective-permute-start.6 = (bf16[48,2048]{1,0:T(8,128)(2,1)S(1)}, bf16[48,2048]{1,0:T(8,128)(2,1)S(1)}, u32[]{:S(2)}, u32[]{:S(2)}) collective-permute-start(bf16[48,2048]{1,0:T(8,128)(2,1)S(1)} %collective-permute-done.5.refs_4_), channel_id=1, source_target_pairs={{0,1},{1,0},{2,3},{3,2},{4,5},{5,4},{6,7},{7,6},{8,9},{9,8},{10,11... | collective-permute-start | bytes 589832 | tf_op jit(solution)/shard_map/ppermute | solution.py:267
  26.8 1.1 %collective-permute-done.3.refs_2_ = bf16[48,2048]{1,0:T(8,128)(2,1)S(1)} collective-permute-done((bf16[48,2048]{1,0:T(8,128)(2,1)S(1)}, bf16[48,2048]{1,0:T(8,128)(2,1)S(1)}, u32[]{:S(2)}, u32[]{:S(2)}) %collective-permute-start.3) | collective-permute-done | bytes 196640 | tf_op jit(solution)/shard_map/ppermute | solution.py:267
  29.0 1.0 %collective-permute-done.4.refs_3_ = bf16[48,2048]{1,0:T(8,128)(2,1)S(1)} collective-permute-done((bf16[48,2048]{1,0:T(8,128)(2,1)S(1)}, bf16[48,2048]{1,0:T(8,128)(2,1)S(1)}, u32[]{:S(2)}, u32[]{:S(2)}) %collective-permute-start.4) | collective-permute-done | bytes 196640 | tf_op jit(solution)/shard_map/ppermute | solution.py:267
  29.9 2.4 %shard_map.47 = bf16[16,96,128]{2,1,0:T(8,128)(2,1)S(1)} custom-call(s32[6]{0:T(128)S(1)} %stack.23.at_ref, bf16[16,2048]{1,0:T(8,128)(2,1)S(1)} %get-tuple-element.14.field_ref, bf16[4,432,128]{2,1,0:T(8,128)(2,1)S(1)} %all-to-all-done.slices_ref, bf16[48,2048]{1,0:T(8,128)(2,1)S(1)} %constant_dynamic-update-slice_fusion.refs_0_, ...), custom_call_target="tpu_custom_call" | custom-call | tf_op jit(solution)/shard_map/pallas_call | solution.py:23
  32.3 18.5 %all_to_all.10.parts_ref = bf16[16,96,128]{2,1,0:T(8,128)(2,1)S(1)} all-to-all(bf16[16,96,128]{2,1,0:T(8,128)(2,1)S(1)} %shard_map.47), channel_id=1, replica_groups=mesh['tm'=8,'z'=4,'x'=4,'c'=2] {'z','x'}, dimensions={0} | all-to-all | bytes 786432 | tf_op jit(solution)/shard_map/all_to_all | solution.py:309
  51.1 1.4 %collective-permute-start.10 = (bf16[192,256]{1,0:T(8,128)(2,1)S(1)}, bf16[192,256]{1,0:T(8,128)(2,1)S(1)}, u32[]{:S(2)}, u32[]{:S(2)}) collective-permute-start(bf16[192,256]{1,0:T(8,128)(2,1)S(1)} %shard_map.48.tie_ref.own_ref), channel_id=1, source_target_pairs={{0,64},{32,96},{64,128},{96,160},{128,192},{160,224},{192,0},{224,... | collective-permute-start | bytes 294920 | tf_op jit(solution)/shard_map/ppermute | solution.py:267
  52.5 5.0 %collective-permute-start.9 = (bf16[192,256]{1,0:T(8,128)(2,1)S(1)}, bf16[192,256]{1,0:T(8,128)(2,1)S(1)}, u32[]{:S(2)}, u32[]{:S(2)}) collective-permute-start(bf16[192,256]{1,0:T(8,128)(2,1)S(1)} %shard_map.48.tie_ref.own_ref), channel_id=1, source_target_pairs={{0,32},{32,64},{64,96},{96,128},{128,160},{160,192},{192,224},{224... | collective-permute-start | bytes 294920 | tf_op jit(solution)/shard_map/ppermute | solution.py:267
  57.5 2.7 %shard_map.49.wide_ref = bf16[9,3,16,16,256]{4,3,2,1,0:T(8,128)(2,1)S(1)} custom-call(s32[6]{0:T(128)S(1)} %stack.23.at_ref, bf16[3,3,3,16,2,16,256]{6,5,4,3,2,1,0:T(8,128)(2,1)} %bitcast.15, bf16[192,256]{1,0:T(8,128)(2,1)S(1)} %shard_map.48.tie_ref.own_ref), custom_call_target="tpu_custom_call" | custom-call | tf_op jit(solution)/shard_map/pallas_call | solution.py:23
  60.6 1.4 %shard_map.50 = (f32[2,192,256]{2,1,0:T(8,128)S(1)}, bf16[2,192,256]{2,1,0:T(8,128)(2,1)S(1)}) custom-call(s32[6]{0:T(128)S(1)} %stack.23.at_ref, bf16[192,256]{1,0:T(8,128)(2,1)S(1)} %shard_map.48.tie_ref.own_ref, bf16[192,256]{1,0:T(8,128)(2,1)S(1)} %collective-permute-done.9.first_ref, bf16[192,256]{1,0:T(8,128)(2,1)S(1)} %collective-permute-done.10.second_ref, ...), custom_call_target="tpu_custom_call" | custom-call | tf_op jit(solution)/shard_map/pallas_call | solution.py:23
  62.1 1.9 %collective-permute-start.11 = (bf16[2,192,256]{2,1,0:T(8,128)(2,1)S(1)}, bf16[2,192,256]{2,1,0:T(8,128)(2,1)S(1)}, u32[]{:S(2)}, u32[]{:S(2)}) collective-permute-start(bf16[2,192,256]{2,1,0:T(8,128)(2,1)S(1)} %get-tuple-element.18), channel_id=1, source_target_pairs={{0,1},{1,0},{2,3},{3,2},{4,5},{5,4},{6,7},{7,6},{8,9},{9,8},{10,11... | collective-permute-start | bytes 589832 | tf_op jit(solution)/shard_map/ppermute | solution.py:267
  64.0 1.1 %collective-permute-done.11.got_ref = bf16[2,192,256]{2,1,0:T(8,128)(2,1)S(1)} collective-permute-done((bf16[2,192,256]{2,1,0:T(8,128)(2,1)S(1)}, bf16[2,192,256]{2,1,0:T(8,128)(2,1)S(1)}, u32[]{:S(2)}, u32[]{:S(2)}) %collective-permute-start.11) | collective-permute-done | bytes 196640 | tf_op jit(solution)/shard_map/ppermute | solution.py:267
  65.0 1.4 %shard_map.51 = (bf16[256,256]{1,0:T(8,128)(2,1)S(1)}, bf16[256,256]{1,0:T(8,128)(2,1)S(1)}, bf16[256,256]{1,0:T(8,128)(2,1)S(1)}, bf16[2,192,256]{2,1,0:T(8,128)(2,1)S(1)}) custom-call(s32[6]{0:T(128)S(1)} %stack.23.at_ref, f32[2,192,256]{2,1,0:T(8,128)S(1)} %get-tuple-element.17.keep_ref, bf16[2,192,256]{2,1,0:T(8,128)(2,1)S(1)} %collective-permute-done.11.got_ref, ...), custom_call_target="tpu_custom_call" | custom-call | tf_op jit(solution)/shard_map/pallas_call | solution.py:23
  66.4 1.1 %collective-permute-start.13 = (bf16[256,256]{1,0:T(8,128)(2,1)S(1)}, bf16[256,256]{1,0:T(8,128)(2,1)S(1)}, u32[]{:S(2)}, u32[]{:S(2)}) collective-permute-start(bf16[256,256]{1,0:T(8,128)(2,1)S(1)} %get-tuple-element.22), channel_id=1, source_target_pairs={{0,64},{32,96},{64,128},{96,160},{128,192},{160,224},{192,0},{224,... | collective-permute-start | bytes 393224 | tf_op jit(solution)/shard_map/ppermute | solution.py:267
  67.5 1.0 %shard_map.52.own_ref = f32[256,256]{1,0:T(8,128)S(1)} custom-call(s32[6]{0:T(128)S(1)} %stack.23.at_ref, bf16[256,256]{1,0:T(8,128)(2,1)S(1)} %get-tuple-element.19.mid_ref, bf16[2,192,256]{2,1,0:T(8,128)(2,1)S(1)} %get-tuple-element.20.act_ref, bf16[3,3,3,256,256]{4,3,2,1,0:T(8,128)(2,1)S(1)} %copy-done, bf16[256,256]{1,0:T(8,128)(2,1)S(1)} %get-tuple-element.21.first_ref), custom_call_target="tpu_custom_call" | custom-call | tf_op jit(solution)/shard_map/pallas_call | solution.py:23
  68.6 4.3 %collective-permute-done.13.second_ref = bf16[256,256]{1,0:T(8,128)(2,1)S(1)} collective-permute-done((bf16[256,256]{1,0:T(8,128)(2,1)S(1)}, bf16[256,256]{1,0:T(8,128)(2,1)S(1)}, u32[]{:S(2)}, u32[]{:S(2)}) %collective-permute-start.13) | collective-permute-done | bytes 131104 | tf_op jit(solution)/shard_map/ppermute | solution.py:267
  72.9 1.3 %collective-permute-done.12.first_ref = bf16[256,256]{1,0:T(8,128)(2,1)S(1)} collective-permute-done((bf16[256,256]{1,0:T(8,128)(2,1)S(1)}, bf16[256,256]{1,0:T(8,128)(2,1)S(1)}, u32[]{:S(2)}, u32[]{:S(2)}) %collective-permute-start.12) | collective-permute-done | bytes 131104 | tf_op jit(solution)/shard_map/ppermute | solution.py:267
  (22 shorter events, 4.1 us)
Async XLA Ops:
  2.1 11.2 %collective-permute-start.1 = (bf16[16,2048]{1,0:T(8,128)(2,1)S(1)}, bf16[16,2048]{1,0:T(8,128)(2,1)S(1)}, u32[]{:S(2)}, u32[]{:S(2)}) collective-permute-start(bf16[16,2048]{1,0:T(8,128)(2,1)S(1)} %get-tuple-element.16), channel_id=1, source_target_pairs={{0,64},{32,96},{64,128},{96,160},{128,192},{160,224},{192,0},{224,... | collective-permute-start | bytes 196616 | tf_op jit(solution)/shard_map/ppermute | solution.py:267
  4.3 8.9 %collective-permute-start = (bf16[16,2048]{1,0:T(8,128)(2,1)S(1)}, bf16[16,2048]{1,0:T(8,128)(2,1)S(1)}, u32[]{:S(2)}, u32[]{:S(2)}) collective-permute-start(bf16[16,2048]{1,0:T(8,128)(2,1)S(1)} %get-tuple-element.16), channel_id=1, source_target_pairs={{0,32},{32,64},{64,96},{96,128},{128,160},{160,192},{192,224},{224... | collective-permute-start | bytes 196616 | tf_op jit(solution)/shard_map/ppermute | solution.py:267
  5.9 24.0 %all-to-all-start = ((bf16[4,432,128]{2,1,0:T(8,128)(2,1)}), bf16[4,432,128]{2,1,0:T(8,128)(2,1)S(1)}, u32[]{:S(2)}, u32[]{:S(2)}) async-start(bf16[4,432,128]{2,1,0:T(8,128)(2,1)} %get-tuple-element.15), calls=%async_computation | async-start | bytes 884736 | tf_op jit(solution)/shard_map/all_to_all | solution.py:294
  13.3 7.1 %collective-permute-start.7 = (bf16[48,2048]{1,0:T(8,128)(2,1)S(1)}, bf16[48,2048]{1,0:T(8,128)(2,1)S(1)}, u32[]{:S(2)}, u32[]{:S(2)}) collective-permute-start(bf16[48,2048]{1,0:T(8,128)(2,1)S(1)} %constant_dynamic-update-slice_fusion.refs_0_), channel_id=1, source_target_pairs={{0,6},{2,0},{4,2},{6,4},{1,7},{3,1},{5,3},{7,5},{8,14},{10,8},{12,... | collective-permute-start | bytes 589832 | tf_op jit(solution)/shard_map/ppermute | solution.py:267
  15.8 9.4 %collective-permute-start.5 = (bf16[48,2048]{1,0:T(8,128)(2,1)S(1)}, bf16[48,2048]{1,0:T(8,128)(2,1)S(1)}, u32[]{:S(2)}, u32[]{:S(2)}) collective-permute-start(bf16[48,2048]{1,0:T(8,128)(2,1)S(1)} %constant_dynamic-update-slice_fusion.refs_0_), channel_id=1, source_target_pairs={{0,4},{2,6},{4,0},{6,2},{1,5},{3,7},{5,1},{7,3},{8,12},{10,14},{12... | collective-permute-start | bytes 589832 | tf_op jit(solution)/shard_map/ppermute | solution.py:267
  16.4 11.6 %collective-permute-start.3 = (bf16[48,2048]{1,0:T(8,128)(2,1)S(1)}, bf16[48,2048]{1,0:T(8,128)(2,1)S(1)}, u32[]{:S(2)}, u32[]{:S(2)}) collective-permute-start(bf16[48,2048]{1,0:T(8,128)(2,1)S(1)} %constant_dynamic-update-slice_fusion.refs_0_), channel_id=1, source_target_pairs={{0,2},{2,4},{4,6},{6,0},{1,3},{3,5},{5,7},{7,1},{8,10},{10,12},{12... | collective-permute-start | bytes 589832 | tf_op jit(solution)/shard_map/ppermute | solution.py:267
  17.0 12.0 %collective-permute-start.2 = (bf16[48,2048]{1,0:T(8,128)(2,1)S(1)}, bf16[48,2048]{1,0:T(8,128)(2,1)S(1)}, u32[]{:S(2)}, u32[]{:S(2)}) collective-permute-start(bf16[48,2048]{1,0:T(8,128)(2,1)S(1)} %constant_dynamic-update-slice_fusion.refs_0_), channel_id=1, source_target_pairs={{0,1},{1,0},{2,3},{3,2},{4,5},{5,4},{6,7},{7,6},{8,9},{9,8},{10,11... | collective-permute-start | bytes 589832 | tf_op jit(solution)/shard_map/ppermute | solution.py:267
  20.4 8.5 %collective-permute-start.8 = (bf16[48,2048]{1,0:T(8,128)(2,1)S(1)}, bf16[48,2048]{1,0:T(8,128)(2,1)S(1)}, u32[]{:S(2)}, u32[]{:S(2)}) collective-permute-start(bf16[48,2048]{1,0:T(8,128)(2,1)S(1)} %collective-permute-done.7.refs_6_), channel_id=1, source_target_pairs={{0,1},{1,0},{2,3},{3,2},{4,5},{5,4},{6,7},{7,6},{8,9},{9,8},{10,11... | collective-permute-start | bytes 589832 | tf_op jit(solution)/shard_map/ppermute | solution.py:267
  25.2 3.8 %collective-permute-start.6 = (bf16[48,2048]{1,0:T(8,128)(2,1)S(1)}, bf16[48,2048]{1,0:T(8,128)(2,1)S(1)}, u32[]{:S(2)}, u32[]{:S(2)}) collective-permute-start(bf16[48,2048]{1,0:T(8,128)(2,1)S(1)} %collective-permute-done.5.refs_4_), channel_id=1, source_target_pairs={{0,1},{1,0},{2,3},{3,2},{4,5},{5,4},{6,7},{7,6},{8,9},{9,8},{10,11... | collective-permute-start | bytes 589832 | tf_op jit(solution)/shard_map/ppermute | solution.py:267
  28.0 2.0 %collective-permute-start.4 = (bf16[48,2048]{1,0:T(8,128)(2,1)S(1)}, bf16[48,2048]{1,0:T(8,128)(2,1)S(1)}, u32[]{:S(2)}, u32[]{:S(2)}) collective-permute-start(bf16[48,2048]{1,0:T(8,128)(2,1)S(1)} %collective-permute-done.3.refs_2_), channel_id=1, source_target_pairs={{0,1},{1,0},{2,3},{3,2},{4,5},{5,4},{6,7},{7,6},{8,9},{9,8},{10,11... | collective-permute-start | bytes 589832 | tf_op jit(solution)/shard_map/ppermute | solution.py:267
  51.1 9.2 %collective-permute-start.10 = (bf16[192,256]{1,0:T(8,128)(2,1)S(1)}, bf16[192,256]{1,0:T(8,128)(2,1)S(1)}, u32[]{:S(2)}, u32[]{:S(2)}) collective-permute-start(bf16[192,256]{1,0:T(8,128)(2,1)S(1)} %shard_map.48.tie_ref.own_ref), channel_id=1, source_target_pairs={{0,64},{32,96},{64,128},{96,160},{128,192},{160,224},{192,0},{224,... | collective-permute-start | bytes 294920 | tf_op jit(solution)/shard_map/ppermute | solution.py:267
  52.5 8.2 %collective-permute-start.9 = (bf16[192,256]{1,0:T(8,128)(2,1)S(1)}, bf16[192,256]{1,0:T(8,128)(2,1)S(1)}, u32[]{:S(2)}, u32[]{:S(2)}) collective-permute-start(bf16[192,256]{1,0:T(8,128)(2,1)S(1)} %shard_map.48.tie_ref.own_ref), channel_id=1, source_target_pairs={{0,32},{32,64},{64,96},{96,128},{128,160},{160,192},{192,224},{224... | collective-permute-start | bytes 294920 | tf_op jit(solution)/shard_map/ppermute | solution.py:267
  60.3 4.8 %copy-start = (bf16[3,3,3,256,256]{4,3,2,1,0:T(8,128)(2,1)S(1)}, bf16[3,3,3,256,256]{4,3,2,1,0:T(8,128)(2,1)}, u32[]{:S(2)}) copy-start(bf16[3,3,3,256,256]{4,3,2,1,0:T(8,128)(2,1)} %last_ref.3) | copy-start | bytes 10616836
  62.1 2.9 %collective-permute-start.11 = (bf16[2,192,256]{2,1,0:T(8,128)(2,1)S(1)}, bf16[2,192,256]{2,1,0:T(8,128)(2,1)S(1)}, u32[]{:S(2)}, u32[]{:S(2)}) collective-permute-start(bf16[2,192,256]{2,1,0:T(8,128)(2,1)S(1)} %get-tuple-element.18), channel_id=1, source_target_pairs={{0,1},{1,0},{2,3},{3,2},{4,5},{5,4},{6,7},{7,6},{8,9},{9,8},{10,11... | collective-permute-start | bytes 589832 | tf_op jit(solution)/shard_map/ppermute | solution.py:267
  66.4 6.4 %collective-permute-start.13 = (bf16[256,256]{1,0:T(8,128)(2,1)S(1)}, bf16[256,256]{1,0:T(8,128)(2,1)S(1)}, u32[]{:S(2)}, u32[]{:S(2)}) collective-permute-start(bf16[256,256]{1,0:T(8,128)(2,1)S(1)} %get-tuple-element.22), channel_id=1, source_target_pairs={{0,64},{32,96},{64,128},{96,160},{128,192},{160,224},{192,0},{224,... | collective-permute-start | bytes 393224 | tf_op jit(solution)/shard_map/ppermute | solution.py:267
  67.5 6.6 %collective-permute-start.12 = (bf16[256,256]{1,0:T(8,128)(2,1)S(1)}, bf16[256,256]{1,0:T(8,128)(2,1)S(1)}, u32[]{:S(2)}, u32[]{:S(2)}) collective-permute-start(bf16[256,256]{1,0:T(8,128)(2,1)S(1)} %get-tuple-element.21.first_ref), channel_id=1, source_target_pairs={{0,32},{32,64},{64,96},{96,128},{128,160},{160,192},{192,224},{224... | collective-permute-start | bytes 393224 | tf_op jit(solution)/shard_map/ppermute | solution.py:267

commit v7 on v6

--- a/solution.py
+++ b/solution.py
@@ -12,16 +12,23 @@
 QUARTERS = 4
 BF16 = jnp.bfloat16
 F32 = jnp.float32
-SMEM = pl.BlockSpec(memory_space=pltpu.SMEM)
 HBM = pl.BlockSpec(memory_space=pltpu.HBM)
 VMEM = pl.BlockSpec(memory_space=pltpu.VMEM)
 LIMIT = 20 * 2**20
 
 
+def where_and(kernel, *refs):
+    place = [lax.axis_index(a) for a in ("z", "x", "c", "tm")]
+    z, x, c = place[:3]
+    count = [lax.axis_size(a) for a in ("z", "x", "c")]
+    strip = (z * count[1] + x) * count[2] + c
+    kernel([*place, strip, count[0] * count[1] * count[2]], *refs)
+
+
 def call(kernel, out_shape, operands, scratch=(), specs=None):
-    specs = specs or [SMEM] + [VMEM] * (len(operands) - 1)
+    specs = specs or [VMEM] * len(operands)
     return pl.pallas_call(
-        kernel,
+        functools.partial(where_and, kernel),
         out_shape=out_shape,
         in_specs=specs,
         out_specs=jax.tree.map(lambda _: VMEM, out_shape),
@@ -48,7 +55,7 @@
     return jnp.where(lane < LANES - PITCH, pltpu.roll(block, LANES - PITCH, 1), 0.0)
 
 
-def pack_kernel(field_ref, weight_ref, packed_ref, act_ref, slices_ref, raw_ref, columns_ref, rows_ref, sems):
+def pack_kernel(place, field_ref, weight_ref, packed_ref, act_ref, slices_ref, raw_ref, columns_ref, rows_ref, sems):
     across, shard, height = field_ref.shape
     deep = height // QUARTERS
     load = pltpu.make_async_copy(field_ref, raw_ref, sems.at[4])
@@ -74,13 +81,13 @@
         copy.wait()
 
 
-def coarse_kernel(at_ref, field_ref, slices_ref, *refs):
+def coarse_kernel(place, field_ref, slices_ref, *refs):
     blocks, (out_ref, all_ref, taps_ref, sum_ref) = refs[:8], refs[8:]
     shard, cells = field_ref.shape
     deep = cells // LANES
     group = 8 * shard
     wide = 4 * shard
-    z, x, c, t = at_ref[0], at_ref[1], at_ref[2], at_ref[3]
+    z, x, c, t = place[0], place[1], place[2], place[3]
     for n, block in enumerate(blocks):
         x_from = lax.rem(x + 4 - n // 2, 4)
         c_from = c if n % 2 == 0 else 1 - c
@@ -148,8 +155,8 @@
     out_ref[...] = order_ref[...].T[: out_ref.shape[0]].astype(BF16)
 
 
-def stage_kernel(at_ref, weight_ref, tie_ref, out_ref, sems):
-    c = at_ref[2]
+def stage_kernel(place, weight_ref, tie_ref, out_ref, sems):
+    c = place[2]
     copies = []
     for n in range(9):
         copies.append(pltpu.make_async_copy(weight_ref.at[:, n // 3, n % 3, :, c], out_ref.at[n], sems.at[n]))
@@ -166,8 +173,8 @@
     return pltpu.roll(v, v.shape[0] - 1, 0)
 
 
-def wide_kernel(at_ref, own_ref, first_ref, second_ref, wide_ref, keep_ref, send_ref, frames_ref, sum_ref):
-    c, t = at_ref[2], at_ref[3]
+def wide_kernel(place, own_ref, first_ref, second_ref, wide_ref, keep_ref, send_ref, frames_ref, sum_ref):
+    c, t = place[2], place[3]
     halves = (own_ref, first_ref, second_ref)
     half, width = own_ref.shape[1], keep_ref.shape[2]
 
@@ -220,8 +227,8 @@
     return jnp.concatenate([at_even, at_odd], 0)
 
 
-def fine_kernel(across, at_ref, keep_ref, got_ref, last_ref, first_ref, second_ref, mid_ref, act_ref):
-    t, strip, strips = at_ref[3], at_ref[4], at_ref[5]
+def fine_kernel(across, place, keep_ref, got_ref, last_ref, first_ref, second_ref, mid_ref, act_ref):
+    t, strip, strips = place[3], place[4], place[5]
     mid = (keep_ref[...] + got_ref[...].astype(F32)).astype(BF16)
     shape = mid.shape[1:]
     row = lax.broadcasted_iota(jnp.int32, shape, 0) // PITCH
@@ -236,15 +243,15 @@
     second_ref[...] = sums[0].astype(BF16)
 
 
-def own_kernel(at_ref, mid_ref, act_ref, last_ref, first_ref, own_ref):
+def own_kernel(place, mid_ref, act_ref, last_ref, first_ref, own_ref):
     acts = [act_ref[p] for p in range(2)]
     own = mid_ref[...].astype(F32) + taps_of(2, acts, last_ref)
     late = first_ref[...].astype(F32)
-    own_ref[...] = own + jnp.where(at_ref[3] == 0, late, jnp.zeros(late.shape, F32))
-
-
-def last_kernel(across, at_ref, own_ref, first_ref, second_ref, out_ref, order_ref):
-    t = at_ref[3]
+    own_ref[...] = own + jnp.where(place[3] == 0, late, jnp.zeros(late.shape, F32))
+
+
+def last_kernel(across, place, own_ref, first_ref, second_ref, out_ref, order_ref):
+    t = place[3]
     zero = jnp.zeros(own_ref.shape, F32)
     total = (
         own_ref[...]
@@ -273,9 +280,6 @@
     channels = weight_one.shape[3]
     cells = height * PITCH
     tp = ("z", "x", "c")
-    at = jnp.stack(
-        [lax.axis_index(a) for a in ("z", "x", "c", "tm")] + [lax.axis_index(tp), lax.axis_size(tp)]
-    ).astype(jnp.int32)
     kernel = jnp.transpose(weight_one, (0, 1, 2, 4, 3)).reshape(27 * shard, channels)
     small = jax.ShapeDtypeStruct((shard, cells), BF16)
     field, act_in, slices = call(
@@ -299,7 +303,7 @@
     cut = call(
         coarse_kernel,
         jax.ShapeDtypeStruct((16, 6 * shard, LANES), BF16),
-        (at, field, slices, *blocks),
+        (field, slices, *blocks),
         (
             pltpu.VMEM((3 * channels // 4, cells + 2 * LANES), BF16),
             pltpu.VMEM((12 * shard, 9 * channels // 4), BF16),
@@ -318,32 +322,32 @@
     wide = call(
         stage_kernel,
         jax.ShapeDtypeStruct((9, 3, channels // 2 // shard, shard, width), BF16),
-        (at, pltpu.with_memory_space_constraint(source, pltpu.HBM), own),
+        (pltpu.with_memory_space_constraint(source, pltpu.HBM), own),
         (pltpu.SemaphoreType.DMA((9,)),),
-        [SMEM, HBM, pl.BlockSpec(memory_space=pl.ANY)],
+        [HBM, pl.BlockSpec(memory_space=pl.ANY)],
     )
     rows = 6 * PITCH
     keep, send = call(
         wide_kernel,
         (jax.ShapeDtypeStruct((2, rows, width), F32), jax.ShapeDtypeStruct((2, rows, width), BF16)),
-        (at, own, turned(own, "tm", 1), turned(own, "tm", 2), wide),
+        (own, turned(own, "tm", 1), turned(own, "tm", 2), wide),
         (pltpu.VMEM((rows, 3 * channels // 2), BF16), pltpu.VMEM((2, 10 * PITCH, width), F32)),
     )
     small = jax.ShapeDtypeStruct((8 * PITCH, width), BF16)
     first, second, mid, act = call(
         functools.partial(fine_kernel, across),
         (small, small, small, jax.ShapeDtypeStruct((2, rows, width), BF16)),
-        (at, keep, turned(send, "c", 1), weight_three),
+        (keep, turned(send, "c", 1), weight_three),
     )
     own = call(
         own_kernel,
         jax.ShapeDtypeStruct((8 * PITCH, width), F32),
-        (at, mid, act, weight_three, first),
+        (mid, act, weight_three, first),
     )
     decoded = call(
         functools.partial(last_kernel, across),
         jax.ShapeDtypeStruct((8 * across, width), BF16),
-        (at, own, turned(first, "tm", 1), turned(second, "tm", 2)),
+        (own, turned(first, "tm", 1), turned(second, "tm", 2)),
         (pltpu.VMEM((2, 8 * PITCH, 128), F32),),
     )
     return jnp.transpose(decoded.reshape(2 * across, 4, width), (1, 0, 2))[None]

time: 76.8 us -> 74.5 us (0.970)
  Pallas kernels: 11.9 us -> 8.47 us
  waiting for transfers between devices: 10.2 us -> 11.4 us
    pallas_call x7, Pallas kernels: 11.7 us -> 8.28 us  [call(): pl.pallas_call(functools.partial(where_and, kernel), out_shape=out_shape,...]
    ppermute x14, waiting for transfers between devices: 10.2 us -> 11.4 us  [turned(): lax.ppermute(block, axis, [(i, (i + distance) % count) for i in range(cou...]
  transfers between devices with their start and end apart: 15 -> 15, of which waited for: 7 -> 7; matrix products, arithmetic and copies ran while one was open for 0% -> 0% of each run, Pallas kernels for 5% -> 4%
where the time goes in v7:
time: 74.5 us; the launch traced here: 73.1 us
  starting transfers between devices  33.9 us (46%)
  blocking collectives  18.5 us (25%)
  waiting for transfers between devices  11.4 us (15%)
  Pallas kernels  8.47 us (11%)
    ppermute x14, starting transfers between devices, turned(): lax.ppermute(block, axis, [(i, (i + distance) % count) for i in range(cou...  26.6 us
    all_to_all x1, blocking collectives, on_device(): parts = lax.all_to_all(cut, ('z', 'x'), 0, 0, tiled=True)  18.5 us
    ppermute x14, waiting for transfers between devices, turned(): lax.ppermute(block, axis, [(i, (i + distance) % count) for i in range(cou...  11.4 us
    pallas_call x7, Pallas kernels, call(): pl.pallas_call(functools.partial(where_and, kernel), out_shape=out_shape,...  8.28 us
    all_to_all x1, starting transfers between devices, on_device(): slices = lax.all_to_all(slices, 'z', 0, 0, tiled=True)  7.28 us
  transfers between devices with their start and end apart: 15, of which 7 were waited for; matrix products, arithmetic and copies ran while one was open for 0% of the time, Pallas kernels for 4%

profile of v7, /device:TPU:1, one launch (start us, length us, event | category | flops | bytes accessed | tf_op | source)
XLA Modules:
  0.0 73.1 jit_solution(11900328393874036302)
XLA Ops:
  0.0 2.1 %shard_map.46 = (bf16[16,2048]{1,0:T(8,128)(2,1)S(1)}, bf16[16,2048]{1,0:T(8,128)(2,1)S(1)}, bf16[4,432,128]{2,1,0:T(8,128)(2,1)}) custom-call(bf16[30,16,64]{2,1,0:T(8,128)(2,1)} %bitcast.12, bf16[432,512]{1,0:T(8,128)(2,1)} %bitcast.11), custom_call_target="tpu_custom_call" | custom-call | tf_op jit(solution)/shard_map/pallas_call | solution.py:30
  2.1 2.2 %collective-permute-start.1 = (bf16[16,2048]{1,0:T(8,128)(2,1)S(1)}, bf16[16,2048]{1,0:T(8,128)(2,1)S(1)}, u32[]{:S(2)}, u32[]{:S(2)}) collective-permute-start(bf16[16,2048]{1,0:T(8,128)(2,1)S(1)} %get-tuple-element.16), channel_id=1, source_target_pairs={{0,64},{32,96},{64,128},{96,160},{128,192},{160,224},{192,0},{224,... | collective-permute-start | bytes 196616 | tf_op jit(solution)/shard_map/ppermute | solution.py:274
  4.3 1.6 %collective-permute-start = (bf16[16,2048]{1,0:T(8,128)(2,1)S(1)}, bf16[16,2048]{1,0:T(8,128)(2,1)S(1)}, u32[]{:S(2)}, u32[]{:S(2)}) collective-permute-start(bf16[16,2048]{1,0:T(8,128)(2,1)S(1)} %get-tuple-element.16), channel_id=1, source_target_pairs={{0,32},{32,64},{64,96},{96,128},{128,160},{160,192},{192,224},{224... | collective-permute-start | bytes 196616 | tf_op jit(solution)/shard_map/ppermute | solution.py:274
  5.9 7.3 %all-to-all-start = ((bf16[4,432,128]{2,1,0:T(8,128)(2,1)}), bf16[4,432,128]{2,1,0:T(8,128)(2,1)S(1)}, u32[]{:S(2)}, u32[]{:S(2)}) async-start(bf16[4,432,128]{2,1,0:T(8,128)(2,1)} %get-tuple-element.15), calls=%async_computation | async-start | bytes 884736 | tf_op jit(solution)/shard_map/all_to_all | solution.py:298
  13.3 2.6 %collective-permute-start.7 = (bf16[48,2048]{1,0:T(8,128)(2,1)S(1)}, bf16[48,2048]{1,0:T(8,128)(2,1)S(1)}, u32[]{:S(2)}, u32[]{:S(2)}) collective-permute-start(bf16[48,2048]{1,0:T(8,128)(2,1)S(1)} %constant_dynamic-update-slice_fusion.refs_2_), channel_id=1, source_target_pairs={{0,6},{2,0},{4,2},{6,4},{1,7},{3,1},{5,3},{7,5},{8,14},{10,8},{12,... | collective-permute-start | bytes 589832 | tf_op jit(solution)/shard_map/ppermute | solution.py:274
  17.0 2.4 %collective-permute-start.2 = (bf16[48,2048]{1,0:T(8,128)(2,1)S(1)}, bf16[48,2048]{1,0:T(8,128)(2,1)S(1)}, u32[]{:S(2)}, u32[]{:S(2)}) collective-permute-start(bf16[48,2048]{1,0:T(8,128)(2,1)S(1)} %constant_dynamic-update-slice_fusion.refs_2_), channel_id=1, source_target_pairs={{0,1},{1,0},{2,3},{3,2},{4,5},{5,4},{6,7},{7,6},{8,9},{9,8},{10,11... | collective-permute-start | bytes 589832 | tf_op jit(solution)/shard_map/ppermute | solution.py:274
  19.3 1.1 %collective-permute-done.7.refs_8_ = bf16[48,2048]{1,0:T(8,128)(2,1)S(1)} collective-permute-done((bf16[48,2048]{1,0:T(8,128)(2,1)S(1)}, bf16[48,2048]{1,0:T(8,128)(2,1)S(1)}, u32[]{:S(2)}, u32[]{:S(2)}) %collective-permute-start.7) | collective-permute-done | bytes 196640 | tf_op jit(solution)/shard_map/ppermute | solution.py:274
  20.4 4.8 %collective-permute-start.8 = (bf16[48,2048]{1,0:T(8,128)(2,1)S(1)}, bf16[48,2048]{1,0:T(8,128)(2,1)S(1)}, u32[]{:S(2)}, u32[]{:S(2)}) collective-permute-start(bf16[48,2048]{1,0:T(8,128)(2,1)S(1)} %collective-permute-done.7.refs_8_), channel_id=1, source_target_pairs={{0,1},{1,0},{2,3},{3,2},{4,5},{5,4},{6,7},{7,6},{8,9},{9,8},{10,11... | collective-permute-start | bytes 589832 | tf_op jit(solution)/shard_map/ppermute | solution.py:274
  25.2 1.6 %collective-permute-start.6 = (bf16[48,2048]{1,0:T(8,128)(2,1)S(1)}, bf16[48,2048]{1,0:T(8,128)(2,1)S(1)}, u32[]{:S(2)}, u32[]{:S(2)}) collective-permute-start(bf16[48,2048]{1,0:T(8,128)(2,1)S(1)} %collective-permute-done.5.refs_6_), channel_id=1, source_target_pairs={{0,1},{1,0},{2,3},{3,2},{4,5},{5,4},{6,7},{7,6},{8,9},{9,8},{10,11... | collective-permute-start | bytes 589832 | tf_op jit(solution)/shard_map/ppermute | solution.py:274
  26.8 1.1 %collective-permute-done.3.refs_4_ = bf16[48,2048]{1,0:T(8,128)(2,1)S(1)} collective-permute-done((bf16[48,2048]{1,0:T(8,128)(2,1)S(1)}, bf16[48,2048]{1,0:T(8,128)(2,1)S(1)}, u32[]{:S(2)}, u32[]{:S(2)}) %collective-permute-start.3) | collective-permute-done | bytes 196640 | tf_op jit(solution)/shard_map/ppermute | solution.py:274
  28.0 0.9 %collective-permute-start.4 = (bf16[48,2048]{1,0:T(8,128)(2,1)S(1)}, bf16[48,2048]{1,0:T(8,128)(2,1)S(1)}, u32[]{:S(2)}, u32[]{:S(2)}) collective-permute-start(bf16[48,2048]{1,0:T(8,128)(2,1)S(1)} %collective-permute-done.3.refs_4_), channel_id=1, source_target_pairs={{0,1},{1,0},{2,3},{3,2},{4,5},{5,4},{6,7},{7,6},{8,9},{9,8},{10,11... | collective-permute-start | bytes 589832 | tf_op jit(solution)/shard_map/ppermute | solution.py:274
  28.9 1.1 %collective-permute-done.4.refs_5_ = bf16[48,2048]{1,0:T(8,128)(2,1)S(1)} collective-permute-done((bf16[48,2048]{1,0:T(8,128)(2,1)S(1)}, bf16[48,2048]{1,0:T(8,128)(2,1)S(1)}, u32[]{:S(2)}, u32[]{:S(2)}) %collective-permute-start.4) | collective-permute-done | bytes 196640 | tf_op jit(solution)/shard_map/ppermute | solution.py:274
  29.9 1.6 %shard_map.47 = bf16[16,96,128]{2,1,0:T(8,128)(2,1)S(1)} custom-call(bf16[16,2048]{1,0:T(8,128)(2,1)S(1)} %get-tuple-element.14.refs_0_, bf16[4,432,128]{2,1,0:T(8,128)(2,1)S(1)} %all-to-all-done.refs_1_, bf16[48,2048]{1,0:T(8,128)(2,1)S(1)} %constant_dynamic-update-slice_fusion.refs_2_, bf16[48,2048]{1,0:T(8,128)(2,1)S(1)} %collective-permute-done.2.refs_3_, ...), custom_call_target="tpu_custom_call" | custom-call | tf_op jit(solution)/shard_map/pallas_call | solution.py:30
  31.5 18.5 %all_to_all.10.parts_ref = bf16[16,96,128]{2,1,0:T(8,128)(2,1)S(1)} all-to-all(bf16[16,96,128]{2,1,0:T(8,128)(2,1)S(1)} %shard_map.47), channel_id=1, replica_groups=mesh['tm'=8,'z'=4,'x'=4,'c'=2] {'z','x'}, dimensions={0} | all-to-all | bytes 786432 | tf_op jit(solution)/shard_map/all_to_all | solution.py:313
  50.3 1.4 %collective-permute-start.10 = (bf16[192,256]{1,0:T(8,128)(2,1)S(1)}, bf16[192,256]{1,0:T(8,128)(2,1)S(1)}, u32[]{:S(2)}, u32[]{:S(2)}) collective-permute-start(bf16[192,256]{1,0:T(8,128)(2,1)S(1)} %shard_map.48.refs_1_.refs_0_), channel_id=1, source_target_pairs={{0,64},{32,96},{64,128},{96,160},{128,192},{160,224},{192,0},{224,... | collective-permute-start | bytes 294920 | tf_op jit(solution)/shard_map/ppermute | solution.py:274
  51.7 5.0 %collective-permute-start.9 = (bf16[192,256]{1,0:T(8,128)(2,1)S(1)}, bf16[192,256]{1,0:T(8,128)(2,1)S(1)}, u32[]{:S(2)}, u32[]{:S(2)}) collective-permute-start(bf16[192,256]{1,0:T(8,128)(2,1)S(1)} %shard_map.48.refs_1_.refs_0_), channel_id=1, source_target_pairs={{0,32},{32,64},{64,96},{96,128},{128,160},{160,192},{192,224},{224... | collective-permute-start | bytes 294920 | tf_op jit(solution)/shard_map/ppermute | solution.py:274
  56.7 2.2 %shard_map.49.refs_3_ = bf16[9,3,16,16,256]{4,3,2,1,0:T(8,128)(2,1)S(1)} custom-call(bf16[3,3,3,16,2,16,256]{6,5,4,3,2,1,0:T(8,128)(2,1)} %bitcast.10, bf16[192,256]{1,0:T(8,128)(2,1)S(1)} %shard_map.48.refs_1_.refs_0_), custom_call_target="tpu_custom_call" | custom-call | tf_op jit(solution)/shard_map/pallas_call | solution.py:30
  58.9 0.9 %collective-permute-done.9.refs_1_ = bf16[192,256]{1,0:T(8,128)(2,1)S(1)} collective-permute-done((bf16[192,256]{1,0:T(8,128)(2,1)S(1)}, bf16[192,256]{1,0:T(8,128)(2,1)S(1)}, u32[]{:S(2)}, u32[]{:S(2)}) %collective-permute-start.9) | collective-permute-done | bytes 98336 | tf_op jit(solution)/shard_map/ppermute | solution.py:274
  59.8 1.0 %shard_map.50 = (f32[2,192,256]{2,1,0:T(8,128)S(1)}, bf16[2,192,256]{2,1,0:T(8,128)(2,1)S(1)}) custom-call(bf16[192,256]{1,0:T(8,128)(2,1)S(1)} %shard_map.48.refs_1_.refs_0_, bf16[192,256]{1,0:T(8,128)(2,1)S(1)} %collective-permute-done.9.refs_1_, bf16[192,256]{1,0:T(8,128)(2,1)S(1)} %collective-permute-done.10.refs_2_, ...), custom_call_target="tpu_custom_call" | custom-call | tf_op jit(solution)/shard_map/pallas_call | solution.py:30
  60.8 1.9 %collective-permute-start.11 = (bf16[2,192,256]{2,1,0:T(8,128)(2,1)S(1)}, bf16[2,192,256]{2,1,0:T(8,128)(2,1)S(1)}, u32[]{:S(2)}, u32[]{:S(2)}) collective-permute-start(bf16[2,192,256]{2,1,0:T(8,128)(2,1)S(1)} %get-tuple-element.18), channel_id=1, source_target_pairs={{0,1},{1,0},{2,3},{3,2},{4,5},{5,4},{6,7},{7,6},{8,9},{9,8},{10,11... | collective-permute-start | bytes 589832 | tf_op jit(solution)/shard_map/ppermute | solution.py:274
  62.7 1.1 %collective-permute-done.11.refs_1_ = bf16[2,192,256]{2,1,0:T(8,128)(2,1)S(1)} collective-permute-done((bf16[2,192,256]{2,1,0:T(8,128)(2,1)S(1)}, bf16[2,192,256]{2,1,0:T(8,128)(2,1)S(1)}, u32[]{:S(2)}, u32[]{:S(2)}) %collective-permute-start.11) | collective-permute-done | bytes 196640 | tf_op jit(solution)/shard_map/ppermute | solution.py:274
  64.6 1.1 %collective-permute-start.13 = (bf16[256,256]{1,0:T(8,128)(2,1)S(1)}, bf16[256,256]{1,0:T(8,128)(2,1)S(1)}, u32[]{:S(2)}, u32[]{:S(2)}) collective-permute-start(bf16[256,256]{1,0:T(8,128)(2,1)S(1)} %get-tuple-element.22), channel_id=1, source_target_pairs={{0,64},{32,96},{64,128},{96,160},{128,192},{160,224},{192,0},{224,... | collective-permute-start | bytes 393224 | tf_op jit(solution)/shard_map/ppermute | solution.py:274
  66.2 4.8 %collective-permute-done.13.refs_2_ = bf16[256,256]{1,0:T(8,128)(2,1)S(1)} collective-permute-done((bf16[256,256]{1,0:T(8,128)(2,1)S(1)}, bf16[256,256]{1,0:T(8,128)(2,1)S(1)}, u32[]{:S(2)}, u32[]{:S(2)}) %collective-permute-start.13) | collective-permute-done | bytes 131104 | tf_op jit(solution)/shard_map/ppermute | solution.py:274
  71.0 1.3 %collective-permute-done.12.refs_1_ = bf16[256,256]{1,0:T(8,128)(2,1)S(1)} collective-permute-done((bf16[256,256]{1,0:T(8,128)(2,1)S(1)}, bf16[256,256]{1,0:T(8,128)(2,1)S(1)}, u32[]{:S(2)}, u32[]{:S(2)}) %collective-permute-start.12) | collective-permute-done | bytes 131104 | tf_op jit(solution)/shard_map/ppermute | solution.py:274
  (21 shorter events, 3.5 us)
Async XLA Ops:
  2.1 11.2 %collective-permute-start.1 = (bf16[16,2048]{1,0:T(8,128)(2,1)S(1)}, bf16[16,2048]{1,0:T(8,128)(2,1)S(1)}, u32[]{:S(2)}, u32[]{:S(2)}) collective-permute-start(bf16[16,2048]{1,0:T(8,128)(2,1)S(1)} %get-tuple-element.16), channel_id=1, source_target_pairs={{0,64},{32,96},{64,128},{96,160},{128,192},{160,224},{192,0},{224,... | collective-permute-start | bytes 196616 | tf_op jit(solution)/shard_map/ppermute | solution.py:274
  4.3 8.9 %collective-permute-start = (bf16[16,2048]{1,0:T(8,128)(2,1)S(1)}, bf16[16,2048]{1,0:T(8,128)(2,1)S(1)}, u32[]{:S(2)}, u32[]{:S(2)}) collective-permute-start(bf16[16,2048]{1,0:T(8,128)(2,1)S(1)} %get-tuple-element.16), channel_id=1, source_target_pairs={{0,32},{32,64},{64,96},{96,128},{128,160},{160,192},{192,224},{224... | collective-permute-start | bytes 196616 | tf_op jit(solution)/shard_map/ppermute | solution.py:274
  5.9 24.0 %all-to-all-start = ((bf16[4,432,128]{2,1,0:T(8,128)(2,1)}), bf16[4,432,128]{2,1,0:T(8,128)(2,1)S(1)}, u32[]{:S(2)}, u32[]{:S(2)}) async-start(bf16[4,432,128]{2,1,0:T(8,128)(2,1)} %get-tuple-element.15), calls=%async_computation | async-start | bytes 884736 | tf_op jit(solution)/shard_map/all_to_all | solution.py:298
  13.3 7.1 %collective-permute-start.7 = (bf16[48,2048]{1,0:T(8,128)(2,1)S(1)}, bf16[48,2048]{1,0:T(8,128)(2,1)S(1)}, u32[]{:S(2)}, u32[]{:S(2)}) collective-permute-start(bf16[48,2048]{1,0:T(8,128)(2,1)S(1)} %constant_dynamic-update-slice_fusion.refs_2_), channel_id=1, source_target_pairs={{0,6},{2,0},{4,2},{6,4},{1,7},{3,1},{5,3},{7,5},{8,14},{10,8},{12,... | collective-permute-start | bytes 589832 | tf_op jit(solution)/shard_map/ppermute | solution.py:274
  15.8 9.4 %collective-permute-start.5 = (bf16[48,2048]{1,0:T(8,128)(2,1)S(1)}, bf16[48,2048]{1,0:T(8,128)(2,1)S(1)}, u32[]{:S(2)}, u32[]{:S(2)}) collective-permute-start(bf16[48,2048]{1,0:T(8,128)(2,1)S(1)} %constant_dynamic-update-slice_fusion.refs_2_), channel_id=1, source_target_pairs={{0,4},{2,6},{4,0},{6,2},{1,5},{3,7},{5,1},{7,3},{8,12},{10,14},{12... | collective-permute-start | bytes 589832 | tf_op jit(solution)/shard_map/ppermute | solution.py:274
  16.4 11.6 %collective-permute-start.3 = (bf16[48,2048]{1,0:T(8,128)(2,1)S(1)}, bf16[48,2048]{1,0:T(8,128)(2,1)S(1)}, u32[]{:S(2)}, u32[]{:S(2)}) collective-permute-start(bf16[48,2048]{1,0:T(8,128)(2,1)S(1)} %constant_dynamic-update-slice_fusion.refs_2_), channel_id=1, source_target_pairs={{0,2},{2,4},{4,6},{6,0},{1,3},{3,5},{5,7},{7,1},{8,10},{10,12},{12... | collective-permute-start | bytes 589832 | tf_op jit(solution)/shard_map/ppermute | solution.py:274
  17.0 11.9 %collective-permute-start.2 = (bf16[48,2048]{1,0:T(8,128)(2,1)S(1)}, bf16[48,2048]{1,0:T(8,128)(2,1)S(1)}, u32[]{:S(2)}, u32[]{:S(2)}) collective-permute-start(bf16[48,2048]{1,0:T(8,128)(2,1)S(1)} %constant_dynamic-update-slice_fusion.refs_2_), channel_id=1, source_target_pairs={{0,1},{1,0},{2,3},{3,2},{4,5},{5,4},{6,7},{7,6},{8,9},{9,8},{10,11... | collective-permute-start | bytes 589832 | tf_op jit(solution)/shard_map/ppermute | solution.py:274
  20.4 8.5 %collective-permute-start.8 = (bf16[48,2048]{1,0:T(8,128)(2,1)S(1)}, bf16[48,2048]{1,0:T(8,128)(2,1)S(1)}, u32[]{:S(2)}, u32[]{:S(2)}) collective-permute-start(bf16[48,2048]{1,0:T(8,128)(2,1)S(1)} %collective-permute-done.7.refs_8_), channel_id=1, source_target_pairs={{0,1},{1,0},{2,3},{3,2},{4,5},{5,4},{6,7},{7,6},{8,9},{9,8},{10,11... | collective-permute-start | bytes 589832 | tf_op jit(solution)/shard_map/ppermute | solution.py:274
  25.2 3.7 %collective-permute-start.6 = (bf16[48,2048]{1,0:T(8,128)(2,1)S(1)}, bf16[48,2048]{1,0:T(8,128)(2,1)S(1)}, u32[]{:S(2)}, u32[]{:S(2)}) collective-permute-start(bf16[48,2048]{1,0:T(8,128)(2,1)S(1)} %collective-permute-done.5.refs_6_), channel_id=1, source_target_pairs={{0,1},{1,0},{2,3},{3,2},{4,5},{5,4},{6,7},{7,6},{8,9},{9,8},{10,11... | collective-permute-start | bytes 589832 | tf_op jit(solution)/shard_map/ppermute | solution.py:274
  28.0 2.0 %collective-permute-start.4 = (bf16[48,2048]{1,0:T(8,128)(2,1)S(1)}, bf16[48,2048]{1,0:T(8,128)(2,1)S(1)}, u32[]{:S(2)}, u32[]{:S(2)}) collective-permute-start(bf16[48,2048]{1,0:T(8,128)(2,1)S(1)} %collective-permute-done.3.refs_4_), channel_id=1, source_target_pairs={{0,1},{1,0},{2,3},{3,2},{4,5},{5,4},{6,7},{7,6},{8,9},{9,8},{10,11... | collective-permute-start | bytes 589832 | tf_op jit(solution)/shard_map/ppermute | solution.py:274
  50.3 8.6 %collective-permute-start.10 = (bf16[192,256]{1,0:T(8,128)(2,1)S(1)}, bf16[192,256]{1,0:T(8,128)(2,1)S(1)}, u32[]{:S(2)}, u32[]{:S(2)}) collective-permute-start(bf16[192,256]{1,0:T(8,128)(2,1)S(1)} %shard_map.48.refs_1_.refs_0_), channel_id=1, source_target_pairs={{0,64},{32,96},{64,128},{96,160},{128,192},{160,224},{192,0},{224,... | collective-permute-start | bytes 294920 | tf_op jit(solution)/shard_map/ppermute | solution.py:274
  51.7 8.2 %collective-permute-start.9 = (bf16[192,256]{1,0:T(8,128)(2,1)S(1)}, bf16[192,256]{1,0:T(8,128)(2,1)S(1)}, u32[]{:S(2)}, u32[]{:S(2)}) collective-permute-start(bf16[192,256]{1,0:T(8,128)(2,1)S(1)} %shard_map.48.refs_1_.refs_0_), channel_id=1, source_target_pairs={{0,32},{32,64},{64,96},{96,128},{128,160},{160,192},{192,224},{224... | collective-permute-start | bytes 294920 | tf_op jit(solution)/shard_map/ppermute | solution.py:274
  58.9 4.8 %copy-start = (bf16[3,3,3,256,256]{4,3,2,1,0:T(8,128)(2,1)S(1)}, bf16[3,3,3,256,256]{4,3,2,1,0:T(8,128)(2,1)}, u32[]{:S(2)}) copy-start(bf16[3,3,3,256,256]{4,3,2,1,0:T(8,128)(2,1)} %refs_2_.3) | copy-start | bytes 10616836
  60.8 2.9 %collective-permute-start.11 = (bf16[2,192,256]{2,1,0:T(8,128)(2,1)S(1)}, bf16[2,192,256]{2,1,0:T(8,128)(2,1)S(1)}, u32[]{:S(2)}, u32[]{:S(2)}) collective-permute-start(bf16[2,192,256]{2,1,0:T(8,128)(2,1)S(1)} %get-tuple-element.18), channel_id=1, source_target_pairs={{0,1},{1,0},{2,3},{3,2},{4,5},{5,4},{6,7},{7,6},{8,9},{9,8},{10,11... | collective-permute-start | bytes 589832 | tf_op jit(solution)/shard_map/ppermute | solution.py:274
  64.6 6.4 %collective-permute-start.13 = (bf16[256,256]{1,0:T(8,128)(2,1)S(1)}, bf16[256,256]{1,0:T(8,128)(2,1)S(1)}, u32[]{:S(2)}, u32[]{:S(2)}) collective-permute-start(bf16[256,256]{1,0:T(8,128)(2,1)S(1)} %get-tuple-element.22), channel_id=1, source_target_pairs={{0,64},{32,96},{64,128},{96,160},{128,192},{160,224},{192,0},{224,... | collective-permute-start | bytes 393224 | tf_op jit(solution)/shard_map/ppermute | solution.py:274
  65.7 6.6 %collective-permute-start.12 = (bf16[256,256]{1,0:T(8,128)(2,1)S(1)}, bf16[256,256]{1,0:T(8,128)(2,1)S(1)}, u32[]{:S(2)}, u32[]{:S(2)}) collective-permute-start(bf16[256,256]{1,0:T(8,128)(2,1)S(1)} %get-tuple-element.21.refs_3_), channel_id=1, source_target_pairs={{0,32},{32,64},{64,96},{96,128},{128,160},{160,192},{192,224},{224... | collective-permute-start | bytes 393224 | tf_op jit(solution)/shard_map/ppermute | solution.py:274

commit v8 on v7

--- a/solution.py
+++ b/solution.py
@@ -213,15 +213,12 @@
 
 def taps_of(k, acts, last_ref):
     size = 4 * PITCH
+    rows = [slice(i * PITCH, i * PITCH + size) for i in range(3)]
+    both = jnp.concatenate([jnp.concatenate([acts[0][at], acts[1][at]], 0) for at in rows], 1)
     parts = []
     for j in range(3):
-        total = None
-        for i in range(3):
-            rows = slice(i * PITCH, i * PITCH + size)
-            both = jnp.concatenate([acts[0][rows], acts[1][rows]], 0)
-            part = jnp.dot(both, last_ref[k, i, j], preferred_element_type=F32)
-            total = part if total is None else total + part
-        parts.append(total)
+        taps = jnp.concatenate([last_ref[k, i, j] for i in range(3)], 0)
+        parts.append(jnp.dot(both, taps, preferred_element_type=F32))
     at_even = down(parts[0][size:]) + parts[1][:size] + parts[2][size:]
     at_odd = parts[0][:size] + parts[1][size:] + up(parts[2][:size])
     return jnp.concatenate([at_even, at_odd], 0)

time: 74.5 us -> 74.5 us (level)
  no operation moved by 1% of the time
where the time goes in v8:
time: 74.5 us; the launch traced here: 73.1 us
  starting transfers between devices  33.9 us (46%)
  blocking collectives  18.5 us (25%)
  waiting for transfers between devices  11.4 us (15%)
  Pallas kernels  8.48 us (11%)
    ppermute x14, starting transfers between devices, turned(): lax.ppermute(block, axis, [(i, (i + distance) % count) for i in range(cou...  26.6 us
    all_to_all x1, blocking collectives, on_device(): parts = lax.all_to_all(cut, ('z', 'x'), 0, 0, tiled=True)  18.5 us
    ppermute x14, waiting for transfers between devices, turned(): lax.ppermute(block, axis, [(i, (i + distance) % count) for i in range(cou...  11.4 us
    pallas_call x7, Pallas kernels, call(): pl.pallas_call(functools.partial(where_and, kernel), out_shape=out_shape,...  8.29 us
    all_to_all x1, starting transfers between devices, on_device(): slices = lax.all_to_all(slices, 'z', 0, 0, tiled=True)  7.28 us
  transfers between devices with their start and end apart: 15, of which 7 were waited for; matrix products, arithmetic and copies ran while one was open for 0% of the time, Pallas kernels for 4%

profile of v8, /device:TPU:1, one launch (start us, length us, event | category | flops | bytes accessed | tf_op | source)
XLA Modules:
  0.0 73.1 jit_solution(7051389988238613987)
XLA Ops:
  0.0 2.1 %shard_map.46 = (bf16[16,2048]{1,0:T(8,128)(2,1)S(1)}, bf16[16,2048]{1,0:T(8,128)(2,1)S(1)}, bf16[4,432,128]{2,1,0:T(8,128)(2,1)}) custom-call(bf16[30,16,64]{2,1,0:T(8,128)(2,1)} %bitcast.12, bf16[432,512]{1,0:T(8,128)(2,1)} %bitcast.11), custom_call_target="tpu_custom_call" | custom-call | tf_op jit(solution)/shard_map/pallas_call | solution.py:30
  2.1 2.2 %collective-permute-start.1 = (bf16[16,2048]{1,0:T(8,128)(2,1)S(1)}, bf16[16,2048]{1,0:T(8,128)(2,1)S(1)}, u32[]{:S(2)}, u32[]{:S(2)}) collective-permute-start(bf16[16,2048]{1,0:T(8,128)(2,1)S(1)} %get-tuple-element.16), channel_id=1, source_target_pairs={{0,64},{32,96},{64,128},{96,160},{128,192},{160,224},{192,0},{224,... | collective-permute-start | bytes 196616 | tf_op jit(solution)/shard_map/ppermute | solution.py:271
  4.3 1.6 %collective-permute-start = (bf16[16,2048]{1,0:T(8,128)(2,1)S(1)}, bf16[16,2048]{1,0:T(8,128)(2,1)S(1)}, u32[]{:S(2)}, u32[]{:S(2)}) collective-permute-start(bf16[16,2048]{1,0:T(8,128)(2,1)S(1)} %get-tuple-element.16), channel_id=1, source_target_pairs={{0,32},{32,64},{64,96},{96,128},{128,160},{160,192},{192,224},{224... | collective-permute-start | bytes 196616 | tf_op jit(solution)/shard_map/ppermute | solution.py:271
  5.9 7.3 %all-to-all-start = ((bf16[4,432,128]{2,1,0:T(8,128)(2,1)}), bf16[4,432,128]{2,1,0:T(8,128)(2,1)S(1)}, u32[]{:S(2)}, u32[]{:S(2)}) async-start(bf16[4,432,128]{2,1,0:T(8,128)(2,1)} %get-tuple-element.15), calls=%async_computation | async-start | bytes 884736 | tf_op jit(solution)/shard_map/all_to_all | solution.py:295
  13.3 2.6 %collective-permute-start.7 = (bf16[48,2048]{1,0:T(8,128)(2,1)S(1)}, bf16[48,2048]{1,0:T(8,128)(2,1)S(1)}, u32[]{:S(2)}, u32[]{:S(2)}) collective-permute-start(bf16[48,2048]{1,0:T(8,128)(2,1)S(1)} %constant_dynamic-update-slice_fusion.refs_2_), channel_id=1, source_target_pairs={{0,6},{2,0},{4,2},{6,4},{1,7},{3,1},{5,3},{7,5},{8,14},{10,8},{12,... | collective-permute-start | bytes 589832 | tf_op jit(solution)/shard_map/ppermute | solution.py:271
  17.0 2.4 %collective-permute-start.2 = (bf16[48,2048]{1,0:T(8,128)(2,1)S(1)}, bf16[48,2048]{1,0:T(8,128)(2,1)S(1)}, u32[]{:S(2)}, u32[]{:S(2)}) collective-permute-start(bf16[48,2048]{1,0:T(8,128)(2,1)S(1)} %constant_dynamic-update-slice_fusion.refs_2_), channel_id=1, source_target_pairs={{0,1},{1,0},{2,3},{3,2},{4,5},{5,4},{6,7},{7,6},{8,9},{9,8},{10,11... | collective-permute-start | bytes 589832 | tf_op jit(solution)/shard_map/ppermute | solution.py:271
  19.3 1.1 %collective-permute-done.7.refs_8_ = bf16[48,2048]{1,0:T(8,128)(2,1)S(1)} collective-permute-done((bf16[48,2048]{1,0:T(8,128)(2,1)S(1)}, bf16[48,2048]{1,0:T(8,128)(2,1)S(1)}, u32[]{:S(2)}, u32[]{:S(2)}) %collective-permute-start.7) | collective-permute-done | bytes 196640 | tf_op jit(solution)/shard_map/ppermute | solution.py:271
  20.4 4.8 %collective-permute-start.8 = (bf16[48,2048]{1,0:T(8,128)(2,1)S(1)}, bf16[48,2048]{1,0:T(8,128)(2,1)S(1)}, u32[]{:S(2)}, u32[]{:S(2)}) collective-permute-start(bf16[48,2048]{1,0:T(8,128)(2,1)S(1)} %collective-permute-done.7.refs_8_), channel_id=1, source_target_pairs={{0,1},{1,0},{2,3},{3,2},{4,5},{5,4},{6,7},{7,6},{8,9},{9,8},{10,11... | collective-permute-start | bytes 589832 | tf_op jit(solution)/shard_map/ppermute | solution.py:271
  25.2 1.6 %collective-permute-start.6 = (bf16[48,2048]{1,0:T(8,128)(2,1)S(1)}, bf16[48,2048]{1,0:T(8,128)(2,1)S(1)}, u32[]{:S(2)}, u32[]{:S(2)}) collective-permute-start(bf16[48,2048]{1,0:T(8,128)(2,1)S(1)} %collective-permute-done.5.refs_6_), channel_id=1, source_target_pairs={{0,1},{1,0},{2,3},{3,2},{4,5},{5,4},{6,7},{7,6},{8,9},{9,8},{10,11... | collective-permute-start | bytes 589832 | tf_op jit(solution)/shard_map/ppermute | solution.py:271
  26.8 1.1 %collective-permute-done.3.refs_4_ = bf16[48,2048]{1,0:T(8,128)(2,1)S(1)} collective-permute-done((bf16[48,2048]{1,0:T(8,128)(2,1)S(1)}, bf16[48,2048]{1,0:T(8,128)(2,1)S(1)}, u32[]{:S(2)}, u32[]{:S(2)}) %collective-permute-start.3) | collective-permute-done | bytes 196640 | tf_op jit(solution)/shard_map/ppermute | solution.py:271
  28.0 0.9 %collective-permute-start.4 = (bf16[48,2048]{1,0:T(8,128)(2,1)S(1)}, bf16[48,2048]{1,0:T(8,128)(2,1)S(1)}, u32[]{:S(2)}, u32[]{:S(2)}) collective-permute-start(bf16[48,2048]{1,0:T(8,128)(2,1)S(1)} %collective-permute-done.3.refs_4_), channel_id=1, source_target_pairs={{0,1},{1,0},{2,3},{3,2},{4,5},{5,4},{6,7},{7,6},{8,9},{9,8},{10,11... | collective-permute-start | bytes 589832 | tf_op jit(solution)/shard_map/ppermute | solution.py:271
  28.9 1.1 %collective-permute-done.4.refs_5_ = bf16[48,2048]{1,0:T(8,128)(2,1)S(1)} collective-permute-done((bf16[48,2048]{1,0:T(8,128)(2,1)S(1)}, bf16[48,2048]{1,0:T(8,128)(2,1)S(1)}, u32[]{:S(2)}, u32[]{:S(2)}) %collective-permute-start.4) | collective-permute-done | bytes 196640 | tf_op jit(solution)/shard_map/ppermute | solution.py:271
  29.9 1.6 %shard_map.47 = bf16[16,96,128]{2,1,0:T(8,128)(2,1)S(1)} custom-call(bf16[16,2048]{1,0:T(8,128)(2,1)S(1)} %get-tuple-element.14.refs_0_, bf16[4,432,128]{2,1,0:T(8,128)(2,1)S(1)} %all-to-all-done.refs_1_, bf16[48,2048]{1,0:T(8,128)(2,1)S(1)} %constant_dynamic-update-slice_fusion.refs_2_, bf16[48,2048]{1,0:T(8,128)(2,1)S(1)} %collective-permute-done.2.refs_3_, ...), custom_call_target="tpu_custom_call" | custom-call | tf_op jit(solution)/shard_map/pallas_call | solution.py:30
  31.5 18.5 %all_to_all.10.parts_ref = bf16[16,96,128]{2,1,0:T(8,128)(2,1)S(1)} all-to-all(bf16[16,96,128]{2,1,0:T(8,128)(2,1)S(1)} %shard_map.47), channel_id=1, replica_groups=mesh['tm'=8,'z'=4,'x'=4,'c'=2] {'z','x'}, dimensions={0} | all-to-all | bytes 786432 | tf_op jit(solution)/shard_map/all_to_all | solution.py:310
  50.3 1.4 %collective-permute-start.10 = (bf16[192,256]{1,0:T(8,128)(2,1)S(1)}, bf16[192,256]{1,0:T(8,128)(2,1)S(1)}, u32[]{:S(2)}, u32[]{:S(2)}) collective-permute-start(bf16[192,256]{1,0:T(8,128)(2,1)S(1)} %shard_map.48.refs_1_.refs_0_), channel_id=1, source_target_pairs={{0,64},{32,96},{64,128},{96,160},{128,192},{160,224},{192,0},{224,... | collective-permute-start | bytes 294920 | tf_op jit(solution)/shard_map/ppermute | solution.py:271
  51.7 5.0 %collective-permute-start.9 = (bf16[192,256]{1,0:T(8,128)(2,1)S(1)}, bf16[192,256]{1,0:T(8,128)(2,1)S(1)}, u32[]{:S(2)}, u32[]{:S(2)}) collective-permute-start(bf16[192,256]{1,0:T(8,128)(2,1)S(1)} %shard_map.48.refs_1_.refs_0_), channel_id=1, source_target_pairs={{0,32},{32,64},{64,96},{96,128},{128,160},{160,192},{192,224},{224... | collective-permute-start | bytes 294920 | tf_op jit(solution)/shard_map/ppermute | solution.py:271
  56.7 2.2 %shard_map.49.refs_3_ = bf16[9,3,16,16,256]{4,3,2,1,0:T(8,128)(2,1)S(1)} custom-call(bf16[3,3,3,16,2,16,256]{6,5,4,3,2,1,0:T(8,128)(2,1)} %bitcast.10, bf16[192,256]{1,0:T(8,128)(2,1)S(1)} %shard_map.48.refs_1_.refs_0_), custom_call_target="tpu_custom_call" | custom-call | tf_op jit(solution)/shard_map/pallas_call | solution.py:30
  58.9 0.9 %collective-permute-done.9.refs_1_ = bf16[192,256]{1,0:T(8,128)(2,1)S(1)} collective-permute-done((bf16[192,256]{1,0:T(8,128)(2,1)S(1)}, bf16[192,256]{1,0:T(8,128)(2,1)S(1)}, u32[]{:S(2)}, u32[]{:S(2)}) %collective-permute-start.9) | collective-permute-done | bytes 98336 | tf_op jit(solution)/shard_map/ppermute | solution.py:271
  59.8 1.0 %shard_map.50 = (f32[2,192,256]{2,1,0:T(8,128)S(1)}, bf16[2,192,256]{2,1,0:T(8,128)(2,1)S(1)}) custom-call(bf16[192,256]{1,0:T(8,128)(2,1)S(1)} %shard_map.48.refs_1_.refs_0_, bf16[192,256]{1,0:T(8,128)(2,1)S(1)} %collective-permute-done.9.refs_1_, bf16[192,256]{1,0:T(8,128)(2,1)S(1)} %collective-permute-done.10.refs_2_, ...), custom_call_target="tpu_custom_call" | custom-call | tf_op jit(solution)/shard_map/pallas_call | solution.py:30
  60.8 1.9 %collective-permute-start.11 = (bf16[2,192,256]{2,1,0:T(8,128)(2,1)S(1)}, bf16[2,192,256]{2,1,0:T(8,128)(2,1)S(1)}, u32[]{:S(2)}, u32[]{:S(2)}) collective-permute-start(bf16[2,192,256]{2,1,0:T(8,128)(2,1)S(1)} %get-tuple-element.18), channel_id=1, source_target_pairs={{0,1},{1,0},{2,3},{3,2},{4,5},{5,4},{6,7},{7,6},{8,9},{9,8},{10,11... | collective-permute-start | bytes 589832 | tf_op jit(solution)/shard_map/ppermute | solution.py:271
  62.7 1.1 %collective-permute-done.11.refs_1_ = bf16[2,192,256]{2,1,0:T(8,128)(2,1)S(1)} collective-permute-done((bf16[2,192,256]{2,1,0:T(8,128)(2,1)S(1)}, bf16[2,192,256]{2,1,0:T(8,128)(2,1)S(1)}, u32[]{:S(2)}, u32[]{:S(2)}) %collective-permute-start.11) | collective-permute-done | bytes 196640 | tf_op jit(solution)/shard_map/ppermute | solution.py:271
  64.6 1.1 %collective-permute-start.13 = (bf16[256,256]{1,0:T(8,128)(2,1)S(1)}, bf16[256,256]{1,0:T(8,128)(2,1)S(1)}, u32[]{:S(2)}, u32[]{:S(2)}) collective-permute-start(bf16[256,256]{1,0:T(8,128)(2,1)S(1)} %get-tuple-element.22), channel_id=1, source_target_pairs={{0,64},{32,96},{64,128},{96,160},{128,192},{160,224},{192,0},{224,... | collective-permute-start | bytes 393224 | tf_op jit(solution)/shard_map/ppermute | solution.py:271
  66.2 4.8 %collective-permute-done.13.refs_2_ = bf16[256,256]{1,0:T(8,128)(2,1)S(1)} collective-permute-done((bf16[256,256]{1,0:T(8,128)(2,1)S(1)}, bf16[256,256]{1,0:T(8,128)(2,1)S(1)}, u32[]{:S(2)}, u32[]{:S(2)}) %collective-permute-start.13) | collective-permute-done | bytes 131104 | tf_op jit(solution)/shard_map/ppermute | solution.py:271
  71.0 1.3 %collective-permute-done.12.refs_1_ = bf16[256,256]{1,0:T(8,128)(2,1)S(1)} collective-permute-done((bf16[256,256]{1,0:T(8,128)(2,1)S(1)}, bf16[256,256]{1,0:T(8,128)(2,1)S(1)}, u32[]{:S(2)}, u32[]{:S(2)}) %collective-permute-start.12) | collective-permute-done | bytes 131104 | tf_op jit(solution)/shard_map/ppermute | solution.py:271
  (21 shorter events, 3.5 us)
Async XLA Ops:
  2.1 11.2 %collective-permute-start.1 = (bf16[16,2048]{1,0:T(8,128)(2,1)S(1)}, bf16[16,2048]{1,0:T(8,128)(2,1)S(1)}, u32[]{:S(2)}, u32[]{:S(2)}) collective-permute-start(bf16[16,2048]{1,0:T(8,128)(2,1)S(1)} %get-tuple-element.16), channel_id=1, source_target_pairs={{0,64},{32,96},{64,128},{96,160},{128,192},{160,224},{192,0},{224,... | collective-permute-start | bytes 196616 | tf_op jit(solution)/shard_map/ppermute | solution.py:271
  4.3 8.9 %collective-permute-start = (bf16[16,2048]{1,0:T(8,128)(2,1)S(1)}, bf16[16,2048]{1,0:T(8,128)(2,1)S(1)}, u32[]{:S(2)}, u32[]{:S(2)}) collective-permute-start(bf16[16,2048]{1,0:T(8,128)(2,1)S(1)} %get-tuple-element.16), channel_id=1, source_target_pairs={{0,32},{32,64},{64,96},{96,128},{128,160},{160,192},{192,224},{224... | collective-permute-start | bytes 196616 | tf_op jit(solution)/shard_map/ppermute | solution.py:271
  5.9 24.0 %all-to-all-start = ((bf16[4,432,128]{2,1,0:T(8,128)(2,1)}), bf16[4,432,128]{2,1,0:T(8,128)(2,1)S(1)}, u32[]{:S(2)}, u32[]{:S(2)}) async-start(bf16[4,432,128]{2,1,0:T(8,128)(2,1)} %get-tuple-element.15), calls=%async_computation | async-start | bytes 884736 | tf_op jit(solution)/shard_map/all_to_all | solution.py:295
  13.3 7.1 %collective-permute-start.7 = (bf16[48,2048]{1,0:T(8,128)(2,1)S(1)}, bf16[48,2048]{1,0:T(8,128)(2,1)S(1)}, u32[]{:S(2)}, u32[]{:S(2)}) collective-permute-start(bf16[48,2048]{1,0:T(8,128)(2,1)S(1)} %constant_dynamic-update-slice_fusion.refs_2_), channel_id=1, source_target_pairs={{0,6},{2,0},{4,2},{6,4},{1,7},{3,1},{5,3},{7,5},{8,14},{10,8},{12,... | collective-permute-start | bytes 589832 | tf_op jit(solution)/shard_map/ppermute | solution.py:271
  15.8 9.4 %collective-permute-start.5 = (bf16[48,2048]{1,0:T(8,128)(2,1)S(1)}, bf16[48,2048]{1,0:T(8,128)(2,1)S(1)}, u32[]{:S(2)}, u32[]{:S(2)}) collective-permute-start(bf16[48,2048]{1,0:T(8,128)(2,1)S(1)} %constant_dynamic-update-slice_fusion.refs_2_), channel_id=1, source_target_pairs={{0,4},{2,6},{4,0},{6,2},{1,5},{3,7},{5,1},{7,3},{8,12},{10,14},{12... | collective-permute-start | bytes 589832 | tf_op jit(solution)/shard_map/ppermute | solution.py:271
  16.4 11.6 %collective-permute-start.3 = (bf16[48,2048]{1,0:T(8,128)(2,1)S(1)}, bf16[48,2048]{1,0:T(8,128)(2,1)S(1)}, u32[]{:S(2)}, u32[]{:S(2)}) collective-permute-start(bf16[48,2048]{1,0:T(8,128)(2,1)S(1)} %constant_dynamic-update-slice_fusion.refs_2_), channel_id=1, source_target_pairs={{0,2},{2,4},{4,6},{6,0},{1,3},{3,5},{5,7},{7,1},{8,10},{10,12},{12... | collective-permute-start | bytes 589832 | tf_op jit(solution)/shard_map/ppermute | solution.py:271
  17.0 11.9 %collective-permute-start.2 = (bf16[48,2048]{1,0:T(8,128)(2,1)S(1)}, bf16[48,2048]{1,0:T(8,128)(2,1)S(1)}, u32[]{:S(2)}, u32[]{:S(2)}) collective-permute-start(bf16[48,2048]{1,0:T(8,128)(2,1)S(1)} %constant_dynamic-update-slice_fusion.refs_2_), channel_id=1, source_target_pairs={{0,1},{1,0},{2,3},{3,2},{4,5},{5,4},{6,7},{7,6},{8,9},{9,8},{10,11... | collective-permute-start | bytes 589832 | tf_op jit(solution)/shard_map/ppermute | solution.py:271
  20.4 8.5 %collective-permute-start.8 = (bf16[48,2048]{1,0:T(8,128)(2,1)S(1)}, bf16[48,2048]{1,0:T(8,128)(2,1)S(1)}, u32[]{:S(2)}, u32[]{:S(2)}) collective-permute-start(bf16[48,2048]{1,0:T(8,128)(2,1)S(1)} %collective-permute-done.7.refs_8_), channel_id=1, source_target_pairs={{0,1},{1,0},{2,3},{3,2},{4,5},{5,4},{6,7},{7,6},{8,9},{9,8},{10,11... | collective-permute-start | bytes 589832 | tf_op jit(solution)/shard_map/ppermute | solution.py:271
  25.2 3.7 %collective-permute-start.6 = (bf16[48,2048]{1,0:T(8,128)(2,1)S(1)}, bf16[48,2048]{1,0:T(8,128)(2,1)S(1)}, u32[]{:S(2)}, u32[]{:S(2)}) collective-permute-start(bf16[48,2048]{1,0:T(8,128)(2,1)S(1)} %collective-permute-done.5.refs_6_), channel_id=1, source_target_pairs={{0,1},{1,0},{2,3},{3,2},{4,5},{5,4},{6,7},{7,6},{8,9},{9,8},{10,11... | collective-permute-start | bytes 589832 | tf_op jit(solution)/shard_map/ppermute | solution.py:271
  28.0 2.0 %collective-permute-start.4 = (bf16[48,2048]{1,0:T(8,128)(2,1)S(1)}, bf16[48,2048]{1,0:T(8,128)(2,1)S(1)}, u32[]{:S(2)}, u32[]{:S(2)}) collective-permute-start(bf16[48,2048]{1,0:T(8,128)(2,1)S(1)} %collective-permute-done.3.refs_4_), channel_id=1, source_target_pairs={{0,1},{1,0},{2,3},{3,2},{4,5},{5,4},{6,7},{7,6},{8,9},{9,8},{10,11... | collective-permute-start | bytes 589832 | tf_op jit(solution)/shard_map/ppermute | solution.py:271
  50.3 8.6 %collective-permute-start.10 = (bf16[192,256]{1,0:T(8,128)(2,1)S(1)}, bf16[192,256]{1,0:T(8,128)(2,1)S(1)}, u32[]{:S(2)}, u32[]{:S(2)}) collective-permute-start(bf16[192,256]{1,0:T(8,128)(2,1)S(1)} %shard_map.48.refs_1_.refs_0_), channel_id=1, source_target_pairs={{0,64},{32,96},{64,128},{96,160},{128,192},{160,224},{192,0},{224,... | collective-permute-start | bytes 294920 | tf_op jit(solution)/shard_map/ppermute | solution.py:271
  51.7 8.2 %collective-permute-start.9 = (bf16[192,256]{1,0:T(8,128)(2,1)S(1)}, bf16[192,256]{1,0:T(8,128)(2,1)S(1)}, u32[]{:S(2)}, u32[]{:S(2)}) collective-permute-start(bf16[192,256]{1,0:T(8,128)(2,1)S(1)} %shard_map.48.refs_1_.refs_0_), channel_id=1, source_target_pairs={{0,32},{32,64},{64,96},{96,128},{128,160},{160,192},{192,224},{224... | collective-permute-start | bytes 294920 | tf_op jit(solution)/shard_map/ppermute | solution.py:271
  58.9 4.8 %copy-start = (bf16[3,3,3,256,256]{4,3,2,1,0:T(8,128)(2,1)S(1)}, bf16[3,3,3,256,256]{4,3,2,1,0:T(8,128)(2,1)}, u32[]{:S(2)}) copy-start(bf16[3,3,3,256,256]{4,3,2,1,0:T(8,128)(2,1)} %refs_2_.3) | copy-start | bytes 10616836
  60.8 2.9 %collective-permute-start.11 = (bf16[2,192,256]{2,1,0:T(8,128)(2,1)S(1)}, bf16[2,192,256]{2,1,0:T(8,128)(2,1)S(1)}, u32[]{:S(2)}, u32[]{:S(2)}) collective-permute-start(bf16[2,192,256]{2,1,0:T(8,128)(2,1)S(1)} %get-tuple-element.18), channel_id=1, source_target_pairs={{0,1},{1,0},{2,3},{3,2},{4,5},{5,4},{6,7},{7,6},{8,9},{9,8},{10,11... | collective-permute-start | bytes 589832 | tf_op jit(solution)/shard_map/ppermute | solution.py:271
  64.6 6.4 %collective-permute-start.13 = (bf16[256,256]{1,0:T(8,128)(2,1)S(1)}, bf16[256,256]{1,0:T(8,128)(2,1)S(1)}, u32[]{:S(2)}, u32[]{:S(2)}) collective-permute-start(bf16[256,256]{1,0:T(8,128)(2,1)S(1)} %get-tuple-element.22), channel_id=1, source_target_pairs={{0,64},{32,96},{64,128},{96,160},{128,192},{160,224},{192,0},{224,... | collective-permute-start | bytes 393224 | tf_op jit(solution)/shard_map/ppermute | solution.py:271
  65.7 6.6 %collective-permute-start.12 = (bf16[256,256]{1,0:T(8,128)(2,1)S(1)}, bf16[256,256]{1,0:T(8,128)(2,1)S(1)}, u32[]{:S(2)}, u32[]{:S(2)}) collective-permute-start(bf16[256,256]{1,0:T(8,128)(2,1)S(1)} %get-tuple-element.21.refs_3_), channel_id=1, source_target_pairs={{0,32},{32,64},{64,96},{96,128},{128,160},{160,192},{192,224},{224... | collective-permute-start | bytes 393224 | tf_op jit(solution)/shard_map/ppermute | solution.py:271

commit v9 on v8

--- a/solution.py
+++ b/solution.py
@@ -129,11 +129,11 @@
         return jnp.where(to < 2, jnp.where(to < 1, moved[0], moved[1]), jnp.where(to < 3, moved[2], moved[3]))
 
     for m in range(deep // 4):
-        rows = [sum_ref[:, (4 * m + r) * LANES : (4 * m + r + 1) * LANES] for r in range(6)]
+        rows = [sum_ref[:, (4 * m + r) * LANES : (4 * m + r + 1) * LANES].astype(BF16) for r in range(6)]
         rest = [rows[4][:half], rows[5][:half], rows[4][half:], rows[5][half:]]
         for q in range(QUARTERS):
-            out_ref[q * (deep // 4) + m, :wide] = placed(rows[:4], q).astype(BF16)
-            out_ref[q * (deep // 4) + m, wide:] = placed(rest, q).astype(BF16)
+            out_ref[q * (deep // 4) + m, :wide] = placed(rows[:4], q)
+            out_ref[q * (deep // 4) + m, wide:] = placed(rest, q)
 
 
 def strip_kernel(across, parts_ref, out_ref, order_ref):

time: 74.5 us -> 74.5 us (level)
  no operation moved by 1% of the time
where the time goes in v9:
time: 74.5 us; the launch traced here: 73.1 us
  starting transfers between devices  33.9 us (46%)
  blocking collectives  18.5 us (25%)
  waiting for transfers between devices  11.4 us (15%)
  Pallas kernels  8.46 us (11%)
    ppermute x14, starting transfers between devices, turned(): lax.ppermute(block, axis, [(i, (i + distance) % count) for i in range(cou...  26.6 us
    all_to_all x1, blocking collectives, on_device(): parts = lax.all_to_all(cut, ('z', 'x'), 0, 0, tiled=True)  18.5 us
    ppermute x14, waiting for transfers between devices, turned(): lax.ppermute(block, axis, [(i, (i + distance) % count) for i in range(cou...  11.4 us
    pallas_call x7, Pallas kernels, call(): pl.pallas_call(functools.partial(where_and, kernel), out_shape=out_shape,...  8.27 us
    all_to_all x1, starting transfers between devices, on_device(): slices = lax.all_to_all(slices, 'z', 0, 0, tiled=True)  7.28 us
  transfers between devices with their start and end apart: 15, of which 7 were waited for; matrix products, arithmetic and copies ran while one was open for 0% of the time, Pallas kernels for 4%

profile of v9, /device:TPU:1, one launch (start us, length us, event | category | flops | bytes accessed | tf_op | source)
XLA Modules:
  0.0 73.1 jit_solution(15065250735218801234)
XLA Ops:
  0.0 2.1 %shard_map.46 = (bf16[16,2048]{1,0:T(8,128)(2,1)S(1)}, bf16[16,2048]{1,0:T(8,128)(2,1)S(1)}, bf16[4,432,128]{2,1,0:T(8,128)(2,1)}) custom-call(bf16[30,16,64]{2,1,0:T(8,128)(2,1)} %bitcast.12, bf16[432,512]{1,0:T(8,128)(2,1)} %bitcast.11), custom_call_target="tpu_custom_call" | custom-call | tf_op jit(solution)/shard_map/pallas_call | solution.py:30
  2.1 2.2 %collective-permute-start.1 = (bf16[16,2048]{1,0:T(8,128)(2,1)S(1)}, bf16[16,2048]{1,0:T(8,128)(2,1)S(1)}, u32[]{:S(2)}, u32[]{:S(2)}) collective-permute-start(bf16[16,2048]{1,0:T(8,128)(2,1)S(1)} %get-tuple-element.16), channel_id=1, source_target_pairs={{0,64},{32,96},{64,128},{96,160},{128,192},{160,224},{192,0},{224,... | collective-permute-start | bytes 196616 | tf_op jit(solution)/shard_map/ppermute | solution.py:271
  4.3 1.6 %collective-permute-start = (bf16[16,2048]{1,0:T(8,128)(2,1)S(1)}, bf16[16,2048]{1,0:T(8,128)(2,1)S(1)}, u32[]{:S(2)}, u32[]{:S(2)}) collective-permute-start(bf16[16,2048]{1,0:T(8,128)(2,1)S(1)} %get-tuple-element.16), channel_id=1, source_target_pairs={{0,32},{32,64},{64,96},{96,128},{128,160},{160,192},{192,224},{224... | collective-permute-start | bytes 196616 | tf_op jit(solution)/shard_map/ppermute | solution.py:271
  5.9 7.3 %all-to-all-start = ((bf16[4,432,128]{2,1,0:T(8,128)(2,1)}), bf16[4,432,128]{2,1,0:T(8,128)(2,1)S(1)}, u32[]{:S(2)}, u32[]{:S(2)}) async-start(bf16[4,432,128]{2,1,0:T(8,128)(2,1)} %get-tuple-element.15), calls=%async_computation | async-start | bytes 884736 | tf_op jit(solution)/shard_map/all_to_all | solution.py:295
  13.3 2.6 %collective-permute-start.7 = (bf16[48,2048]{1,0:T(8,128)(2,1)S(1)}, bf16[48,2048]{1,0:T(8,128)(2,1)S(1)}, u32[]{:S(2)}, u32[]{:S(2)}) collective-permute-start(bf16[48,2048]{1,0:T(8,128)(2,1)S(1)} %constant_dynamic-update-slice_fusion.refs_2_), channel_id=1, source_target_pairs={{0,6},{2,0},{4,2},{6,4},{1,7},{3,1},{5,3},{7,5},{8,14},{10,8},{12,... | collective-permute-start | bytes 589832 | tf_op jit(solution)/shard_map/ppermute | solution.py:271
  17.0 2.4 %collective-permute-start.2 = (bf16[48,2048]{1,0:T(8,128)(2,1)S(1)}, bf16[48,2048]{1,0:T(8,128)(2,1)S(1)}, u32[]{:S(2)}, u32[]{:S(2)}) collective-permute-start(bf16[48,2048]{1,0:T(8,128)(2,1)S(1)} %constant_dynamic-update-slice_fusion.refs_2_), channel_id=1, source_target_pairs={{0,1},{1,0},{2,3},{3,2},{4,5},{5,4},{6,7},{7,6},{8,9},{9,8},{10,11... | collective-permute-start | bytes 589832 | tf_op jit(solution)/shard_map/ppermute | solution.py:271
  19.3 1.1 %collective-permute-done.7.refs_8_ = bf16[48,2048]{1,0:T(8,128)(2,1)S(1)} collective-permute-done((bf16[48,2048]{1,0:T(8,128)(2,1)S(1)}, bf16[48,2048]{1,0:T(8,128)(2,1)S(1)}, u32[]{:S(2)}, u32[]{:S(2)}) %collective-permute-start.7) | collective-permute-done | bytes 196640 | tf_op jit(solution)/shard_map/ppermute | solution.py:271
  20.4 4.8 %collective-permute-start.8 = (bf16[48,2048]{1,0:T(8,128)(2,1)S(1)}, bf16[48,2048]{1,0:T(8,128)(2,1)S(1)}, u32[]{:S(2)}, u32[]{:S(2)}) collective-permute-start(bf16[48,2048]{1,0:T(8,128)(2,1)S(1)} %collective-permute-done.7.refs_8_), channel_id=1, source_target_pairs={{0,1},{1,0},{2,3},{3,2},{4,5},{5,4},{6,7},{7,6},{8,9},{9,8},{10,11... | collective-permute-start | bytes 589832 | tf_op jit(solution)/shard_map/ppermute | solution.py:271
  25.2 1.6 %collective-permute-start.6 = (bf16[48,2048]{1,0:T(8,128)(2,1)S(1)}, bf16[48,2048]{1,0:T(8,128)(2,1)S(1)}, u32[]{:S(2)}, u32[]{:S(2)}) collective-permute-start(bf16[48,2048]{1,0:T(8,128)(2,1)S(1)} %collective-permute-done.5.refs_6_), channel_id=1, source_target_pairs={{0,1},{1,0},{2,3},{3,2},{4,5},{5,4},{6,7},{7,6},{8,9},{9,8},{10,11... | collective-permute-start | bytes 589832 | tf_op jit(solution)/shard_map/ppermute | solution.py:271
  26.8 1.1 %collective-permute-done.3.refs_4_ = bf16[48,2048]{1,0:T(8,128)(2,1)S(1)} collective-permute-done((bf16[48,2048]{1,0:T(8,128)(2,1)S(1)}, bf16[48,2048]{1,0:T(8,128)(2,1)S(1)}, u32[]{:S(2)}, u32[]{:S(2)}) %collective-permute-start.3) | collective-permute-done | bytes 196640 | tf_op jit(solution)/shard_map/ppermute | solution.py:271
  28.0 0.9 %collective-permute-start.4 = (bf16[48,2048]{1,0:T(8,128)(2,1)S(1)}, bf16[48,2048]{1,0:T(8,128)(2,1)S(1)}, u32[]{:S(2)}, u32[]{:S(2)}) collective-permute-start(bf16[48,2048]{1,0:T(8,128)(2,1)S(1)} %collective-permute-done.3.refs_4_), channel_id=1, source_target_pairs={{0,1},{1,0},{2,3},{3,2},{4,5},{5,4},{6,7},{7,6},{8,9},{9,8},{10,11... | collective-permute-start | bytes 589832 | tf_op jit(solution)/shard_map/ppermute | solution.py:271
  28.9 1.1 %collective-permute-done.4.refs_5_ = bf16[48,2048]{1,0:T(8,128)(2,1)S(1)} collective-permute-done((bf16[48,2048]{1,0:T(8,128)(2,1)S(1)}, bf16[48,2048]{1,0:T(8,128)(2,1)S(1)}, u32[]{:S(2)}, u32[]{:S(2)}) %collective-permute-start.4) | collective-permute-done | bytes 196640 | tf_op jit(solution)/shard_map/ppermute | solution.py:271
  29.9 1.6 %shard_map.47 = bf16[16,96,128]{2,1,0:T(8,128)(2,1)S(1)} custom-call(bf16[16,2048]{1,0:T(8,128)(2,1)S(1)} %get-tuple-element.14.refs_0_, bf16[4,432,128]{2,1,0:T(8,128)(2,1)S(1)} %all-to-all-done.refs_1_, bf16[48,2048]{1,0:T(8,128)(2,1)S(1)} %constant_dynamic-update-slice_fusion.refs_2_, bf16[48,2048]{1,0:T(8,128)(2,1)S(1)} %collective-permute-done.2.refs_3_, ...), custom_call_target="tpu_custom_call" | custom-call | tf_op jit(solution)/shard_map/pallas_call | solution.py:30
  31.5 18.5 %all_to_all.10.parts_ref = bf16[16,96,128]{2,1,0:T(8,128)(2,1)S(1)} all-to-all(bf16[16,96,128]{2,1,0:T(8,128)(2,1)S(1)} %shard_map.47), channel_id=1, replica_groups=mesh['tm'=8,'z'=4,'x'=4,'c'=2] {'z','x'}, dimensions={0} | all-to-all | bytes 786432 | tf_op jit(solution)/shard_map/all_to_all | solution.py:310
  50.3 1.4 %collective-permute-start.10 = (bf16[192,256]{1,0:T(8,128)(2,1)S(1)}, bf16[192,256]{1,0:T(8,128)(2,1)S(1)}, u32[]{:S(2)}, u32[]{:S(2)}) collective-permute-start(bf16[192,256]{1,0:T(8,128)(2,1)S(1)} %shard_map.48.refs_1_.refs_0_), channel_id=1, source_target_pairs={{0,64},{32,96},{64,128},{96,160},{128,192},{160,224},{192,0},{224,... | collective-permute-start | bytes 294920 | tf_op jit(solution)/shard_map/ppermute | solution.py:271
  51.7 5.0 %collective-permute-start.9 = (bf16[192,256]{1,0:T(8,128)(2,1)S(1)}, bf16[192,256]{1,0:T(8,128)(2,1)S(1)}, u32[]{:S(2)}, u32[]{:S(2)}) collective-permute-start(bf16[192,256]{1,0:T(8,128)(2,1)S(1)} %shard_map.48.refs_1_.refs_0_), channel_id=1, source_target_pairs={{0,32},{32,64},{64,96},{96,128},{128,160},{160,192},{192,224},{224... | collective-permute-start | bytes 294920 | tf_op jit(solution)/shard_map/ppermute | solution.py:271
  56.7 2.2 %shard_map.49.refs_3_ = bf16[9,3,16,16,256]{4,3,2,1,0:T(8,128)(2,1)S(1)} custom-call(bf16[3,3,3,16,2,16,256]{6,5,4,3,2,1,0:T(8,128)(2,1)} %bitcast.10, bf16[192,256]{1,0:T(8,128)(2,1)S(1)} %shard_map.48.refs_1_.refs_0_), custom_call_target="tpu_custom_call" | custom-call | tf_op jit(solution)/shard_map/pallas_call | solution.py:30
  58.9 0.9 %collective-permute-done.9.refs_1_ = bf16[192,256]{1,0:T(8,128)(2,1)S(1)} collective-permute-done((bf16[192,256]{1,0:T(8,128)(2,1)S(1)}, bf16[192,256]{1,0:T(8,128)(2,1)S(1)}, u32[]{:S(2)}, u32[]{:S(2)}) %collective-permute-start.9) | collective-permute-done | bytes 98336 | tf_op jit(solution)/shard_map/ppermute | solution.py:271
  59.8 0.9 %shard_map.50 = (f32[2,192,256]{2,1,0:T(8,128)S(1)}, bf16[2,192,256]{2,1,0:T(8,128)(2,1)S(1)}) custom-call(bf16[192,256]{1,0:T(8,128)(2,1)S(1)} %shard_map.48.refs_1_.refs_0_, bf16[192,256]{1,0:T(8,128)(2,1)S(1)} %collective-permute-done.9.refs_1_, bf16[192,256]{1,0:T(8,128)(2,1)S(1)} %collective-permute-done.10.refs_2_, ...), custom_call_target="tpu_custom_call" | custom-call | tf_op jit(solution)/shard_map/pallas_call | solution.py:30
  60.8 1.9 %collective-permute-start.11 = (bf16[2,192,256]{2,1,0:T(8,128)(2,1)S(1)}, bf16[2,192,256]{2,1,0:T(8,128)(2,1)S(1)}, u32[]{:S(2)}, u32[]{:S(2)}) collective-permute-start(bf16[2,192,256]{2,1,0:T(8,128)(2,1)S(1)} %get-tuple-element.18), channel_id=1, source_target_pairs={{0,1},{1,0},{2,3},{3,2},{4,5},{5,4},{6,7},{7,6},{8,9},{9,8},{10,11... | collective-permute-start | bytes 589832 | tf_op jit(solution)/shard_map/ppermute | solution.py:271
  62.6 1.1 %collective-permute-done.11.refs_1_ = bf16[2,192,256]{2,1,0:T(8,128)(2,1)S(1)} collective-permute-done((bf16[2,192,256]{2,1,0:T(8,128)(2,1)S(1)}, bf16[2,192,256]{2,1,0:T(8,128)(2,1)S(1)}, u32[]{:S(2)}, u32[]{:S(2)}) %collective-permute-start.11) | collective-permute-done | bytes 196640 | tf_op jit(solution)/shard_map/ppermute | solution.py:271
  64.6 1.1 %collective-permute-start.13 = (bf16[256,256]{1,0:T(8,128)(2,1)S(1)}, bf16[256,256]{1,0:T(8,128)(2,1)S(1)}, u32[]{:S(2)}, u32[]{:S(2)}) collective-permute-start(bf16[256,256]{1,0:T(8,128)(2,1)S(1)} %get-tuple-element.22), channel_id=1, source_target_pairs={{0,64},{32,96},{64,128},{96,160},{128,192},{160,224},{192,0},{224,... | collective-permute-start | bytes 393224 | tf_op jit(solution)/shard_map/ppermute | solution.py:271
  66.2 4.8 %collective-permute-done.13.refs_2_ = bf16[256,256]{1,0:T(8,128)(2,1)S(1)} collective-permute-done((bf16[256,256]{1,0:T(8,128)(2,1)S(1)}, bf16[256,256]{1,0:T(8,128)(2,1)S(1)}, u32[]{:S(2)}, u32[]{:S(2)}) %collective-permute-start.13) | collective-permute-done | bytes 131104 | tf_op jit(solution)/shard_map/ppermute | solution.py:271
  71.0 1.3 %collective-permute-done.12.refs_1_ = bf16[256,256]{1,0:T(8,128)(2,1)S(1)} collective-permute-done((bf16[256,256]{1,0:T(8,128)(2,1)S(1)}, bf16[256,256]{1,0:T(8,128)(2,1)S(1)}, u32[]{:S(2)}, u32[]{:S(2)}) %collective-permute-start.12) | collective-permute-done | bytes 131104 | tf_op jit(solution)/shard_map/ppermute | solution.py:271
  (21 shorter events, 3.5 us)
Async XLA Ops:
  2.1 11.2 %collective-permute-start.1 = (bf16[16,2048]{1,0:T(8,128)(2,1)S(1)}, bf16[16,2048]{1,0:T(8,128)(2,1)S(1)}, u32[]{:S(2)}, u32[]{:S(2)}) collective-permute-start(bf16[16,2048]{1,0:T(8,128)(2,1)S(1)} %get-tuple-element.16), channel_id=1, source_target_pairs={{0,64},{32,96},{64,128},{96,160},{128,192},{160,224},{192,0},{224,... | collective-permute-start | bytes 196616 | tf_op jit(solution)/shard_map/ppermute | solution.py:271
  4.3 8.9 %collective-permute-start = (bf16[16,2048]{1,0:T(8,128)(2,1)S(1)}, bf16[16,2048]{1,0:T(8,128)(2,1)S(1)}, u32[]{:S(2)}, u32[]{:S(2)}) collective-permute-start(bf16[16,2048]{1,0:T(8,128)(2,1)S(1)} %get-tuple-element.16), channel_id=1, source_target_pairs={{0,32},{32,64},{64,96},{96,128},{128,160},{160,192},{192,224},{224... | collective-permute-start | bytes 196616 | tf_op jit(solution)/shard_map/ppermute | solution.py:271
  5.9 24.0 %all-to-all-start = ((bf16[4,432,128]{2,1,0:T(8,128)(2,1)}), bf16[4,432,128]{2,1,0:T(8,128)(2,1)S(1)}, u32[]{:S(2)}, u32[]{:S(2)}) async-start(bf16[4,432,128]{2,1,0:T(8,128)(2,1)} %get-tuple-element.15), calls=%async_computation | async-start | bytes 884736 | tf_op jit(solution)/shard_map/all_to_all | solution.py:295
  13.3 7.1 %collective-permute-start.7 = (bf16[48,2048]{1,0:T(8,128)(2,1)S(1)}, bf16[48,2048]{1,0:T(8,128)(2,1)S(1)}, u32[]{:S(2)}, u32[]{:S(2)}) collective-permute-start(bf16[48,2048]{1,0:T(8,128)(2,1)S(1)} %constant_dynamic-update-slice_fusion.refs_2_), channel_id=1, source_target_pairs={{0,6},{2,0},{4,2},{6,4},{1,7},{3,1},{5,3},{7,5},{8,14},{10,8},{12,... | collective-permute-start | bytes 589832 | tf_op jit(solution)/shard_map/ppermute | solution.py:271
  15.8 9.4 %collective-permute-start.5 = (bf16[48,2048]{1,0:T(8,128)(2,1)S(1)}, bf16[48,2048]{1,0:T(8,128)(2,1)S(1)}, u32[]{:S(2)}, u32[]{:S(2)}) collective-permute-start(bf16[48,2048]{1,0:T(8,128)(2,1)S(1)} %constant_dynamic-update-slice_fusion.refs_2_), channel_id=1, source_target_pairs={{0,4},{2,6},{4,0},{6,2},{1,5},{3,7},{5,1},{7,3},{8,12},{10,14},{12... | collective-permute-start | bytes 589832 | tf_op jit(solution)/shard_map/ppermute | solution.py:271
  16.4 11.6 %collective-permute-start.3 = (bf16[48,2048]{1,0:T(8,128)(2,1)S(1)}, bf16[48,2048]{1,0:T(8,128)(2,1)S(1)}, u32[]{:S(2)}, u32[]{:S(2)}) collective-permute-start(bf16[48,2048]{1,0:T(8,128)(2,1)S(1)} %constant_dynamic-update-slice_fusion.refs_2_), channel_id=1, source_target_pairs={{0,2},{2,4},{4,6},{6,0},{1,3},{3,5},{5,7},{7,1},{8,10},{10,12},{12... | collective-permute-start | bytes 589832 | tf_op jit(solution)/shard_map/ppermute | solution.py:271
  17.0 11.9 %collective-permute-start.2 = (bf16[48,2048]{1,0:T(8,128)(2,1)S(1)}, bf16[48,2048]{1,0:T(8,128)(2,1)S(1)}, u32[]{:S(2)}, u32[]{:S(2)}) collective-permute-start(bf16[48,2048]{1,0:T(8,128)(2,1)S(1)} %constant_dynamic-update-slice_fusion.refs_2_), channel_id=1, source_target_pairs={{0,1},{1,0},{2,3},{3,2},{4,5},{5,4},{6,7},{7,6},{8,9},{9,8},{10,11... | collective-permute-start | bytes 589832 | tf_op jit(solution)/shard_map/ppermute | solution.py:271
  20.4 8.5 %collective-permute-start.8 = (bf16[48,2048]{1,0:T(8,128)(2,1)S(1)}, bf16[48,2048]{1,0:T(8,128)(2,1)S(1)}, u32[]{:S(2)}, u32[]{:S(2)}) collective-permute-start(bf16[48,2048]{1,0:T(8,128)(2,1)S(1)} %collective-permute-done.7.refs_8_), channel_id=1, source_target_pairs={{0,1},{1,0},{2,3},{3,2},{4,5},{5,4},{6,7},{7,6},{8,9},{9,8},{10,11... | collective-permute-start | bytes 589832 | tf_op jit(solution)/shard_map/ppermute | solution.py:271
  25.2 3.7 %collective-permute-start.6 = (bf16[48,2048]{1,0:T(8,128)(2,1)S(1)}, bf16[48,2048]{1,0:T(8,128)(2,1)S(1)}, u32[]{:S(2)}, u32[]{:S(2)}) collective-permute-start(bf16[48,2048]{1,0:T(8,128)(2,1)S(1)} %collective-permute-done.5.refs_6_), channel_id=1, source_target_pairs={{0,1},{1,0},{2,3},{3,2},{4,5},{5,4},{6,7},{7,6},{8,9},{9,8},{10,11... | collective-permute-start | bytes 589832 | tf_op jit(solution)/shard_map/ppermute | solution.py:271
  28.0 2.0 %collective-permute-start.4 = (bf16[48,2048]{1,0:T(8,128)(2,1)S(1)}, bf16[48,2048]{1,0:T(8,128)(2,1)S(1)}, u32[]{:S(2)}, u32[]{:S(2)}) collective-permute-start(bf16[48,2048]{1,0:T(8,128)(2,1)S(1)} %collective-permute-done.3.refs_4_), channel_id=1, source_target_pairs={{0,1},{1,0},{2,3},{3,2},{4,5},{5,4},{6,7},{7,6},{8,9},{9,8},{10,11... | collective-permute-start | bytes 589832 | tf_op jit(solution)/shard_map/ppermute | solution.py:271
  50.3 8.6 %collective-permute-start.10 = (bf16[192,256]{1,0:T(8,128)(2,1)S(1)}, bf16[192,256]{1,0:T(8,128)(2,1)S(1)}, u32[]{:S(2)}, u32[]{:S(2)}) collective-permute-start(bf16[192,256]{1,0:T(8,128)(2,1)S(1)} %shard_map.48.refs_1_.refs_0_), channel_id=1, source_target_pairs={{0,64},{32,96},{64,128},{96,160},{128,192},{160,224},{192,0},{224,... | collective-permute-start | bytes 294920 | tf_op jit(solution)/shard_map/ppermute | solution.py:271
  51.7 8.2 %collective-permute-start.9 = (bf16[192,256]{1,0:T(8,128)(2,1)S(1)}, bf16[192,256]{1,0:T(8,128)(2,1)S(1)}, u32[]{:S(2)}, u32[]{:S(2)}) collective-permute-start(bf16[192,256]{1,0:T(8,128)(2,1)S(1)} %shard_map.48.refs_1_.refs_0_), channel_id=1, source_target_pairs={{0,32},{32,64},{64,96},{96,128},{128,160},{160,192},{192,224},{224... | collective-permute-start | bytes 294920 | tf_op jit(solution)/shard_map/ppermute | solution.py:271
  58.9 4.8 %copy-start = (bf16[3,3,3,256,256]{4,3,2,1,0:T(8,128)(2,1)S(1)}, bf16[3,3,3,256,256]{4,3,2,1,0:T(8,128)(2,1)}, u32[]{:S(2)}) copy-start(bf16[3,3,3,256,256]{4,3,2,1,0:T(8,128)(2,1)} %refs_2_.3) | copy-start | bytes 10616836
  60.8 2.9 %collective-permute-start.11 = (bf16[2,192,256]{2,1,0:T(8,128)(2,1)S(1)}, bf16[2,192,256]{2,1,0:T(8,128)(2,1)S(1)}, u32[]{:S(2)}, u32[]{:S(2)}) collective-permute-start(bf16[2,192,256]{2,1,0:T(8,128)(2,1)S(1)} %get-tuple-element.18), channel_id=1, source_target_pairs={{0,1},{1,0},{2,3},{3,2},{4,5},{5,4},{6,7},{7,6},{8,9},{9,8},{10,11... | collective-permute-start | bytes 589832 | tf_op jit(solution)/shard_map/ppermute | solution.py:271
  64.6 6.4 %collective-permute-start.13 = (bf16[256,256]{1,0:T(8,128)(2,1)S(1)}, bf16[256,256]{1,0:T(8,128)(2,1)S(1)}, u32[]{:S(2)}, u32[]{:S(2)}) collective-permute-start(bf16[256,256]{1,0:T(8,128)(2,1)S(1)} %get-tuple-element.22), channel_id=1, source_target_pairs={{0,64},{32,96},{64,128},{96,160},{128,192},{160,224},{192,0},{224,... | collective-permute-start | bytes 393224 | tf_op jit(solution)/shard_map/ppermute | solution.py:271
  65.7 6.6 %collective-permute-start.12 = (bf16[256,256]{1,0:T(8,128)(2,1)S(1)}, bf16[256,256]{1,0:T(8,128)(2,1)S(1)}, u32[]{:S(2)}, u32[]{:S(2)}) collective-permute-start(bf16[256,256]{1,0:T(8,128)(2,1)S(1)} %get-tuple-element.21.refs_3_), channel_id=1, source_target_pairs={{0,32},{32,64},{64,96},{96,128},{128,160},{160,192},{192,224},{224... | collective-permute-start | bytes 393224 | tf_op jit(solution)/shard_map/ppermute | solution.py:271
